TPU v7x, 32 devices: a whole 2x2x4 slice. The times are simulated.
32 devices in a mesh: rows: 4 (over y, x), heads: 8 (over z, core).
Axes of the slice: x: 2, y: 2, z: 4, core: 2. Of those that a mesh axis runs over, the one named last changes fastest.
Arguments:
- tokens: bfloat16 [1408, 8, 1152], P('heads', 'rows'), may hold values from -6 to 6
- cond: bfloat16 [8, 11, 1152], P('rows'), may hold values from -6 to 6
- lengths: int32 [8, 11], P('rows'), may hold values from 0 to 512, as said below
- pads: int32 [8, 11], P('rows'), may hold values from 0 to 128, as said below
- timesteps: int32 [8, 11], P('rows'), may hold values from 0 to 999
- head_mask: int32 [8, 11, 16], P('rows'), may hold values 0 or 1
- group_mask: int32 [8, 11, 16], P('rows'), may hold values 0 or 1
- keep: int32 [1408, 8], P('heads', 'rows'), may hold values 0 or 1
- ada_w: bfloat16 [1152, 6912], P(None, 'heads'), may hold values from -0.1875 to 0.1875
- ada_b: bfloat16 [6912], P('heads'), may hold values from -1.5 to 1.5
- w_qkv: bfloat16 [1152, 3456], P(None, 'heads'), may hold values from -0.1875 to 0.1875
- b_qv: bfloat16 [2304], P('heads'), may hold values from -1.5 to 1.5
- w_out: bfloat16 [1152, 1152], P('heads'), may hold values from -1.5 to 1.5
- b_out: bfloat16 [1152], replicated, may hold values from -1.5 to 1.5
- w_up: bfloat16 [1152, 4608], P(None, 'heads'), may hold values from -0.1875 to 0.1875
- b_up: bfloat16 [4608], P('heads'), may hold values from -1.5 to 1.5
- w_down: bfloat16 [4608, 1152], P('heads'), may hold values from -0.1875 to 0.1875
- b_down: bfloat16 [1152], replicated, may hold values from -1.5 to 1.5
- w_route: bfloat16 [1152], replicated, may hold values from -0.1875 to 0.1875
- grad_out: bfloat16 [1408, 8, 1152], P('heads', 'rows'), may hold values from -6 to 6
Outputs:
- final: bfloat16 [1408, 8, 1152], P('heads', 'rows')
- grad_tokens: float32 [1408, 8, 1152], P('heads', 'rows')
- grad_cond: float32 [8, 11, 1152], P('rows')
- grad_ada_w: float32 [1152, 6912], P(None, 'heads')
- grad_ada_b: float32 [6912], P('heads')
- grad_w_qkv: float32 [1152, 3456], P(None, 'heads')
- grad_b_qv: float32 [2304], P('heads')
- grad_w_out: float32 [1152, 1152], P('heads')
- grad_b_out: float32 [1152], P('heads')
- grad_w_up: float32 [1152, 4608], P(None, 'heads')
- grad_b_up: float32 [4608], P('heads')
- grad_w_down: float32 [4608, 1152], P('heads')
- grad_b_down: float32 [1152], P('heads')
- grad_w_route: float32 [1152], P('heads')
Inputs may be any that keep to these rules, and one draw needn't show every extreme that they name: Each row's nonzero crop lengths are multiples of 64 from 128 to 512, fill the leading slots, are followed by zeros, and sum to 1408. `pads`: at most a quarter of the crop's length; 0 in empty slots.
All inputs are finite; a program needn't handle non-finite values. No bound on the sum of `head_mask` or of `group_mask` or of `keep` on one device may be relied on, other than what follows from the above.
Results may differ from a plain program's by a relative error of at most 0.015.
The roundings to bfloat16 on the way count: a program that leaves them out, or rounds other values in their place, can miss the bound.
Values may be sent and summed in bfloat16 or wider, within the bound.
A program may use at most 256 MiB of HBM per device.

v0:
```python
import math

import jax
import jax.numpy as jnp
from jax import lax
from jax.sharding import PartitionSpec as P

D = 1152
H = 16
HD = 72
GW = 288
SEQ = 1408


EPSILON = 1e-06
MASKED_SCORE = -1000000000.0


def time_embed(timesteps):
    halves = D // 2
    frequency = jnp.exp(-math.log(10000.0) * jnp.arange(halves, dtype=jnp.float32) / halves)
    angles = timesteps.astype(jnp.float32)[..., None] * frequency
    return jnp.concatenate([jnp.cos(angles), jnp.sin(angles)], axis=-1)


def gelu_tanh(values):
    return (
        0.5
        * values
        * (1.0 + jnp.tanh(0.7978845608028654 * (values + 0.044715 * values * values * values)))
    )


def norm_rows(values):
    average = jnp.mean(values, axis=-1, keepdims=True)
    centred = values - average
    inverse_dev = lax.rsqrt(jnp.mean(centred * centred, axis=-1, keepdims=True) + EPSILON)
    return (centred * inverse_dev, inverse_dev)


def norm_back(grad_normed, normed, inverse_dev):
    first_mean = jnp.mean(grad_normed, axis=-1, keepdims=True)
    second_mean = jnp.mean(grad_normed * normed, axis=-1, keepdims=True)
    return inverse_dev * (grad_normed - first_mean - normed * second_mean)


def crop_layout(lengths, pads, offset, amount):
    crop_ends = jnp.cumsum(lengths, axis=1)
    starts = crop_ends - lengths
    places = offset + jnp.arange(amount, dtype=jnp.int32)
    inside = (places[:, None, None] >= starts[None]) & (places[:, None, None] < crop_ends[None])
    live_part = places[:, None, None] < (crop_ends - pads)[None]
    one_hot = inside.astype(jnp.float32)
    item_ids = jnp.sum(
        inside.astype(jnp.int32) * jnp.arange(lengths.shape[1], dtype=jnp.int32), axis=2
    )
    valid = jnp.sum((inside & live_part).astype(jnp.float32), axis=2)
    return (one_hot, item_ids, valid)


def masked_scores(queries, key_rows, item_row, key_live, score_scale):
    raw = jnp.einsum("shd,thd->hst", queries, key_rows, preferred_element_type=jnp.float32)
    allowed = (item_row[:, None] == item_row[None, :]) & key_live[None, :]
    return jnp.where(allowed[None], raw * score_scale, MASKED_SCORE)


def attend_row(triple_row, item_row, key_live, score_scale):
    queries = triple_row[:, :, 0]
    key_rows = triple_row[:, :, 1]
    values = triple_row[:, :, 2]
    scores = masked_scores(queries, key_rows, item_row, key_live, score_scale)
    row_top = jnp.max(scores, axis=-1, keepdims=True)
    log_total = row_top + jnp.log(jnp.sum(jnp.exp(scores - row_top), axis=-1, keepdims=True))
    probability = jnp.exp(scores - log_total).astype(jnp.bfloat16)
    attended = jnp.einsum("hst,thd->shd", probability, values, preferred_element_type=jnp.float32)
    return (attended, log_total)


def attend_back(triple_row, grad_row, total_row, item_row, key_live, score_scale):
    queries = triple_row[:, :, 0]
    key_rows = triple_row[:, :, 1]
    values = triple_row[:, :, 2]
    scores = masked_scores(queries, key_rows, item_row, key_live, score_scale)
    probability = jnp.exp(scores - total_row)
    grad_prob = jnp.einsum("shd,thd->hst", grad_row, values, preferred_element_type=jnp.float32)
    grad_values = jnp.einsum(
        "hst,shd->thd",
        probability.astype(jnp.bfloat16),
        grad_row,
        preferred_element_type=jnp.float32,
    )
    inner = jnp.sum(probability * grad_prob, axis=-1, keepdims=True)
    grad_raw = (probability * (grad_prob - inner) * score_scale).astype(jnp.bfloat16)
    grad_queries = jnp.einsum(
        "hst,thd->shd", grad_raw, key_rows, preferred_element_type=jnp.float32
    )
    grad_keys = jnp.einsum("hst,shd->thd", grad_raw, queries, preferred_element_type=jnp.float32)
    return jnp.stack([grad_queries, grad_keys, grad_values], axis=2).astype(jnp.bfloat16)


def project_rows(source, weight):
    return jnp.einsum("sbk,kd->sbd", source, weight, preferred_element_type=jnp.float32)


def back_rows(source, weight):
    return jnp.einsum("sbk,dk->sbd", source, weight, preferred_element_type=jnp.float32)


def per_device(
    tokens,
    cond,
    lengths,
    pads,
    timesteps,
    head_mask,
    group_mask,
    keep,
    ada_w,
    ada_b,
    w_qkv,
    b_qv,
    w_out,
    b_out,
    w_up,
    b_up,
    w_down,
    b_down,
    w_route,
    grad_out,
):
    highest = lax.Precision.HIGHEST
    groups = lax.axis_size("heads")
    head_rank = lax.axis_index("heads")
    shard_len = tokens.shape[0]
    batch_local = tokens.shape[1]
    local_heads = H // groups
    score_scale = HD ** (-0.5)
    local_hot, local_items, local_valid = crop_layout(
        lengths, pads, head_rank * shard_len, shard_len
    )
    full_hot, full_items, full_valid = crop_layout(lengths, pads, 0, SEQ)
    cond_all = cond.astype(jnp.float32) + time_embed(timesteps)
    sigmoid_cond = lax.logistic(cond_all)
    silu_low = (cond_all * sigmoid_cond).astype(jnp.bfloat16)
    modulation_part = jnp.einsum(
        "bcd,dm->bcm", silu_low, ada_w, preferred_element_type=jnp.float32
    ) + ada_b.astype(jnp.float32)
    modulation = lax.all_gather(modulation_part, "heads", axis=2, tiled=True)
    token_mod = jnp.einsum("sbc,bcm->sbm", local_hot, modulation, precision=highest)
    shift_one, scale_one, gate_one, shift_two, scale_two, gate_two = jnp.split(
        token_mod, 6, axis=-1
    )
    token_values = tokens.astype(jnp.float32)
    normed_one, inverse_one = norm_rows(token_values)
    hidden_one = (normed_one * (1.0 + scale_one) + shift_one).astype(jnp.bfloat16)
    hidden_all = lax.all_gather(hidden_one, "heads", axis=0, tiled=True)
    bias_pairs = b_qv.astype(jnp.float32).reshape(local_heads, 2, HD)
    bias_triple = jnp.stack(
        [bias_pairs[:, 0], jnp.zeros_like(bias_pairs[:, 0]), bias_pairs[:, 1]], axis=1
    ).reshape(-1)
    triple_all = (
        jnp.einsum("sbd,dm->sbm", hidden_all, w_qkv, preferred_element_type=jnp.float32)
        + bias_triple
    ).astype(jnp.bfloat16)
    triple_rows = jnp.moveaxis(triple_all.reshape(SEQ, batch_local, local_heads, 3, HD), 1, 0)
    item_rows = jnp.transpose(full_items)
    live_rows = jnp.transpose(full_valid > 0.5)
    attended, totals = lax.map(
        lambda packed: attend_row(packed[0], packed[1], packed[2], score_scale),
        (triple_rows, item_rows, live_rows),
    )
    head_table = lax.dynamic_slice_in_dim(
        head_mask, head_rank * local_heads, local_heads, 2
    ).astype(jnp.float32)
    head_full = jnp.einsum("sbc,bch->sbh", full_hot, head_table, precision=highest)
    out_mask = head_full * full_valid[..., None]
    attn_low = (
        (jnp.moveaxis(attended, 0, 1) * out_mask[..., None])
        .reshape(SEQ, batch_local, local_heads * HD)
        .astype(jnp.bfloat16)
    )
    projected = lax.psum_scatter(
        project_rows(attn_low, w_out), "heads", scatter_dimension=0, tiled=True
    )
    b_out_values = b_out.astype(jnp.float32)
    mixed = token_values + gate_one * (projected + b_out_values)
    normed_two, inverse_two = norm_rows(mixed)
    hidden_two = normed_two * (1.0 + scale_two) + shift_two
    hidden_two_low = hidden_two.astype(jnp.bfloat16)
    route_values = w_route.astype(jnp.float32)
    route = lax.logistic(jnp.einsum("sbd,d->sb", hidden_two, route_values, precision=highest))
    keep_values = keep.astype(jnp.float32)
    route_keep = keep_values * route
    group_table = lax.dynamic_slice_in_dim(
        group_mask, head_rank * local_heads, local_heads, 2
    ).astype(jnp.float32)
    hidden_two_all = lax.all_gather(hidden_two_low, "heads", axis=0, tiled=True)
    group_tok = jnp.einsum("sbc,bch->sbh", full_hot, group_table, precision=highest)
    upper = jnp.einsum(
        "sbd,dk->sbk", hidden_two_all, w_up, preferred_element_type=jnp.float32
    ) + b_up.astype(jnp.float32)
    active, gelu_back = jax.vjp(gelu_tanh, upper)
    group_wide = jnp.repeat(group_tok, GW, axis=-1)
    active_low = (active * group_wide).astype(jnp.bfloat16)
    lowered = lax.psum_scatter(
        project_rows(active_low, w_down), "heads", scatter_dimension=0, tiled=True
    )
    branch = lowered + b_down.astype(jnp.float32)
    final = mixed + gate_two * route_keep[..., None] * branch
    grad_final = grad_out.astype(jnp.float32)
    grad_branch = grad_final * gate_two * route_keep[..., None]
    grad_gate_two = grad_final * route_keep[..., None] * branch
    grad_route = jnp.sum(grad_final * gate_two * branch, axis=-1) * keep_values
    grad_logit = grad_route * route * (1.0 - route)
    part_route = jnp.einsum("sb,sbd->d", grad_logit, hidden_two, precision=highest)
    part_b_down = jnp.sum(grad_branch, axis=(0, 1))
    grad_low = grad_branch.astype(jnp.bfloat16)
    grad_all = lax.all_gather(grad_low, "heads", axis=0, tiled=True)
    grad_active = jnp.einsum("sbd,kd->sbk", grad_all, w_down, preferred_element_type=jnp.float32)
    (grad_upper,) = gelu_back(grad_active * group_wide)
    upper_low = grad_upper.astype(jnp.bfloat16)
    grad_w_up = jnp.einsum(
        "sbd,sbk->dk", hidden_two_all, upper_low, preferred_element_type=jnp.float32
    )
    grad_b_up = jnp.sum(upper_low, axis=(0, 1), dtype=jnp.float32)
    grad_w_down = jnp.einsum(
        "sbk,sbd->kd", active_low, grad_all, preferred_element_type=jnp.float32
    )
    grad_hidden_two = lax.psum_scatter(
        back_rows(upper_low, w_up), "heads", scatter_dimension=0, tiled=True
    )
    grad_hidden_two = grad_hidden_two + grad_logit[..., None] * route_values
    grad_scale_two = grad_hidden_two * normed_two
    grad_mixed = grad_final + norm_back(
        grad_hidden_two * (1.0 + scale_two), normed_two, inverse_two
    )
    grad_gate_one = grad_mixed * (projected + b_out_values)
    grad_projected = grad_mixed * gate_one
    part_b_out = jnp.sum(grad_projected, axis=(0, 1))
    projected_low = grad_projected.astype(jnp.bfloat16)
    grad_proj_all = lax.all_gather(projected_low, "heads", axis=0, tiled=True)
    grad_attn = jnp.einsum(
        "sbd,kd->sbk", grad_proj_all, w_out, preferred_element_type=jnp.float32
    ).astype(jnp.bfloat16)
    grad_w_out = jnp.einsum(
        "sbk,sbd->kd", attn_low, grad_proj_all, preferred_element_type=jnp.float32
    )
    grad_masked = grad_attn.reshape(SEQ, batch_local, local_heads, HD) * out_mask[..., None].astype(
        jnp.bfloat16
    )
    grad_rows = jnp.moveaxis(grad_masked, 1, 0)
    grad_triple_rows = lax.map(
        lambda packed: attend_back(
            packed[0], packed[1], packed[2], packed[3], packed[4], score_scale
        ),
        (triple_rows, grad_rows, totals, item_rows, live_rows),
    )
    grad_triple = jnp.moveaxis(grad_triple_rows, 0, 1).reshape(
        SEQ, batch_local, local_heads * 3 * HD
    )
    grad_w_qkv = jnp.einsum(
        "sbd,sbm->dm", hidden_all, grad_triple, preferred_element_type=jnp.float32
    )
    bias_sums = jnp.sum(grad_triple, axis=(0, 1), dtype=jnp.float32).reshape(local_heads, 3, HD)
    grad_b_qv = jnp.stack([bias_sums[:, 0], bias_sums[:, 2]], axis=1).reshape(-1)
    grad_hidden_one = lax.psum_scatter(
        back_rows(grad_triple, w_qkv), "heads", scatter_dimension=0, tiled=True
    )
    grad_tokens = grad_mixed + norm_back(
        grad_hidden_one * (1.0 + scale_one), normed_one, inverse_one
    )
    grad_token_mod = jnp.concatenate(
        [
            grad_hidden_one,
            grad_hidden_one * normed_one,
            grad_gate_one,
            grad_hidden_two,
            grad_scale_two,
            grad_gate_two,
        ],
        axis=-1,
    )
    part_mod = jnp.einsum("sbc,sbm->bcm", local_hot, grad_token_mod, precision=highest)
    grad_mod, share_b_out, share_b_down, share_route = (
        lax.psum_scatter(part_mod, "heads", scatter_dimension=2, tiled=True),
        lax.psum_scatter(part_b_out, "heads", scatter_dimension=0, tiled=True),
        lax.psum_scatter(part_b_down, "heads", scatter_dimension=0, tiled=True),
        lax.psum_scatter(part_route, "heads", scatter_dimension=0, tiled=True),
    )
    mod_low = grad_mod.astype(jnp.bfloat16)
    grad_ada_w = jnp.einsum("bcd,bcm->dm", silu_low, mod_low, preferred_element_type=jnp.float32)
    grad_ada_b = jnp.sum(mod_low, axis=(0, 1), dtype=jnp.float32)
    part_activ = jnp.einsum("bcm,dm->bcd", mod_low, ada_w, preferred_element_type=jnp.float32)
    grad_activ = lax.psum(part_activ.astype(jnp.bfloat16), "heads").astype(jnp.float32)
    grad_cond = grad_activ * sigmoid_cond * (1.0 + cond_all * (1.0 - sigmoid_cond))
    summed = (
        lax.psum(grad_ada_w.astype(jnp.bfloat16), "rows").astype(jnp.float32),
        lax.psum(grad_ada_b.astype(jnp.bfloat16), "rows").astype(jnp.float32),
        lax.psum(grad_w_qkv.astype(jnp.bfloat16), "rows").astype(jnp.float32),
        lax.psum(grad_b_qv.astype(jnp.bfloat16), "rows").astype(jnp.float32),
        lax.psum(grad_w_out.astype(jnp.bfloat16), "rows").astype(jnp.float32),
        lax.psum(share_b_out.astype(jnp.bfloat16), "rows").astype(jnp.float32),
        lax.psum(grad_w_up.astype(jnp.bfloat16), "rows").astype(jnp.float32),
        lax.psum(grad_b_up.astype(jnp.bfloat16), "rows").astype(jnp.float32),
        lax.psum(grad_w_down.astype(jnp.bfloat16), "rows").astype(jnp.float32),
        lax.psum(share_b_down.astype(jnp.bfloat16), "rows").astype(jnp.float32),
        lax.psum(share_route.astype(jnp.bfloat16), "rows").astype(jnp.float32),
    )
    return (
        final.astype(jnp.bfloat16),
        grad_tokens,
        grad_cond,
        summed[0],
        summed[1],
        summed[2],
        summed[3],
        summed[4],
        summed[5],
        summed[6],
        summed[7],
        summed[8],
        summed[9],
        summed[10],
    )


def solution(mesh):
    in_specs = (
        P("heads", "rows", None),
        P("rows", None, None),
        P("rows", None),
        P("rows", None),
        P("rows", None),
        P("rows", None, None),
        P("rows", None, None),
        P("heads", "rows"),
        P(None, "heads"),
        P("heads"),
        P(None, "heads"),
        P("heads"),
        P("heads", None),
        P(),
        P(None, "heads"),
        P("heads"),
        P("heads", None),
        P(),
        P(),
        P("heads", "rows", None),
    )
    out_specs = (
        P("heads", "rows", None),
        P("heads", "rows", None),
        P("rows", None, None),
        P(None, "heads"),
        P("heads"),
        P(None, "heads"),
        P("heads"),
        P("heads", None),
        P("heads"),
        P(None, "heads"),
        P("heads"),
        P("heads", None),
        P("heads"),
        P("heads"),
    )
    return jax.shard_map(
        per_device, mesh=mesh, in_specs=in_specs, out_specs=out_specs, check_vma=False
    )
```

profile of v0, /device:TPU:0, one launch (start us, length us, event | category | flops | bytes accessed | tf_op | source)
XLA Modules:
  0.0 1399.0 jit_solution(8388406987155349283)
XLA Ops:
  15.3 64.2 %all_gather.15 = f32[2,11,6912]{1,0,2:T(2,128)} all-gather(f32[2,11,864]{1,0,2:T(2,128)S(1)} %copy.67), channel_id=1, replica_groups=mesh['rows'=4,'heads'=8] {'heads'}, dimensions={2}, use_global_device_ids=true | all-gather | bytes 684288 | tf_op jit(solution)/shard_map/all_gather | solution.py:148
  79.7 7.6 convolution_bitcast_fusion
  94.0 66.6 %all-gather.5.cloned.1.call-done = bf16[1408,2,1152]{2,0,1:T(8,128)(2,1)} async-done(((bf16[176,2,1152]{2,0,1:T(8,128)(2,1)}), bf16[1408,2,1152]{2,0,1:T(8,128)(2,1)}) %all-gather.5.cloned.1.call-update) | async-done | bytes 6488080 | tf_op jit(solution)/shard_map/all_gather | solution.py:156
  160.6 6.4 add_convert_fusion
  168.6 54.9 %while.22 = (s32[]{:T(128)}, f32[2,1408,2,72]{1,3,2,0:T(8,128)}, f32[2,2,1408,1]{2,1,3,0:T(2,128)S(1)}, bf16[2,1408,2,3,72]{1,4,2,3,0:T(8,128)(2,1)}, s32[2,1408...) while((s32[]{:T(128)}, f32[2,1408,2,72]{1,3,2,0:T(8,128)}, f32[2,2,1408,1]{2,1,3,0:T(2,128)S(1)}, ...), condition=%wide.region_8.9_spmd, body=%wide.region_5.8_spmd.sunk | while | flops 1173615872 | bytes 69092128 | solution.py:168
  172.2 7.2 fusion.162
  179.4 7.7 exponential_reduce_fusion.2
  187.2 8.0 fusion.163
  199.4 7.2 fusion.162
  206.7 7.7 exponential_reduce_fusion.2
  214.4 8.0 fusion.163
  226.0 6.8 fusion.97
  233.5 131.1 %reduce-scatter.8.cloned.1.call-done = f32[176,2,1152]{2,0,1:T(8,128)} async-done(((f32[1408,2,1152]{2,0,1:T(8,128)}), f32[176,2,1152]{2,0,1:T(8,128)}) %reduce-scatter.8.cloned.1.call-update) | async-done | bytes 1622032 | tf_op jit(solution)/shard_map/reduce_scatter | solution.py:182
  371.9 64.2 %all-gather.7.cloned.1.call-done = bf16[1408,2,1152]{2,0,1:T(8,128)(2,1)} async-done(((bf16[176,2,1152]{2,0,1:T(8,128)(2,1)}), bf16[1408,2,1152]{2,0,1:T(8,128)(2,1)}) %all-gather.7.cloned.1.call-update) | async-done | bytes 6488080 | tf_op jit(solution)/shard_map/all_gather | solution.py:197
  436.1 11.4 fusion.52
  449.2 8.7 fusion.81
  461.0 128.7 %reduce-scatter.10.cloned.1.call-done = f32[176,2,1152]{2,0,1:T(8,128)} async-done(((f32[1408,2,1152]{2,0,1:T(8,128)}), f32[176,2,1152]{2,0,1:T(8,128)}) %reduce-scatter.10.cloned.1.call-update) | async-done | bytes 1622032 | tf_op jit(solution)/shard_map/reduce_scatter | solution.py:205
  589.7 4.8 multiply_reduce_fusion.4
  594.7 64.6 %all-gather.9.cloned.1.call-done = bf16[1408,2,1152]{2,0,1:T(8,128)(2,1)} async-done(((bf16[176,2,1152]{2,0,1:T(8,128)(2,1)}), bf16[1408,2,1152]{2,0,1:T(8,128)(2,1)}) %all-gather.9.cloned.1.call-update) | async-done | bytes 6488080 | tf_op jit(solution)/shard_map/all_gather | solution.py:218
  659.4 12.8 fusion.49
  673.8 8.6 fusion.83
  682.5 131.7 %reduce-scatter.12.cloned.1.call-done = f32[176,2,1152]{2,0,1:T(8,128)} async-done(((f32[1408,2,1152]{2,0,1:T(8,128)}), f32[176,2,1152]{2,0,1:T(8,128)}) %reduce-scatter.12.cloned.1.call-update) | async-done | bytes 1622032 | tf_op jit(solution)/shard_map/reduce_scatter | solution.py:229
  821.2 64.8 %all-gather.11.cloned.1.call-done = bf16[1408,2,1152]{2,0,1:T(8,128)(2,1)} async-done(((bf16[176,2,1152]{2,0,1:T(8,128)(2,1)}), bf16[1408,2,1152]{2,0,1:T(8,128)(2,1)}) %all-gather.11.cloned.1.call-update) | async-done | bytes 6488080 | tf_op jit(solution)/shard_map/all_gather | solution.py:241
  886.0 4.7 convolution_convert_fusion
  891.7 135.0 %while.23 = (s32[]{:T(128)}, bf16[2,1408,2,3,72]{1,4,3,2,0:T(8,128)(2,1)}, bf16[2,1408,2,3,72]{1,4,2,3,0:T(8,128)(2,1)}, s32[2,1408]{1,0:T(2,128)S(1)}, pred[2,1...) while((s32[]{:T(128)}, ...), condition=%wide.region_19.20_spmd, body=%wide.region_17.19_spmd.sunk | while | flops 2916055040 | bytes 254080816 | solution.py:252
  895.3 4.4 subtract_exponential_fusion.2
  899.7 4.3 fusion.169
  905.4 7.8 fusion.170
  913.2 21.9 %fusion.172 = bf16[1,1408,2,1,72]{1,4,2,3,0:T(8,128)(2,1)} fusion(f32[2,1408,1408]{1,2,0:T(8,128)} %copy-done.1, f32[2,1408,1408]{1,2,0:T(8,128)} %fusion.170, bf16[1408,2,3,72]{0,3,1,2:T(8,128)(2,1)S(1)} %dynamic-slice_bitcast_fusion.8), kind=kOutput, calls=%fused_computation.31.clone.1 | convolution fusion | flops 590981248 | bytes 64249856 | tf_op jit(solution)/shard_map/while/body/eval_jaxpr/hst,thd->shd/dot_general | solution.py:94
  935.1 21.9 %fusion.171 = bf16[1,1408,2,1,72]{1,4,2,3,0:T(8,128)(2,1)} fusion(f32[2,1408,1408]{1,2,0:T(8,128)} %copy-done.1, f32[2,1408,1408]{1,2,0:T(8,128)} %fusion.170, bf16[1408,2,3,72]{0,3,1,2:T(8,128)(2,1)S(1)} %dynamic-slice_bitcast_fusion.8), kind=kOutput, calls=%fused_computation.30.clone.1 | convolution fusion | flops 590981248 | bytes 64249856 | tf_op jit(solution)/shard_map/while/body/eval_jaxpr/hst,shd->thd/dot_general | solution.py:97
  962.5 4.4 subtract_exponential_fusion.2
  967.0 4.3 fusion.169
  972.6 7.8 fusion.170
  980.4 21.9 %fusion.172 = bf16[1,1408,2,1,72]{1,4,2,3,0:T(8,128)(2,1)} fusion(f32[2,1408,1408]{1,2,0:T(8,128)} %copy-done.1, f32[2,1408,1408]{1,2,0:T(8,128)} %fusion.170, bf16[1408,2,3,72]{0,3,1,2:T(8,128)(2,1)S(1)} %dynamic-slice_bitcast_fusion.8), kind=kOutput, calls=%fused_computation.31.clone.1 | convolution fusion | flops 590981248 | bytes 64249856 | tf_op jit(solution)/shard_map/while/body/eval_jaxpr/hst,thd->shd/dot_general | solution.py:94
  1002.4 21.9 %fusion.171 = bf16[1,1408,2,1,72]{1,4,2,3,0:T(8,128)(2,1)} fusion(f32[2,1408,1408]{1,2,0:T(8,128)} %copy-done.1, f32[2,1408,1408]{1,2,0:T(8,128)} %fusion.170, bf16[1408,2,3,72]{0,3,1,2:T(8,128)(2,1)S(1)} %dynamic-slice_bitcast_fusion.8), kind=kOutput, calls=%fused_computation.30.clone.1 | convolution fusion | flops 590981248 | bytes 64249856 | tf_op jit(solution)/shard_map/while/body/eval_jaxpr/hst,shd->thd/dot_general | solution.py:97
  1026.8 10.6 fusion.91
  1037.4 9.4 fusion.53
  1046.8 8.5 fusion.54
  1055.3 113.8 %reduce-scatter.14.cloned.1.call-done = f32[176,2,1152]{2,0,1:T(8,128)} async-done(((f32[1408,2,1152]{2,0,1:T(8,128)}), f32[176,2,1152]{2,0,1:T(8,128)}) %reduce-scatter.14.cloned.1.call-update) | async-done | bytes 1622032 | tf_op jit(solution)/shard_map/reduce_scatter | solution.py:266
  1184.9 6.7 copy.83
  1191.6 7.8 reshape.311
  1200.6 5.0 fusion.56
  1205.6 7.2 fusion.55
  1212.8 29.0 %reduce-scatter.16.cloned.1.call-done = f32[864,22]{1,0:T(8,128)} async-done(((f32[6912,22]{1,0:T(8,128)}), f32[864,22]{1,0:T(8,128)}) %reduce-scatter.16.cloned.1.call-update) | async-done | bytes 76048
  1255.7 26.3 %all-reduce.3 = (bf16[1152]{0:T(1024)(128)(2,1)S(1)}, bf16[1152]{0:T(1024)(128)(2,1)S(1)}, bf16[1152]{0:T(1024)(128)(2,1)S(1)}) all-reduce(f32[1152]{0:T(1024)S(1)} %get-tuple-element.133, f32[1152]{0:T(1024)S(1)} %copy-done.58, f32[1152]{0:T(1024)S(1)} %convolution_reduce_fusion), channel_id=7, replica_groups=mesh['rows'=4,'heads'=8] {'heads'}, use_global_device_ids=true, to_apply=%region_33.34.clone | all-reduce | flops 3456 | bytes 20736
  1285.7 10.2 all-reduce.4
  1299.8 26.8 %psum.84 = bf16[2,11,1152]{2,1,0:T(8,128)(2,1)S(1)} all-reduce(bf16[2,11,1152]{2,1,0:T(8,128)(2,1)S(1)} %convolution_convert_fusion.1), channel_id=1, replica_groups=mesh['rows'=4,'heads'=8] {'heads'}, use_global_device_ids=true, to_apply=%region_24.25 | all-reduce | flops 25344 | bytes 101376 | tf_op jit(solution)/shard_map/psum | solution.py:294
  1327.5 53.4 %all-reduce.8.cloned.1.call-done = (bf16[1152,864]{0,1:T(8,128)(2,1)}, bf16[1152,432]{0,1:T(8,128)(2,1)}, bf16[144,1152]{1,0:T(8,128)(2,1)}, bf16[1152,576]{0,1:T(8,128)(2,1)}, bf16[576,1152]{1,0:T(8,128)(2,1)}) async-done(((bf16[1152,864]{0,1:T(8,128)(2,1)}, bf16[1152,432]{0,1:T(8,128)(2,1)}, bf16[144,1152]{1,0:T(8,128)(2,1)}, bf16[1152,576]{0,1:T(8,128)(2,1)}, bf16[576,1152]{1,0:T(8,128)(2,1)}), ...) | async-done | bytes 5971984 | tf_op jit(solution)/shard_map/psum | solution.py:297
  (290 shorter events, 113.0 us)
Async XLA Ops:
  7.2 5.5 copy-start
  7.2 153.4 %all-gather.5.cloned.1.call-start = ((), (), s32[]{:S(2)}) async-start(), calls=%async_computation.5 | async-start | bytes 7299072 | tf_op jit(solution)/shard_map/all_gather | solution.py:156
  7.3 72.4 %copy-start.65 = (s32[176]{0:T(256)}, s32[176]{0:T(256)S(1)}, u32[]{:S(2)}) copy-start(s32[176]{0:T(256)S(1)} %iota_add_fusion) | copy-start | bytes 2116
  9.4 77.9 %copy-start.48 = (f32[176,2]{0,1:T(2,128)}, f32[176,2]{0,1:T(2,128)S(1)}, u32[]{:S(2)}) copy-start(f32[176,2]{0,1:T(2,128)S(1)} %broadcast_multiply_fusion.5) | copy-start | bytes 4228
  10.9 76.4 %copy-start.56 = (f32[176,2]{0,1:T(2,128)}, f32[176,2]{0,1:T(2,128)S(1)}, u32[]{:S(2)}) copy-start(f32[176,2]{0,1:T(2,128)S(1)} %add_rsqrt_fusion.1) | copy-start | bytes 4228
  15.2 64.2 %copy-start.70 = (s32[2,11]{1,0:T(2,128)S(1)}, s32[2,11]{1,0:T(2,128)}, u32[]{:S(2)}) copy-start(s32[2,11]{1,0:T(2,128)} %param.26) | copy-start | bytes 268
  15.2 64.4 %copy-start.72 = (s32[2,11]{1,0:T(2,128)S(1)}, s32[2,11]{1,0:T(2,128)}, u32[]{:S(2)}) copy-start(s32[2,11]{1,0:T(2,128)} %param.27) | copy-start | bytes 268
  79.7 291.9 %copy-start.52 = (s32[2,11]{1,0:T(2,128)}, s32[2,11]{1,0:T(2,128)S(1)}, u32[]{:S(2)}) copy-start(s32[2,11]{1,0:T(2,128)S(1)} %reduce_window_sum.12) | copy-start | bytes 268
  79.7 291.9 %copy-start.54 = (s32[2,11]{1,0:T(2,128)}, s32[2,11]{1,0:T(2,128)S(1)}, u32[]{:S(2)}) copy-start(s32[2,11]{1,0:T(2,128)S(1)} %get-tuple-element.199) | copy-start | bytes 268
  79.7 11.2 copy-start.6
  92.2 272.4 %reduce-scatter.8.cloned.1.call-start = ((), (), s32[]{:S(2)}) async-start(), calls=%async_computation.6 | async-start | bytes 14598144 | tf_op jit(solution)/shard_map/reduce_scatter | solution.py:182
  179.4 7.7 copy-start.24
  206.7 7.7 copy-start.24
  232.8 203.3 %all-gather.7.cloned.1.call-start = ((), (), s32[]{:S(2)}) async-start(), calls=%async_computation.7 | async-start | bytes 7299072 | tf_op jit(solution)/shard_map/all_gather | solution.py:197
  233.5 133.4 %copy-start.40 = (f32[1152]{0:T(1024)}, f32[1152]{0:T(1024)S(1)}, u32[]{:S(2)}) copy-start(f32[1152]{0:T(1024)S(1)} %convert_element_type.189) | copy-start | bytes 13828
  366.9 4.3 copy-start.2
  366.9 450.6 %copy-start.42 = (f32[176,2]{0,1:T(2,128)}, f32[176,2]{0,1:T(2,128)S(1)}, u32[]{:S(2)}) copy-start(f32[176,2]{0,1:T(2,128)S(1)} %broadcast_multiply_fusion.4) | copy-start | bytes 4228
  367.2 450.3 %copy-start.50 = (f32[176,2]{0,1:T(2,128)}, f32[176,2]{0,1:T(2,128)S(1)}, u32[]{:S(2)}) copy-start(f32[176,2]{0,1:T(2,128)S(1)} %add_rsqrt_fusion) | copy-start | bytes 4228
  367.2 4.2 copy-start.71
  371.2 218.4 %reduce-scatter.10.cloned.1.call-start = ((), (), s32[]{:S(2)}) async-start(), calls=%async_computation.8 | async-start | bytes 14598144 | tf_op jit(solution)/shard_map/reduce_scatter | solution.py:205
  371.9 77.3 %copy-start.28 = (bf16[576,1152]{1,0:T(8,128)(2,1)S(1)}, bf16[576,1152]{1,0:T(8,128)(2,1)}, u32[]{:S(2)}) copy-start(bf16[576,1152]{1,0:T(8,128)(2,1)} %param.40) | copy-start | bytes 3981316
  457.9 131.8 %copy-start.14 = (bf16[176,2,1152]{2,1,0:T(2,128)(2,1)S(1)}, bf16[176,2,1152]{2,1,0:T(2,128)(2,1)}, u32[]{:S(2)}) copy-start(bf16[176,2,1152]{2,1,0:T(2,128)(2,1)} %param.43) | copy-start | bytes 2433028
  457.9 201.4 %all-gather.9.cloned.1.call-start = ((), (), s32[]{:S(2)}) async-start(), calls=%async_computation.9 | async-start | bytes 7299072 | tf_op jit(solution)/shard_map/all_gather | solution.py:218
  458.6 135.9 %copy-start.44 = (f32[1152]{0:T(1024)}, f32[1152]{0:T(1024)S(1)}, u32[]{:S(2)}) copy-start(f32[1152]{0:T(1024)S(1)} %convert_element_type.195) | copy-start | bytes 13828
  461.0 133.5 %copy-start.59 = (f32[176,2]{0,1:T(2,128)}, f32[176,2]{0,1:T(2,128)S(1)}, u32[]{:S(2)}) copy-start(f32[176,2]{0,1:T(2,128)S(1)} %convert_multiply_fusion.2) | copy-start | bytes 4228
  594.5 219.7 %reduce-scatter.12.cloned.1.call-start = ((), (), s32[]{:S(2)}) async-start(), calls=%async_computation.10 | async-start | bytes 14598144 | tf_op jit(solution)/shard_map/reduce_scatter | solution.py:229
  659.4 14.4 %copy-start.29 = (bf16[1152,576]{0,1:T(8,128)(2,1)S(1)}, bf16[1152,576]{0,1:T(8,128)(2,1)}, u32[]{:S(2)}) copy-start(bf16[1152,576]{0,1:T(8,128)(2,1)} %param.38) | copy-start | bytes 3981316
  682.4 203.6 %all-gather.11.cloned.1.call-start = ((), (), s32[]{:S(2)}) async-start(), calls=%async_computation.11 | async-start | bytes 7299072 | tf_op jit(solution)/shard_map/all_gather | solution.py:241
  682.5 134.9 %copy-start.38 = (f32[1152]{0:T(1024)}, f32[1152]{0:T(1024)S(1)}, u32[]{:S(2)}) copy-start(f32[1152]{0:T(1024)S(1)} %convert_element_type.200) | copy-start | bytes 13828
  682.5 134.9 %copy-start.46 = (f32[176,2]{0,1:T(2,128)}, f32[176,2]{0,1:T(2,128)S(1)}, u32[]{:S(2)}) copy-start(f32[176,2]{0,1:T(2,128)S(1)} %subtract_multiply_fusion.1) | copy-start | bytes 4228
  817.5 68.5 %copy-start.37 = (bf16[144,1152]{1,0:T(8,128)(2,1)S(1)}, bf16[144,1152]{1,0:T(8,128)(2,1)}, u32[]{:S(2)}) copy-start(bf16[144,1152]{1,0:T(8,128)(2,1)} %param.36) | copy-start | bytes 995332
  821.1 348.0 %reduce-scatter.14.cloned.1.call-start = ((), (), s32[]{:S(2)}) async-start(), calls=%async_computation.12 | async-start | bytes 14598144 | tf_op jit(solution)/shard_map/reduce_scatter | solution.py:266
  821.2 69.6 %copy-start.64 = (bf16[1408,2,2]{0,2,1:T(2,128)(2,1)S(1)}, bf16[1408,2,2]{0,2,1:T(2,128)(2,1)}, u32[]{:S(2)}) copy-start(bf16[1408,2,2]{0,2,1:T(2,128)(2,1)} %get-tuple-element.202) | copy-start | bytes 33796
  895.3 4.5 copy-start.8
  899.7 5.7 copy-start.1
  962.5 4.5 copy-start.8
  967.0 5.7 copy-start.1
  1037.3 204.4 %reduce-scatter.16.cloned.1.call-start = ((), (), s32[]{:S(2)}) async-start(), calls=%async_computation.13 | async-start | bytes 3981312
  1037.4 9.4 copy-start.13
  1046.8 122.3 %copy-start.7 = (bf16[176,2,1152]{2,1,0:T(2,128)(2,1)S(1)}, bf16[176,2,1152]{2,1,0:T(2,128)(2,1)}, u32[]{:S(2)}) copy-start(bf16[176,2,1152]{2,1,0:T(2,128)(2,1)} %param.24) | copy-start | bytes 2433028
  1046.8 122.3 %copy-start.49 = (f32[176,2]{0,1:T(2,128)S(1)}, f32[176,2]{0,1:T(2,128)}, u32[]{:S(2)}) copy-start(f32[176,2]{0,1:T(2,128)} %copy-done.48) | copy-start | bytes 4228
  1046.8 122.3 %copy-start.57 = (f32[176,2]{0,1:T(2,128)S(1)}, f32[176,2]{0,1:T(2,128)}, u32[]{:S(2)}) copy-start(f32[176,2]{0,1:T(2,128)} %copy-done.56) | copy-start | bytes 4228
  1199.5 181.4 %all-reduce.8.cloned.1.call-start = ((), (), s32[]{:S(2)}) async-start(), calls=%async_computation.14 | async-start | bytes 11943936 | tf_op jit(solution)/shard_map/psum | solution.py:297
  1200.6 5.0 copy-start.23
  1205.5 38.2 %copy-start.31 = (f32[2,11,576]{2,1,0:T(8,128)S(1)}, f32[2,11,576]{2,1,0:T(8,128)}, u32[]{:S(2)}) copy-start(f32[2,11,576]{2,1,0:T(8,128)} %copy-done.30) | copy-start | bytes 152068
  1205.5 38.2 %copy-start.33 = (f32[2,11,576]{2,1,0:T(8,128)S(1)}, f32[2,11,576]{2,1,0:T(8,128)}, u32[]{:S(2)}) copy-start(f32[2,11,576]{2,1,0:T(8,128)} %copy-done.32) | copy-start | bytes 152068
  1205.5 38.2 %copy-start.35 = (bf16[2,11,1152]{2,0,1:T(2,128)(2,1)S(1)}, bf16[2,11,1152]{2,0,1:T(2,128)(2,1)}, u32[]{:S(2)}) copy-start(bf16[2,11,1152]{2,0,1:T(2,128)(2,1)} %param.25) | copy-start | bytes 152068
  1250.1 5.6 copy-start.58
  (41 other events, 71.9 us)
Sparse Core Ops, SparseCore 0:
  92.4 68.1 all-gather.4
  233.0 131.5 reduce-scatter.7
  371.4 64.6 all-gather.6
  458.0 131.5 reduce-scatter.9
  594.6 64.6 all-gather.8
  682.6 131.5 reduce-scatter.11
  821.2 64.6 all-gather.10
  1037.5 131.5 reduce-scatter.13
  1199.6 42.1 reduce-scatter.15
  1247.1 133.7 all-reduce.7
where the time goes:
time: 1410 us; the launch traced here: 1400 us
  waiting for transfers between devices  848 us (60%)
  matrix products  270 us (19%)
  blocking collectives  128 us (9%)
  other arithmetic  81.9 us (6%)
  local copies, waits for them, and re-layouts  53.2 us (4%)
  between operations  15.9 us (1%)
    reduce_scatter x1, waiting for transfers between devices, per_device(): lax.psum_scatter(back_rows(upper_low, w_up), 'heads', scatter_dimension=0...  132 us
    reduce_scatter x1, waiting for transfers between devices, per_device(): lax.psum_scatter(project_rows(attn_low, w_out), 'heads', scatter_dimensio...  131 us
    reduce_scatter x1, waiting for transfers between devices, per_device(): lax.psum_scatter(project_rows(active_low, w_down), 'heads', scatter_dimen...  129 us
    reduce_scatter x1, waiting for transfers between devices, per_device(): lax.psum_scatter(back_rows(grad_triple, w_qkv), 'heads', scatter_dimensio...  114 us
    all_gather x1, waiting for transfers between devices, per_device(): hidden_all = lax.all_gather(hidden_one, 'heads', axis=0, tiled=True)  66.6 us
    all_gather x1, waiting for transfers between devices, per_device(): grad_proj_all = lax.all_gather(projected_low, 'heads', axis=0, tiled=True)  64.8 us
    all_gather x1, waiting for transfers between devices, per_device(): grad_all = lax.all_gather(grad_low, 'heads', axis=0, tiled=True)  64.6 us
    all_gather x1, waiting for transfers between devices, per_device(): hidden_two_all = lax.all_gather(hidden_two_low, 'heads', axis=0, tiled=True)  64.2 us
  transfers between devices with their start and end apart: 10, of which 10 were waited for; matrix products, arithmetic and copies ran while one was open for 4% of the time, Pallas kernels for 0%

commit v1 on v0

--- a/solution.py
+++ b/solution.py
@@ -2,7 +2,11 @@
 
 import jax
 import jax.numpy as jnp
+import numpy as np
 from jax import lax
+from jax.experimental import pallas as pl
+from jax.experimental.pallas import tpu as pltpu
+from jax.sharding import Mesh
 from jax.sharding import PartitionSpec as P
 
 D = 1152
@@ -10,10 +14,16 @@
 HD = 72
 GW = 288
 SEQ = 1408
-
-
+CROPS = 11
+UNIT = 64
+LANES = 128
 EPSILON = 1e-06
 MASKED_SCORE = -1000000000.0
+MESH = pl.DeviceIdType.MESH
+SWAP = [(0, 1), (1, 0)]
+F32 = jnp.float32
+BF16 = jnp.bfloat16
+SCALE = HD ** (-0.5)
 
 
 def time_embed(timesteps):
@@ -324,45 +334,681 @@
     )
 
 
+BLK = 176
+NH = 4
+HALF = SEQ // 2
+
+
+def block_place(scal, dq, dc, slot):
+    q = lax.rem(scal[0] + dq, 2)
+    c = lax.rem(scal[1] + dc, 2)
+    return pl.multiple_of(slot * HALF + q * (2 * BLK) + c * BLK, 16)
+
+
+def load_blocks(scal, refs, buf, sem):
+    copies = []
+    for dq in range(2):
+        for dc in range(2):
+            for slot in range(2):
+                copies.append(
+                    pltpu.make_async_copy(
+                        refs[dq].at[dc, slot],
+                        buf.at[pl.ds(block_place(scal, dq, dc, slot), BLK)],
+                        sem.at[dq * 4 + dc * 2 + slot],
+                    )
+                )
+    for copy in copies:
+        copy.start()
+    return copies
+
+
+def store_blocks(scal, buf, refs, sem):
+    copies = []
+    for dq in range(2):
+        for dc in range(2):
+            for slot in range(2):
+                copies.append(
+                    pltpu.make_async_copy(
+                        buf.at[pl.ds(block_place(scal, dq, dc, slot), BLK)],
+                        refs[dq].at[dc, slot],
+                        sem.at[dq * 4 + dc * 2 + slot],
+                    )
+                )
+    for copy in copies:
+        copy.start()
+    for copy in copies:
+        copy.wait()
+
+
+def each_crop(scal, body):
+    def step(item, carry):
+        units = scal[2 + CROPS + item]
+        for count in range(2, 9):
+
+            @pl.when(units == count)
+            def _():
+                body(item, pl.multiple_of(scal[2 + item], UNIT), count * UNIT)
+
+        return carry
+
+    lax.fori_loop(0, CROPS, step, 0)
+
+
+def nt(a, b):
+    return lax.dot_general(a, b, (((1,), (1,)), ((), ())), preferred_element_type=F32)
+
+
+def tn(a, b):
+    return lax.dot_general(a, b, (((0,), (0,)), ((), ())), preferred_element_type=F32)
+
+
+def attn_fwd_kernel(scal, t0, t1, pack, o0, o1, lse, buf, obuf, sem):
+    for copy in load_blocks(scal, (t0, t1), buf, sem):
+        copy.wait()
+    lane = lax.broadcasted_iota(jnp.int32, (1, LANES), 1)
+
+    def body(item, start, size):
+        live = scal[2 + 2 * CROPS + item]
+        keys_live = lax.broadcasted_iota(jnp.int32, (1, size), 1) < live
+        rows_live = (lax.broadcasted_iota(jnp.int32, (size, 1), 0) < live).astype(F32)
+        window = pl.ds(start, size)
+        packed = jnp.zeros((size, NH * HD), F32)
+        totals = jnp.zeros((size, LANES), F32)
+        for head in range(NH):
+            at = head * 3 * LANES
+            queries = buf[window, at : at + LANES]
+            keys = buf[window, at + LANES : at + 2 * LANES]
+            values = buf[window, at + 2 * LANES : at + 3 * LANES]
+            scores = jnp.where(keys_live, nt(queries, keys) * SCALE, MASKED_SCORE)
+            top = jnp.max(scores, axis=1, keepdims=True)
+            expo = jnp.exp(scores - top)
+            total = jnp.sum(expo, axis=1, keepdims=True)
+            prob = (expo * (1.0 / total)).astype(BF16)
+            mixed = jnp.dot(prob, values, preferred_element_type=F32)
+            mask = scal[2 + 3 * CROPS + item * NH + head].astype(F32)
+            mixed = (mixed * (rows_live * mask)).astype(BF16)
+            packed += jnp.dot(
+                mixed, pack[head * LANES : (head + 1) * LANES, :], preferred_element_type=F32
+            )
+            totals = jnp.where(lane == head, top + jnp.log(total), totals)
+        obuf[window, :] = packed.astype(BF16)
+        lse[window, :] = totals
+
+    each_crop(scal, body)
+    store_blocks(scal, obuf, (o0, o1), sem)
+
+
+def attn_bwd_kernel(scal, t0, t1, g0, g1, lse, pack, d0, d1, buf, gbuf, dbuf, sem, gsem):
+    first = load_blocks(scal, (t0, t1), buf, sem)
+    second = load_blocks(scal, (g0, g1), gbuf, gsem)
+    for copy in first + second:
+        copy.wait()
+
+    def body(item, start, size):
+        live = scal[2 + 2 * CROPS + item]
+        keys_live = lax.broadcasted_iota(jnp.int32, (1, size), 1) < live
+        rows_live = lax.broadcasted_iota(jnp.int32, (size, 1), 0) < live
+        window = pl.ds(start, size)
+        grads = gbuf[window, :]
+        grads = jnp.where(rows_live, grads.astype(F32), 0.0).astype(BF16)
+        for head in range(NH):
+            at = head * 3 * LANES
+            queries = buf[window, at : at + LANES]
+            keys = buf[window, at + LANES : at + 2 * LANES]
+            values = buf[window, at + 2 * LANES : at + 3 * LANES]
+            mask = scal[2 + 3 * CROPS + item * NH + head].astype(F32)
+            grad = (nt(grads, pack[head * LANES : (head + 1) * LANES, :]) * mask).astype(BF16)
+            scores = jnp.where(keys_live, nt(queries, keys) * SCALE, MASKED_SCORE)
+            prob = jnp.exp(scores - lse[window, head : head + 1])
+            grad_prob = nt(grad, values)
+            grad_values = tn(prob.astype(BF16), grad)
+            inner = jnp.sum(prob * grad_prob, axis=1, keepdims=True)
+            grad_raw = (prob * (grad_prob - inner) * SCALE).astype(BF16)
+            dbuf[window, at : at + LANES] = jnp.dot(
+                grad_raw, keys, preferred_element_type=F32
+            ).astype(BF16)
+            dbuf[window, at + LANES : at + 2 * LANES] = tn(grad_raw, queries).astype(BF16)
+            dbuf[window, at + 2 * LANES : at + 3 * LANES] = grad_values.astype(BF16)
+
+    each_crop(scal, body)
+    store_blocks(scal, dbuf, (d0, d1), sem)
+
+
+WIDE = NH * 3 * LANES
+SMEM_SPEC = pl.BlockSpec(memory_space=pltpu.SMEM)
+VMEM_SPEC = pl.BlockSpec(memory_space=pltpu.VMEM)
+ANY_SPEC = pl.BlockSpec(memory_space=pl.ANY)
+
+
+def attn_fwd(scal, t0, t1, pack):
+    return pl.pallas_call(
+        attn_fwd_kernel,
+        out_shape=(
+            jax.ShapeDtypeStruct((2, 2, BLK, NH * HD), BF16),
+            jax.ShapeDtypeStruct((2, 2, BLK, NH * HD), BF16),
+            jax.ShapeDtypeStruct((SEQ, LANES), F32),
+        ),
+        in_specs=[SMEM_SPEC, ANY_SPEC, ANY_SPEC, VMEM_SPEC],
+        out_specs=(ANY_SPEC, ANY_SPEC, VMEM_SPEC),
+        scratch_shapes=[
+            pltpu.VMEM((SEQ, WIDE), BF16),
+            pltpu.VMEM((SEQ, NH * HD), BF16),
+            pltpu.SemaphoreType.DMA((8,)),
+        ],
+        compiler_params=pltpu.CompilerParams(vmem_limit_bytes=48 * 2**20),
+        cost_estimate=pl.CostEstimate(
+            flops=4 * 10**9, bytes_accessed=6 * 10**6, transcendentals=4 * 10**6
+        ),
+        name="attn_fwd",
+    )(scal, t0, t1, pack)
+
+
+def attn_bwd(scal, t0, t1, g0, g1, lse, pack):
+    return pl.pallas_call(
+        attn_bwd_kernel,
+        out_shape=(
+            jax.ShapeDtypeStruct((2, 2, BLK, WIDE), BF16),
+            jax.ShapeDtypeStruct((2, 2, BLK, WIDE), BF16),
+        ),
+        in_specs=[SMEM_SPEC] + [ANY_SPEC] * 4 + [VMEM_SPEC] * 2,
+        out_specs=(ANY_SPEC, ANY_SPEC),
+        scratch_shapes=[
+            pltpu.VMEM((SEQ, WIDE), BF16),
+            pltpu.VMEM((SEQ, NH * HD), BF16),
+            pltpu.VMEM((SEQ, WIDE), BF16),
+            pltpu.SemaphoreType.DMA((8,)),
+            pltpu.SemaphoreType.DMA((8,)),
+        ],
+        compiler_params=pltpu.CompilerParams(vmem_limit_bytes=48 * 2**20),
+        cost_estimate=pl.CostEstimate(
+            flops=12 * 10**9, bytes_accessed=12 * 10**6, transcendentals=4 * 10**6
+        ),
+        name="attn_bwd",
+    )(scal, t0, t1, g0, g1, lse, pack)
+
+
+def line_kernel(pick, src, out, send_sem, recv_sem, loc_sem):
+    p, q, c = lax.axis_index("p"), lax.axis_index("q"), lax.axis_index("c")
+    me = p * 4 + q * 2 + c
+    peers = []
+    for k in range(1, 8):
+        pp, qq, cc = lax.rem(p + k // 4, 2), lax.rem(q + (k // 2) % 2, 2), lax.rem(c + k % 2, 2)
+        peers.append((pp, qq, cc))
+    barrier = pltpu.get_barrier_semaphore()
+    for pp, qq, cc in peers:
+        pl.semaphore_signal(
+            barrier, inc=1, device_id={"p": pp, "q": qq, "c": cc}, device_id_type=MESH
+        )
+    pl.semaphore_wait(barrier, 7)
+
+    def source(pp, qq, cc):
+        if pick == "row":
+            return src.at[pp]
+        if pick == "all":
+            return src
+        return src.at[pp * 4 + qq * 2 + cc]
+
+    copies = []
+    for k, (pp, qq, cc) in enumerate(peers):
+        copy = pltpu.make_async_remote_copy(
+            src_ref=source(pp, qq, cc),
+            dst_ref=out.at[me],
+            send_sem=send_sem.at[k],
+            recv_sem=recv_sem.at[k],
+            device_id={"p": pp, "q": qq, "c": cc},
+            device_id_type=MESH,
+        )
+        copy.start()
+        copies.append(copy)
+    own = pltpu.make_async_copy(source(p, q, c), out.at[me], loc_sem)
+    own.start()
+    own.wait()
+    for copy in copies:
+        copy.wait()
+
+
+def line_exchange(src, pick, collective_id, name):
+    shape = src.shape if pick == "all" else src.shape[1:]
+    return pl.pallas_call(
+        lambda *refs: line_kernel(pick, *refs),
+        out_shape=jax.ShapeDtypeStruct((8,) + shape, src.dtype),
+        in_specs=[VMEM_SPEC],
+        out_specs=VMEM_SPEC,
+        scratch_shapes=[
+            pltpu.SemaphoreType.DMA((7,)),
+            pltpu.SemaphoreType.DMA((7,)),
+            pltpu.SemaphoreType.DMA,
+        ],
+        compiler_params=pltpu.CompilerParams(collective_id=collective_id, has_side_effects=True),
+        name=name,
+    )(src)
+
+
+def plane_kernel(src, out, send_sem, recv_sem, loc_sem):
+    y, x = lax.axis_index("y"), lax.axis_index("x")
+    me = y * 2 + x
+    peers = [(lax.rem(y + k // 2, 2), lax.rem(x + k % 2, 2)) for k in range(1, 4)]
+    barrier = pltpu.get_barrier_semaphore()
+    for yy, xx in peers:
+        pl.semaphore_signal(barrier, inc=1, device_id={"y": yy, "x": xx}, device_id_type=MESH)
+    pl.semaphore_wait(barrier, 3)
+    copies = []
+    for k, (yy, xx) in enumerate(peers):
+        copy = pltpu.make_async_remote_copy(
+            src_ref=src,
+            dst_ref=out.at[me],
+            send_sem=send_sem.at[k],
+            recv_sem=recv_sem.at[k],
+            device_id={"y": yy, "x": xx},
+            device_id_type=MESH,
+        )
+        copy.start()
+        copies.append(copy)
+    own = pltpu.make_async_copy(src, out.at[me], loc_sem)
+    own.start()
+    own.wait()
+    for copy in copies:
+        copy.wait()
+
+
+def plane_exchange(src, collective_id, name):
+    return pl.pallas_call(
+        plane_kernel,
+        out_shape=jax.ShapeDtypeStruct((4,) + src.shape, src.dtype),
+        in_specs=[VMEM_SPEC],
+        out_specs=VMEM_SPEC,
+        scratch_shapes=[
+            pltpu.SemaphoreType.DMA((3,)),
+            pltpu.SemaphoreType.DMA((3,)),
+            pltpu.SemaphoreType.DMA,
+        ],
+        compiler_params=pltpu.CompilerParams(collective_id=collective_id, has_side_effects=True),
+        name=name,
+    )(src)
+
+
+def swap(values, axis):
+    return lax.ppermute(values, axis, SWAP)
+
+
+def at_index(stacked, index):
+    return lax.dynamic_index_in_dim(stacked, index, 0, keepdims=False)
+
+
+def plane_gather(part, rank):
+    half = part.shape[0] // 2
+    by_x = swap(part, "x")
+    by_y = swap(part, "y")
+    far = jnp.concatenate([swap(by_x[:half], "y"), swap(by_y[half:], "x")], axis=0)
+    out = jnp.zeros((4,) + part.shape, part.dtype)
+    for k, block in enumerate((part, by_x, by_y, far)):
+        out = lax.dynamic_update_index_in_dim(out, block, rank ^ k, 0)
+    return out
+
+
+def plane_scatter(parts, rank):
+    half = parts.shape[1] // 2
+    rel = [at_index(parts, rank ^ k) for k in range(4)]
+    low = [v[:half] for v in rel]
+    high = [v[half:] for v in rel]
+    in_x = swap(jnp.stack([low[1], low[3]]), "x").astype(F32)
+    in_y = swap(jnp.stack([high[2], high[3]]), "y").astype(F32)
+    low_own = low[0].astype(F32) + in_x[0]
+    high_own = high[0].astype(F32) + in_y[0]
+    low_rest = (low[2].astype(F32) + in_x[1]).astype(BF16)
+    high_rest = (high[1].astype(F32) + in_y[1]).astype(BF16)
+    low_own = low_own + swap(low_rest, "y").astype(F32)
+    high_own = high_own + swap(high_rest, "x").astype(F32)
+    return jnp.concatenate([low_own, high_own], axis=0)
+
+
+def layer_device(
+    tokens, cond, lengths, pads, timesteps, head_mask, group_mask, keep, ada_w, ada_b, w_qkv, b_qv,
+    w_out, b_out, w_up, b_up, w_down, b_down, w_route, grad_out,
+):
+    highest = lax.Precision.HIGHEST
+    y, x, p, q, c = (lax.axis_index(name) for name in "yxpqc")
+    rank = y * 2 + x
+    first = p == 0
+    shard = p * 4 + q * 2 + c
+    partner = shard ^ 4
+
+    def to_rows(values):
+        mine = jnp.where(first, values[:, 0], values[:, 1])
+        other = swap(jnp.where(first, values[:, 1], values[:, 0]), "p")
+        return jnp.stack([jnp.where(first, mine, other), jnp.where(first, other, mine)])
+
+    def other_shard(weight):
+        quarter = weight.shape[0] // 4
+        mine = lax.dynamic_slice_in_dim(weight, rank * quarter, quarter, 0)
+        return plane_gather(swap(mine, "p"), rank).reshape(weight.shape)
+
+    token_low = to_rows(tokens)
+    spread = np.zeros((6 * HD, 6 * LANES), np.float32)
+    for unit in range(6):
+        spread[np.arange(HD) + unit * HD, np.arange(HD) + unit * LANES] = 1.0
+    spread = jnp.asarray(spread, BF16)
+    qkv_other = other_shard(w_qkv)
+    w_qkv_wide = jnp.concatenate(
+        [
+            jnp.dot(w_qkv, spread, preferred_element_type=F32).astype(BF16),
+            jnp.dot(qkv_other, spread, preferred_element_type=F32).astype(BF16),
+        ],
+        axis=1,
+    )
+    biases = jnp.concatenate([b_up, b_qv])
+    biases_other = swap(biases, "p")
+    pairs = jnp.stack([b_qv, biases_other[2 * GW :]]).reshape(4, 2, HD).astype(F32)
+    bias_wide = jnp.pad(
+        jnp.stack([pairs[:, 0], jnp.zeros_like(pairs[:, 0]), pairs[:, 1]], axis=1),
+        ((0, 0), (0, 0), (0, LANES - HD)),
+    ).reshape(WIDE)
+
+    cvec = cond.astype(F32) + time_embed(timesteps)
+    sig = lax.logistic(cvec)
+    act_low = jnp.pad((cvec * sig).astype(BF16), ((0, 0), (0, 5), (0, 0)))
+    mod_part = jnp.einsum("bcd,dm->bcm", act_low, ada_w, preferred_element_type=F32) + ada_b.astype(
+        F32
+    )
+    mod = line_exchange(mod_part, "row", 1, "mod_exchange")
+    mod = jnp.transpose(mod, (1, 0, 2)).reshape(16, 6 * D)
+
+    def row_of(values):
+        return jnp.where(first, values[0], values[1])
+
+    row_len = row_of(lengths)
+    row_pad = row_of(pads)
+    ends = jnp.cumsum(row_len)
+    starts = ends - row_len
+
+    def group_hot(dq, dc):
+        base = (q ^ dq) * (2 * BLK) + (c ^ dc) * BLK
+        places = base + jnp.arange(2)[:, None] * HALF + jnp.arange(BLK // 16)[None, :] * 16
+        inside = (places[..., None] >= starts) & (places[..., None] < ends)
+        return jnp.pad(inside.astype(F32), ((0, 0), (0, 0), (0, 5)))
+
+    hot = group_hot(0, 0)
+    mod_groups = jnp.einsum("sgc,cm->sgm", hot, mod, precision=highest)
+    shift_one, scale_one, gate_one, shift_two, scale_two, gate_two = (
+        mod_groups[:, :, None, k * D : (k + 1) * D] for k in range(6)
+    )
+
+    def grouped(values):
+        return values.reshape(2, BLK // 16, 16, -1)
+
+    def flat(values):
+        return values.reshape(2, BLK, -1)
+
+    token_values = grouped(token_low.astype(F32))
+    normed_one, inverse_one = norm_rows(token_values)
+    hidden_one = flat((normed_one * (1.0 + scale_one) + shift_one).astype(BF16))
+
+    def group_gather(block):
+        far = swap(block, "q")
+        near = swap(block, "c")
+        far_near = swap(far, "c")
+        return (
+            jnp.stack([block, near]).reshape(4 * BLK, -1),
+            jnp.stack([far, far_near]).reshape(4 * BLK, -1),
+        )
+
+    def group_scatter(near_part, far_part):
+        far_sum = (far_part[0].astype(F32) + swap(far_part[1], "c").astype(F32)).astype(BF16)
+        far_in = swap(far_sum, "q")
+        near_sum = near_part[0].astype(F32) + swap(near_part[1], "c").astype(F32)
+        return near_sum + far_in.astype(F32)
+
+    h1_near, h1_far = group_gather(hidden_one)
+
+    def project(h):
+        return (
+            (jnp.dot(h, w_qkv_wide, preferred_element_type=F32) + bias_wide)
+            .astype(BF16)
+            .reshape(2, 2, BLK, WIDE)
+        )
+
+    t_near, t_far = project(h1_near), project(h1_far)
+
+    head_row = row_of(head_mask)
+    heads_here = jnp.concatenate(
+        [
+            lax.dynamic_slice_in_dim(head_row, shard * 2, 2, 1),
+            lax.dynamic_slice_in_dim(head_row, partner * 2, 2, 1),
+        ],
+        axis=1,
+    )
+    scal = jnp.concatenate(
+        [
+            jnp.stack([q, c]).astype(jnp.int32),
+            starts,
+            row_len // UNIT,
+            row_len - row_pad,
+            heads_here.reshape(-1),
+        ]
+    ).astype(jnp.int32)
+    pack = np.zeros((NH * LANES, NH * HD), np.float32)
+    for head in range(NH):
+        pack[np.arange(HD) + head * LANES, np.arange(HD) + head * HD] = 1.0
+    pack = jnp.asarray(pack, BF16)
+    o_near, o_far, lse = attn_fwd(scal, t_near, t_far, pack)
+
+    w_out_two = jnp.concatenate([w_out, other_shard(w_out)], axis=0)
+    w_out_far = swap(w_out_two, "q")
+    o_mine = o_near.reshape(4 * BLK, NH * HD)
+    o_in = swap(o_far, "q").reshape(4 * BLK, NH * HD)
+    y_part = jnp.dot(o_mine, w_out_two, preferred_element_type=F32) + jnp.dot(
+        o_in, w_out_far, preferred_element_type=F32
+    )
+    y_part = y_part.astype(BF16).reshape(2, 2, BLK, D)
+    projected = grouped(y_part[0].astype(F32) + swap(y_part[1], "c").astype(F32))
+    branch_one = projected + b_out.astype(F32)
+    mixed = token_values + gate_one * branch_one
+    normed_two, inverse_two = norm_rows(mixed)
+    hidden_two = normed_two * (1.0 + scale_two) + shift_two
+    route_w = w_route.astype(F32)
+    route = lax.logistic(jnp.sum(hidden_two * route_w, axis=-1, keepdims=True))
+    keep_values = grouped(to_rows(keep.astype(F32)[..., None]))
+    route_keep = keep_values * route
+    grad_low = to_rows(grad_out)
+    grad_final = grouped(grad_low.astype(F32))
+    grad_branch = grad_final * gate_two * route_keep
+    h2_near, h2_far = group_gather(flat(hidden_two.astype(BF16)))
+    dz_near, dz_far = group_gather(flat(grad_branch.astype(BF16)))
+
+    w_up_two = jnp.concatenate([w_up, other_shard(w_up)], axis=1)
+    w_down_two = jnp.concatenate([w_down, other_shard(w_down)], axis=0)
+    b_up_two = jnp.concatenate([b_up, biases_other[: 2 * GW]]).astype(F32)
+    group_row = row_of(group_mask)
+    groups_here = jnp.concatenate(
+        [
+            lax.dynamic_slice_in_dim(group_row, shard * 2, 2, 1),
+            lax.dynamic_slice_in_dim(group_row, partner * 2, 2, 1),
+        ],
+        axis=1,
+    ).astype(F32)
+    groups_here = jnp.pad(groups_here, ((0, 5), (0, 0)))
+
+    def feed(h2, dz, dq):
+        hots = jnp.stack([group_hot(dq, 0), group_hot(dq, 1)])
+        mask = jnp.einsum("usgc,ch->usgh", hots, groups_here, precision=highest)
+        mask = jnp.repeat(mask, GW, axis=-1)[:, :, :, None, :]
+
+        def spread_mask(values):
+            return (values.reshape(2, 2, BLK // 16, 16, 4 * GW) * mask).reshape(4 * BLK, 4 * GW)
+
+        upper = jnp.dot(h2, w_up_two, preferred_element_type=F32) + b_up_two
+        active, back = jax.vjp(gelu_tanh, upper)
+        active_low = spread_mask(active).astype(BF16)
+        z_part = jnp.dot(active_low, w_down_two, preferred_element_type=F32).astype(BF16)
+        grad_active = lax.dot_general(
+            dz, w_down_two, (((1,), (1,)), ((), ())), preferred_element_type=F32
+        )
+        (grad_upper,) = back(spread_mask(grad_active))
+        upper_low = grad_upper.astype(BF16)
+        dh_part = lax.dot_general(
+            upper_low, w_up_two, (((1,), (1,)), ((), ())), preferred_element_type=F32
+        ).astype(BF16)
+        return active_low, upper_low, z_part.reshape(2, 2, BLK, D), dh_part.reshape(2, 2, BLK, D)
+
+    a_far, u_far, z_far, dh_far = feed(h2_far, dz_far, 1)
+    a_near, u_near, z_near, dh_near = feed(h2_near, dz_near, 0)
+    lowered = grouped(group_scatter(z_near, z_far))
+    grad_hidden_two = grouped(group_scatter(dh_near, dh_far))
+    grad_w_up = tn(h2_near, u_near) + tn(h2_far, u_far)
+    grad_w_down = tn(a_near, dz_near) + tn(a_far, dz_far)
+    grad_b_up = jnp.sum(u_near, axis=0, dtype=F32) + jnp.sum(u_far, axis=0, dtype=F32)
+
+    branch = lowered + b_down.astype(F32)
+    final = mixed + gate_two * route_keep * branch
+    grad_gate_two = grad_final * route_keep * branch
+    grad_logit = (
+        jnp.sum(grad_final * gate_two * branch, axis=-1, keepdims=True)
+        * keep_values
+        * route
+        * (1.0 - route)
+    )
+    part_route = jnp.sum(grad_logit * hidden_two, axis=(0, 1, 2))
+    part_b_down = jnp.sum(grad_branch, axis=(0, 1, 2))
+    grad_hidden_two = grad_hidden_two + grad_logit * route_w
+    grad_scale_two = grad_hidden_two * normed_two
+    grad_mixed = grad_final + norm_back(
+        grad_hidden_two * (1.0 + scale_two), normed_two, inverse_two
+    )
+    grad_gate_one = grad_mixed * branch_one
+    grad_projected = grad_mixed * gate_one
+    part_b_out = jnp.sum(grad_projected, axis=(0, 1, 2))
+    dy_own = flat(grad_projected.astype(BF16))
+    dy = jnp.stack([dy_own, swap(dy_own, "c")]).reshape(4 * BLK, D)
+    do_out = nt(dy, w_out_far).astype(BF16).reshape(2, 2, BLK, NH * HD)
+    do_far = swap(do_out, "q")
+    do_near = nt(dy, w_out_two).astype(BF16).reshape(2, 2, BLK, NH * HD)
+    d_near, d_far = attn_bwd(scal, t_near, t_far, do_near, do_far, lse, pack)
+    d_near = d_near.reshape(4 * BLK, WIDE)
+    d_far = d_far.reshape(4 * BLK, WIDE)
+    dh1_far = nt(d_far, w_qkv_wide).astype(BF16).reshape(2, 2, BLK, D)
+    dh1_near = nt(d_near, w_qkv_wide).astype(BF16).reshape(2, 2, BLK, D)
+    grad_hidden_one = grouped(group_scatter(dh1_near, dh1_far))
+
+    def reduce_pair(mine, other):
+        both = plane_scatter(jnp.concatenate([mine, other], axis=2), rank)
+        width = mine.shape[2]
+        total = both[:, :width] + swap(both[:, width:].astype(BF16), "p").astype(F32)
+        return plane_gather(total.astype(BF16), rank).astype(F32)
+
+    down_low = grad_w_down.astype(BF16).reshape(2, 4, GW // 2, D)
+    out_w_down = reduce_pair(down_low[0], down_low[1]).reshape(2 * GW, D)
+    up_low = grad_w_up.astype(BF16).reshape(4, D // 4, 4 * GW)
+    out_w_up = reduce_pair(up_low[:, :, : 2 * GW], up_low[:, :, 2 * GW :]).reshape(D, 2 * GW)
+    wo_near = tn(o_mine, dy).astype(BF16)
+    wo_far = swap(tn(o_in, dy).astype(BF16), "q").astype(F32)
+    wo_low = (wo_near.astype(F32) + wo_far).astype(BF16).reshape(2, 4, HD // 2, D)
+    out_w_out = reduce_pair(wo_low[0], wo_low[1]).reshape(2 * HD, D)
+    wide_low = (tn(h1_near, d_near) + tn(h1_far, d_far)).astype(BF16)
+    narrow = [
+        nt(wide_low[:, k * 6 * LANES : (k + 1) * 6 * LANES], spread)
+        .astype(BF16)
+        .reshape(4, D // 4, 6 * HD)
+        for k in range(2)
+    ]
+    out_w_qkv = reduce_pair(narrow[0], narrow[1]).reshape(D, 6 * HD)
+
+    grad_tokens = flat(
+        grad_mixed + norm_back(grad_hidden_one * (1.0 + scale_one), normed_one, inverse_one)
+    )
+
+    def from_rows(values, dtype):
+        mine = jnp.where(first, values[0], values[1])
+        other = swap(jnp.where(first, values[1], values[0]).astype(BF16), "p").astype(dtype)
+        return jnp.stack(
+            [jnp.where(first, mine, other), jnp.where(first, other, mine)], axis=1
+        ).astype(dtype)
+
+    out_final = from_rows(flat(final.astype(BF16)), BF16)
+    out_tokens = from_rows(grad_tokens, F32)
+
+    group_sums = [
+        jnp.sum(v, axis=2)
+        for v in (
+            grad_hidden_one,
+            grad_hidden_one * normed_one,
+            grad_gate_one,
+            grad_hidden_two,
+            grad_scale_two,
+            grad_final * route_keep * branch,
+        )
+    ]
+    part_mod = jnp.einsum(
+        "sgc,sgm->cm", hot, jnp.concatenate(group_sums, axis=-1), precision=highest
+    )[:CROPS]
+    part_mod = jnp.transpose(part_mod.reshape(CROPS, 8, 6 * D // 8), (1, 0, 2))
+    smalls = jnp.stack([part_b_out, part_b_down, part_route]).reshape(3, 8, D // 8)
+    smalls = jnp.pad(jnp.transpose(smalls, (1, 0, 2)), ((0, 0), (0, 0), (0, 5 * D // 8)))
+    d_ones = jnp.sum(d_near, axis=0, dtype=F32) + jnp.sum(d_far, axis=0, dtype=F32)
+    d_ones = d_ones.reshape(2, 2, 3, LANES)[..., :HD]
+    qv_sums = jnp.stack([d_ones[:, :, 0], d_ones[:, :, 2]], axis=2).reshape(2, 4 * HD)
+    bias_sums = jnp.concatenate([grad_b_up.reshape(2, 2 * GW), qv_sums], axis=1)
+    who = jnp.arange(8)[:, None]
+    bias_rows = jnp.where(
+        who == shard, bias_sums[0], jnp.where(who == partner, bias_sums[1], 0.0)
+    )
+    parcel = jnp.concatenate(
+        [part_mod, smalls, bias_rows[:, None], jnp.zeros((8, 1, 6 * D // 8), F32)], axis=1
+    )
+    parcels = line_exchange(parcel, "slice", 2, "dmod_exchange")
+    line_sum = jnp.sum(parcels.reshape(2, 4, 16, 6 * D // 8), axis=1)
+    line_low = line_sum.astype(BF16)
+    mod_low = line_low[:, :CROPS]
+    act_all = plane_exchange(act_low, 3, "act_exchange")
+    plane_low = plane_exchange(line_low, 4, "small_exchange")
+    mod_all = plane_low[:, :, :CROPS]
+    grad_ada_w = jnp.einsum(
+        "rbcd,rbcm->dm", act_all[:, :, :CROPS], mod_all, preferred_element_type=F32
+    )
+    grad_ada_b = jnp.sum(mod_all, axis=(0, 1, 2), dtype=F32)
+    rest = jnp.sum(plane_low[:, :, CROPS:], axis=(0, 1), dtype=F32)
+    grad_b_out, grad_b_down, grad_w_route = (rest[k, : D // 8] for k in range(3))
+    out_b_up = rest[3, : 2 * GW]
+    out_b_qv = rest[3, 2 * GW :]
+    part_activ = jnp.einsum("bcm,dm->bcd", mod_low, ada_w, preferred_element_type=F32)
+    part_activ = jnp.pad(part_activ.astype(BF16), ((0, 0), (0, 5), (0, 0)))
+    grad_activ = jnp.sum(
+        line_exchange(part_activ, "all", 5, "cond_exchange").astype(F32), axis=0
+    )[:, :CROPS]
+    grad_cond = grad_activ * sig * (1.0 + cvec * (1.0 - sig))
+    return (
+        out_final, out_tokens, grad_cond, grad_ada_w, grad_ada_b, out_w_qkv, out_b_qv, out_w_out,
+        grad_b_out, out_w_up, out_b_up, out_w_down, grad_b_down, grad_w_route,
+    )
+
+
+IN_SPECS = (
+    ("heads", "rows", None), ("rows", None, None), ("rows", None), ("rows", None), ("rows", None),
+    ("rows", None, None), ("rows", None, None), ("heads", "rows"), (None, "heads"), ("heads",),
+    (None, "heads"), ("heads",), ("heads", None), (), (None, "heads"), ("heads",), ("heads", None),
+    (), (), ("heads", "rows", None),
+)
+OUT_SPECS = (
+    ("heads", "rows", None), ("heads", "rows", None), ("rows", None, None), (None, "heads"),
+    ("heads",), (None, "heads"), ("heads",), ("heads", None), ("heads",), (None, "heads"),
+    ("heads",), ("heads", None), ("heads",), ("heads",),
+)
+
+
 def solution(mesh):
-    in_specs = (
-        P("heads", "rows", None),
-        P("rows", None, None),
-        P("rows", None),
-        P("rows", None),
-        P("rows", None),
-        P("rows", None, None),
-        P("rows", None, None),
-        P("heads", "rows"),
-        P(None, "heads"),
-        P("heads"),
-        P(None, "heads"),
-        P("heads"),
-        P("heads", None),
-        P(),
-        P(None, "heads"),
-        P("heads"),
-        P("heads", None),
-        P(),
-        P(),
-        P("heads", "rows", None),
-    )
-    out_specs = (
-        P("heads", "rows", None),
-        P("heads", "rows", None),
-        P("rows", None, None),
-        P(None, "heads"),
-        P("heads"),
-        P(None, "heads"),
-        P("heads"),
-        P("heads", None),
-        P("heads"),
-        P(None, "heads"),
-        P("heads"),
-        P("heads", None),
-        P("heads"),
-        P("heads"),
-    )
+    paired = mesh.shape["rows"] == 4 and mesh.shape["heads"] == 8
+    if paired:
+        mesh = Mesh(mesh.devices.reshape(2, 2, 2, 2, 2), ("y", "x", "p", "q", "c"))
+        names = {"rows": ("y", "x"), "heads": ("p", "q", "c"), None: None}
+    else:
+        names = {"rows": "rows", "heads": "heads", None: None}
+
+    def specs(items):
+        return tuple(P(*(names[name] for name in item)) for item in items)
+
     return jax.shard_map(
-        per_device, mesh=mesh, in_specs=in_specs, out_specs=out_specs, check_vma=False
-    )
+        layer_device if paired else per_device,
+        mesh=mesh,
+        in_specs=specs(IN_SPECS),
+        out_specs=specs(OUT_SPECS),
+        check_vma=False,
+    )

time: 1410 us -> 759 us (0.54)
  waiting for transfers between devices: 848 us -> 163 us
  matrix products: 270 us -> 102 us
  Pallas kernels: 0 us -> 138 us
  blocking collectives: 128 us -> 0 us
  starting transfers between devices: 1.05 us -> 88.3 us
  local copies, waits for them, and re-layouts: 53.2 us -> 138 us
  other arithmetic: 81.9 us -> 120 us
    reduce_scatter x4 -> x0, waiting for transfers between devices: 505 us -> none  [the longest x1 132 us: per_device(): lax.psum_scatter(back_rows(upper_low, w_up), 'heads', scatter_dimension=0...]
    all_gather x4 -> x0, waiting for transfers between devices: 260 us -> none  [the longest x1 66.6 us: per_device(): hidden_all = lax.all_gather(hidden_one, 'heads', axis=0, tiled=True)]
    dot_general x35, matrix products: 270 us -> 102 us  [the longest x8 24.7 us: tn(): lax.dot_general(a, b, (((0,), (0,)), ((), ())), preferred_element_type=F32)]
    ppermute x0 -> x86, waiting for transfers between devices: none -> 163 us  [swap(): return lax.ppermute(values, axis, SWAP)]
    pallas_call x0 -> x7, Pallas kernels: none -> 138 us  [the longest x3 89.3 us: line_exchange(): pl.pallas_call(lambda *refs: line_kernel(pick, *refs), out_shape=jax.Shap...]
    ppermute x0 -> x86, starting transfers between devices: none -> 88.3 us  [swap(): return lax.ppermute(values, axis, SWAP)]
    all_gather x1 -> x0, blocking collectives: 64.2 us -> none  [per_device(): modulation = lax.all_gather(modulation_part, 'heads', axis=2, tiled=True)]
    psum x1 -> x0, waiting for transfers between devices: 53.4 us -> none  [per_device(): lax.psum(grad_ada_w.astype(jnp.bfloat16), 'rows').astype(jnp.float32)]
  transfers between devices with their start and end apart: 10 -> 86, of which waited for: 10 -> 30; matrix products, arithmetic and copies ran while one was open for 4% -> 40% of each run, Pallas kernels for 0% -> 15%
where the time goes in v1:
time: 759 us; the launch traced here: 752 us
  waiting for transfers between devices  163 us (21%)
  local copies, waits for them, and re-layouts  138 us (18%)
  Pallas kernels  138 us (18%)
  other arithmetic  120 us (16%)
  matrix products  102 us (13%)
  starting transfers between devices  88.3 us (12%)
    ppermute x86, waiting for transfers between devices, swap(): return lax.ppermute(values, axis, SWAP)  163 us
    pallas_call x3, Pallas kernels, line_exchange(): pl.pallas_call(lambda *refs: line_kernel(pick, *refs), out_shape=jax.Shap...  89.3 us
    ppermute x86, starting transfers between devices, swap(): return lax.ppermute(values, axis, SWAP)  88.3 us
    unnamed x344, local copies, waits for them, and re-layouts  30.9 us
    dot_general x8, matrix products, tn(): lax.dot_general(a, b, (((0,), (0,)), ((), ())), preferred_element_type=F32)  24.7 us
    dynamic_update_slice x22, local copies, waits for them, and re-layouts, plane_gather(): out = lax.dynamic_update_index_in_dim(out, block, rank ^ k, 0)  21.2 us
    pallas_call x2, Pallas kernels, plane_exchange(): pl.pallas_call(plane_kernel, out_shape=jax.ShapeDtypeStruct((4,) + src.sh...  17.5 us
    pallas_call x1, Pallas kernels, attn_bwd(): pl.pallas_call(attn_bwd_kernel, out_shape=(jax.ShapeDtypeStruct((2, 2, BL...  16.9 us
  transfers between devices with their start and end apart: 86, of which 30 were waited for; matrix products, arithmetic and copies ran while one was open for 40% of the time, Pallas kernels for 15%

profile of v1, /device:TPU:0, one launch (start us, length us, event | category | flops | bytes accessed | tf_op | source)
XLA Modules:
  0.0 752.5 jit_solution(16545991275256801060)
XLA Ops:
  0.7 3.8 fusion.207
  7.0 4.0 collective-permute-start.36
  28.8 40.1 %mod_exchange.1 = f32[8,16,864]{2,1,0:T(8,128)} custom-call(f32[2,16,864]{2,1,0:T(8,128)} %fusion.70.refs_0_), custom_call_target="tpu_custom_call" | custom-call | tf_op jit(solution)/shard_map/mod_exchange/pallas_call | solution.py:572
  76.0 3.9 fusion.25
  86.2 9.6 %act_exchange.1 = bf16[4,2,16,1152]{3,2,1,0:T(8,128)(2,1)} custom-call(bf16[2,16,1152]{2,1,0:T(8,128)(2,1)} %pad.41.src), custom_call_target="tpu_custom_call" | custom-call | tf_op jit(solution)/shard_map/act_exchange/pallas_call | solution.py:615
  98.4 4.3 collective-permute-start.10
  157.9 4.7 add_convert_fusion.1
  164.6 5.4 add_convert_fusion
  170.0 14.0 %attn_fwd.1 = (bf16[2,2,176,288]{3,2,1,0:T(8,128)(2,1)S(1)}, bf16[2,2,176,288]{3,2,1,0:T(8,128)(2,1)S(1)}, f32[1408,128]{1,0:T(8,128)S(1)}) custom-call(s32[79]{0:T(128)S(1)} %concatenate.145.scal, bf16[2,2,176,1536]{3,2,1,0:T(8,128)(2,1)S(1)} %bitcast.450, bf16[2,2,176,1536]{3,2,1,0:T(8,128)(2,1)} %bitcast.554, bf16[512,288]{1,0:T(8,128)(2,1)S(1)} %copy-done.4), custom_call_target="tpu_custom_call" | custom-call | flops 4000000000 | bytes 6000000 | tf_op jit(solution)/shard_map/attn_fwd/pallas_call | solution.py:484
  185.2 13.6 %collective-permute-done.15 = bf16[2,2,176,288]{3,2,1,0:T(8,128)(2,1)S(1)} collective-permute-done((bf16[2,2,176,288]{3,2,1,0:T(8,128)(2,1)S(1)}, bf16[2,2,176,288]{3,2,1,0:T(8,128)(2,1)S(1)}, u32[]{:S(2)}, u32[]{:S(2)}) %collective-permute-start.15) | collective-permute-done | bytes 405536 | tf_op jit(solution)/shard_map/ppermute | solution.py:631
  213.2 5.0 collective-permute-done.22
  242.0 9.8 %collective-permute-done.31 = bf16[2,176,1152]{2,1,0:T(8,128)(2,1)} collective-permute-done((bf16[2,176,1152]{2,1,0:T(8,128)(2,1)}, bf16[2,176,1152]{2,1,0:T(8,128)(2,1)}, u32[]{:S(2)}, u32[]{:S(2)}) %collective-permute-start.31) | collective-permute-done | bytes 811040 | tf_op jit(solution)/shard_map/ppermute | solution.py:631
  268.2 6.4 fusion.24
  276.8 6.6 fusion.23
  283.4 4.6 convolution_convert_fusion.6
  288.2 3.8 convolution_convert_fusion.7
  296.1 16.9 %collective-permute-done.34 = bf16[2,176,1152]{2,1,0:T(8,128)(2,1)S(1)} collective-permute-done((bf16[2,176,1152]{2,1,0:T(8,128)(2,1)S(1)}, bf16[2,176,1152]{2,1,0:T(8,128)(2,1)S(1)}, u32[]{:S(2)}, u32[]{:S(2)}) %collective-permute-start.34) | collective-permute-done | bytes 811040 | tf_op jit(solution)/shard_map/ppermute | solution.py:631
  321.2 4.0 convolution_multiply_fusion.1
  328.5 3.9 convolution_convert_fusion.5
  333.7 3.6 collective-permute-done.39
  344.4 4.0 convolution_multiply_fusion
  351.4 3.9 convolution_convert_fusion.4
  367.8 9.7 %collective-permute-done.68 = bf16[2,144,1152]{2,1,0:T(8,128)(2,1)S(1)} collective-permute-done((bf16[2,144,1152]{2,1,0:T(8,128)(2,1)S(1)}, bf16[2,144,1152]{2,1,0:T(8,128)(2,1)S(1)}, u32[]{:S(2)}, u32[]{:S(2)}) %collective-permute-start.68) | collective-permute-done | bytes 663584 | tf_op jit(solution)/shard_map/ppermute | solution.py:631
  380.0 10.8 %collective-permute-done.77 = bf16[2,72,2304]{2,1,0:T(8,128)(2,1)S(1)} collective-permute-done((bf16[2,72,2304]{2,1,0:T(8,128)(2,1)S(1)}, bf16[2,72,2304]{2,1,0:T(8,128)(2,1)S(1)}, u32[]{:S(2)}, u32[]{:S(2)}) %collective-permute-start.77) | collective-permute-done | bytes 663584 | tf_op jit(solution)/shard_map/ppermute | solution.py:631
  391.9 3.4 collective-permute-done.79
  398.7 3.8 collective-permute-done.69
  411.9 14.7 %collective-permute-done.72 = bf16[288,576]{1,0:T(8,128)(2,1)} collective-permute-done((bf16[288,576]{1,0:T(8,128)(2,1)}, bf16[288,576]{1,0:T(8,128)(2,1)}, u32[]{:S(2)}, u32[]{:S(2)}) %collective-permute-start.72) | collective-permute-done | bytes 331808 | tf_op jit(solution)/shard_map/ppermute | solution.py:631
  430.7 4.3 collective-permute-done.81
  439.8 4.6 fusion.186
  447.0 4.3 fusion.184
  454.1 4.8 multiply_reduce_fusion.1
  497.0 5.7 collective-permute-done.44.g1
  502.7 16.9 %attn_bwd.1 = (bf16[2,2,176,1536]{3,2,1,0:T(8,128)(2,1)S(1)}, bf16[2,2,176,1536]{3,2,1,0:T(8,128)(2,1)}) custom-call(s32[79]{0:T(128)S(1)} %concatenate.145.scal, bf16[2,2,176,1536]{3,2,1,0:T(8,128)(2,1)} %bitcast.451, bf16[2,2,176,1536]{3,2,1,0:T(8,128)(2,1)} %bitcast.555, bf16[2,2,176,288]{3,2,1,0:T(8,128)(2,1)S(1)} %bitcast.449, ...), custom_call_target="tpu_custom_call" | custom-call | flops 12000000000 | bytes 12000000 | tf_op jit(solution)/shard_map/attn_bwd/pallas_call | solution.py:507
  521.9 4.1 convolution_bitcast_fusion
  527.2 4.6 fusion.1
  562.0 11.4 %collective-permute-done.59 = bf16[2,18,2304]{2,1,0:T(8,128)(2,1)S(1)} collective-permute-done((bf16[2,18,2304]{2,1,0:T(8,128)(2,1)S(1)}, bf16[2,18,2304]{2,1,0:T(8,128)(2,1)S(1)}, u32[]{:S(2)}, u32[]{:S(2)}) %collective-permute-start.59) | collective-permute-done | bytes 165920 | tf_op jit(solution)/shard_map/ppermute | solution.py:631
  583.8 7.2 collective-permute-done.51
  593.4 3.8 collective-permute-done.65
  600.1 4.2 collective-permute-done.52
  608.3 10.3 %collective-permute-done.53 = bf16[288,432]{1,0:T(8,128)(2,1)} collective-permute-done((bf16[288,432]{1,0:T(8,128)(2,1)}, bf16[288,432]{1,0:T(8,128)(2,1)}, u32[]{:S(2)}, u32[]{:S(2)}) %collective-permute-start.53) | collective-permute-done | bytes 248864 | tf_op jit(solution)/shard_map/ppermute | solution.py:631
  624.5 3.9 collective-permute-done.55
  639.7 3.9 collective-permute-done.47
  643.7 3.6 multiply_reduce_fusion.7
  647.3 3.8 fusion.54
  662.5 13.7 %dmod_exchange.1 = f32[8,16,864]{2,1,0:T(8,128)} custom-call(f32[8,16,864]{2,1,0:T(8,128)} %fusion.114.refs_0_), custom_call_target="tpu_custom_call" | custom-call | tf_op jit(solution)/shard_map/dmod_exchange/pallas_call | solution.py:572
  679.0 7.9 %small_exchange.1 = bf16[4,2,16,864]{3,2,1,0:T(8,128)(2,1)} custom-call(bf16[2,16,864]{2,1,0:T(8,128)(2,1)} %copy-done.103), custom_call_target="tpu_custom_call" | custom-call | tf_op jit(solution)/shard_map/small_exchange/pallas_call | solution.py:615
  700.2 3.9 fusion.44
  706.1 35.5 %cond_exchange.1 = bf16[8,2,16,1152]{3,2,1,0:T(8,128)(2,1)} custom-call(bf16[2,16,1152]{2,1,0:T(8,128)(2,1)} %pad.48.refs_0_), custom_call_target="tpu_custom_call" | custom-call | tf_op jit(solution)/shard_map/cond_exchange/pallas_call | solution.py:572
  (807 shorter events, 368.1 us)
Async XLA Ops:
  7.0 286.3 %collective-permute-start.36 = (bf16[176,1152]{1,0:T(8,128)(2,1)}, bf16[176,1152]{1,0:T(8,128)(2,1)}, u32[]{:S(2)}, u32[]{:S(2)}) collective-permute-start(bf16[176,1152]{1,0:T(8,128)(2,1)} %select_bitcast_fusion), channel_id=1, source_target_pairs={{0,4},{4,0},{1,5},{5,1},{2,6},{6,2},{3,7},{7,3},{8,12},{12,8},{9,1... | collective-permute-start | bytes 1216520 | tf_op jit(solution)/shard_map/ppermute | solution.py:631
  11.7 93.6 %collective-permute-start.7 = (bf16[864]{0:T(1024)(128)(2,1)}, bf16[864]{0:T(1024)(128)(2,1)}, u32[]{:S(2)}, u32[]{:S(2)}) collective-permute-start(bf16[864]{0:T(1024)(128)(2,1)} %pad_maximum_fusion.31), channel_id=1, source_target_pairs={{0,4},{4,0},{1,5},{5,1},{2,6},{6,2},{3,7},{7,3},{8,12},{12,8},{9,1... | collective-permute-start | bytes 5192 | tf_op jit(solution)/shard_map/ppermute | solution.py:631
  14.6 110.7 %collective-permute-start = (bf16[176,1152]{1,0:T(8,128)(2,1)}, bf16[176,1152]{1,0:T(8,128)(2,1)}, u32[]{:S(2)}, u32[]{:S(2)}) collective-permute-start(bf16[176,1152]{1,0:T(8,128)(2,1)} %select_bitcast_fusion.1), channel_id=1, source_target_pairs={{0,4},{4,0},{1,5},{5,1},{2,6},{6,2},{3,7},{7,3},{8,12},{12,8},{9,1... | collective-permute-start | bytes 1216520 | tf_op jit(solution)/shard_map/ppermute | solution.py:631
  19.4 100.3 %collective-permute-start.2 = (bf16[288,432]{0,1:T(8,128)(2,1)}, bf16[288,432]{0,1:T(8,128)(2,1)}, u32[]{:S(2)}, u32[]{:S(2)}) collective-permute-start(bf16[288,432]{0,1:T(8,128)(2,1)} %constant_dynamic-slice_fusion.13), channel_id=1, source_target_pairs={{0,4},{4,0},{1,5},{5,1},{2,6},{6,2},{3,7},{7,3},{8,12},{12,8},{9,1... | collective-permute-start | bytes 746504 | tf_op jit(solution)/shard_map/ppermute | solution.py:631
  20.0 78.4 %collective-permute-start.18 = (f32[176,1]{0,1:T(1,128)}, f32[176,1]{0,1:T(1,128)}, u32[]{:S(2)}, u32[]{:S(2)}) collective-permute-start(f32[176,1]{0,1:T(1,128)} %fusion.163), channel_id=1, source_target_pairs={{0,4},{4,0},{1,5},{5,1},{2,6},{6,2},{3,7},{7,3},{8,12},{12,8},{9,1... | collective-permute-start | bytes 2120 | tf_op jit(solution)/shard_map/ppermute | solution.py:631
  130.1 22.3 %collective-permute-start.1 = (bf16[2,176,1152]{2,1,0:T(8,128)(2,1)}, bf16[2,176,1152]{2,1,0:T(8,128)(2,1)}, u32[]{:S(2)}, u32[]{:S(2)}) collective-permute-start(bf16[2,176,1152]{2,1,0:T(8,128)(2,1)} %fusion.51), channel_id=1, source_target_pairs={{0,1},{1,0},{2,3},{3,2},{4,5},{5,4},{6,7},{7,6},{8,9},{9,8},{10,11... | collective-permute-start | bytes 2433032 | tf_op jit(solution)/shard_map/ppermute | solution.py:631
  130.1 26.0 %collective-permute-start.8 = (bf16[2,176,1152]{2,1,0:T(8,128)(2,1)}, bf16[2,176,1152]{2,1,0:T(8,128)(2,1)}, u32[]{:S(2)}, u32[]{:S(2)}) collective-permute-start(bf16[2,176,1152]{2,1,0:T(8,128)(2,1)} %fusion.51), channel_id=1, source_target_pairs={{0,2},{2,0},{1,3},{3,1},{4,6},{6,4},{5,7},{7,5},{8,10},{10,8},{9,1... | collective-permute-start | bytes 2433032 | tf_op jit(solution)/shard_map/ppermute | solution.py:631
  142.9 59.0 %collective-permute-start.20 = (bf16[288,576]{0,1:T(8,128)(2,1)}, bf16[288,576]{0,1:T(8,128)(2,1)}, u32[]{:S(2)}, u32[]{:S(2)}) collective-permute-start(bf16[288,576]{0,1:T(8,128)(2,1)} %constant_dynamic-slice_fusion.11), channel_id=1, source_target_pairs={{0,4},{4,0},{1,5},{5,1},{2,6},{6,2},{3,7},{7,3},{8,12},{12,8},{9,1... | collective-permute-start | bytes 995336 | tf_op jit(solution)/shard_map/ppermute | solution.py:631
  144.9 61.3 %collective-permute-start.25 = (bf16[144,1152]{1,0:T(8,128)(2,1)}, bf16[144,1152]{1,0:T(8,128)(2,1)}, u32[]{:S(2)}, u32[]{:S(2)}) collective-permute-start(bf16[144,1152]{1,0:T(8,128)(2,1)} %constant_dynamic-slice_fusion.8), channel_id=1, source_target_pairs={{0,4},{4,0},{1,5},{5,1},{2,6},{6,2},{3,7},{7,3},{8,12},{12,8},{9,1... | collective-permute-start | bytes 995336 | tf_op jit(solution)/shard_map/ppermute | solution.py:631
  152.4 32.7 %collective-permute-start.16 = (bf16[288,1152]{1,0:T(8,128)(2,1)S(1)}, bf16[288,1152]{1,0:T(8,128)(2,1)S(1)}, u32[]{:S(2)}, u32[]{:S(2)}) collective-permute-start(bf16[288,1152]{1,0:T(8,128)(2,1)S(1)} %copy-done.79), channel_id=1, source_target_pairs={{0,2},{2,0},{1,3},{3,1},{4,6},{6,4},{5,7},{7,5},{8,10},{10,8},{9,1... | collective-permute-start | bytes 1990664 | tf_op jit(solution)/shard_map/ppermute | solution.py:631
  184.0 14.8 %collective-permute-start.15 = (bf16[2,2,176,288]{3,2,1,0:T(8,128)(2,1)S(1)}, bf16[2,2,176,288]{3,2,1,0:T(8,128)(2,1)S(1)}, u32[]{:S(2)}, u32[]{:S(2)}) collective-permute-start(bf16[2,2,176,288]{3,2,1,0:T(8,128)(2,1)S(1)} %get-tuple-element.20), channel_id=1, source_target_pairs={{0,2},{2,0},{1,3},{3,1},{4,6},{6,4},{5,7},{7,5},{8,10},{10,8},{9,1... | collective-permute-start | bytes 1216520 | tf_op jit(solution)/shard_map/ppermute | solution.py:631
  201.1 21.1 %collective-permute-start.17 = (bf16[2,176,1152]{2,1,0:T(8,128)(2,1)}, bf16[2,176,1152]{2,1,0:T(8,128)(2,1)}, u32[]{:S(2)}, u32[]{:S(2)}) collective-permute-start(bf16[2,176,1152]{2,1,0:T(8,128)(2,1)} %bitcast.42), channel_id=1, source_target_pairs={{0,1},{1,0},{2,3},{3,2},{4,5},{5,4},{6,7},{7,6},{8,9},{9,8},{10,11... | collective-permute-start | bytes 2433032 | tf_op jit(solution)/shard_map/ppermute | solution.py:631
  203.9 16.0 %collective-permute-start.21 = (bf16[288,576]{0,1:T(8,128)(2,1)}, bf16[288,576]{0,1:T(8,128)(2,1)S(1)}, u32[]{:S(2)}, u32[]{:S(2)}) collective-permute-start(bf16[288,576]{0,1:T(8,128)(2,1)} %collective-permute-done.20), channel_id=1, source_target_pairs={{0,8},{8,0},{1,9},{9,1},{2,10},{10,2},{3,11},{11,3},{4,12},{12,4},... | collective-permute-start | bytes 995336 | tf_op jit(solution)/shard_map/ppermute | solution.py:631
  206.1 26.5 %collective-permute-start.26 = (bf16[144,1152]{1,0:T(8,128)(2,1)}, bf16[144,1152]{1,0:T(8,128)(2,1)}, u32[]{:S(2)}, u32[]{:S(2)}) collective-permute-start(bf16[144,1152]{1,0:T(8,128)(2,1)} %collective-permute-done.25), channel_id=1, source_target_pairs={{0,8},{8,0},{1,9},{9,1},{2,10},{10,2},{3,11},{11,3},{4,12},{12,4},... | collective-permute-start | bytes 995336 | tf_op jit(solution)/shard_map/ppermute | solution.py:631
  218.2 16.4 %collective-permute-start.27 = (bf16[144,1152]{1,0:T(8,128)(2,1)}, bf16[144,1152]{1,0:T(8,128)(2,1)}, u32[]{:S(2)}, u32[]{:S(2)}) collective-permute-start(bf16[144,1152]{1,0:T(8,128)(2,1)} %collective-permute-done.25), channel_id=1, source_target_pairs={{0,16},{16,0},{1,17},{17,1},{2,18},{18,2},{3,19},{19,3},{4,20},{20... | collective-permute-start | bytes 995336 | tf_op jit(solution)/shard_map/ppermute | solution.py:631
  219.9 36.9 %collective-permute-start.24 = (bf16[144,576]{0,1:T(8,128)(2,1)}, bf16[144,576]{0,1:T(8,128)(2,1)}, u32[]{:S(2)}, u32[]{:S(2)}) collective-permute-start(bf16[144,576]{0,1:T(8,128)(2,1)} %slice.637), channel_id=1, source_target_pairs={{0,8},{8,0},{1,9},{9,1},{2,10},{10,2},{3,11},{11,3},{4,12},{12,4},... | collective-permute-start | bytes 497672 | tf_op jit(solution)/shard_map/ppermute | solution.py:631
  222.3 35.6 %collective-permute-start.23 = (bf16[144,576]{0,1:T(8,128)(2,1)}, bf16[144,576]{0,1:T(8,128)(2,1)}, u32[]{:S(2)}, u32[]{:S(2)}) collective-permute-start(bf16[144,576]{0,1:T(8,128)(2,1)} %slice.636), channel_id=1, source_target_pairs={{0,16},{16,0},{1,17},{17,1},{2,18},{18,2},{3,19},{19,3},{4,20},{20... | collective-permute-start | bytes 497672 | tf_op jit(solution)/shard_map/ppermute | solution.py:631
  232.6 19.2 %collective-permute-start.31 = (bf16[2,176,1152]{2,1,0:T(8,128)(2,1)}, bf16[2,176,1152]{2,1,0:T(8,128)(2,1)}, u32[]{:S(2)}, u32[]{:S(2)}) collective-permute-start(bf16[2,176,1152]{2,1,0:T(8,128)(2,1)} %get-tuple-element.90), channel_id=1, source_target_pairs={{0,2},{2,0},{1,3},{3,1},{4,6},{6,4},{5,7},{7,5},{8,10},{10,8},{9,1... | collective-permute-start | bytes 2433032 | tf_op jit(solution)/shard_map/ppermute | solution.py:631
  234.6 31.7 %collective-permute-start.19 = (bf16[2,176,1152]{2,1,0:T(8,128)(2,1)}, bf16[2,176,1152]{2,1,0:T(8,128)(2,1)}, u32[]{:S(2)}, u32[]{:S(2)}) collective-permute-start(bf16[2,176,1152]{2,1,0:T(8,128)(2,1)} %get-tuple-element.90), channel_id=1, source_target_pairs={{0,1},{1,0},{2,3},{3,2},{4,5},{5,4},{6,7},{7,6},{8,9},{9,8},{10,11... | collective-permute-start | bytes 2433032 | tf_op jit(solution)/shard_map/ppermute | solution.py:631
  251.8 22.8 %collective-permute-start.32 = (bf16[2,176,1152]{2,1,0:T(8,128)(2,1)}, bf16[2,176,1152]{2,1,0:T(8,128)(2,1)}, u32[]{:S(2)}, u32[]{:S(2)}) collective-permute-start(bf16[2,176,1152]{2,1,0:T(8,128)(2,1)} %collective-permute-done.31), channel_id=1, source_target_pairs={{0,1},{1,0},{2,3},{3,2},{4,5},{5,4},{6,7},{7,6},{8,9},{9,8},{10,11... | collective-permute-start | bytes 2433032 | tf_op jit(solution)/shard_map/ppermute | solution.py:631
  292.9 20.1 %collective-permute-start.34 = (bf16[2,176,1152]{2,1,0:T(8,128)(2,1)S(1)}, bf16[2,176,1152]{2,1,0:T(8,128)(2,1)S(1)}, u32[]{:S(2)}, u32[]{:S(2)}) collective-permute-start(bf16[2,176,1152]{2,1,0:T(8,128)(2,1)S(1)} %fusion.67), channel_id=1, source_target_pairs={{0,2},{2,0},{1,3},{3,1},{4,6},{6,4},{5,7},{7,5},{8,10},{10,8},{9,1... | collective-permute-start | bytes 2433032 | tf_op jit(solution)/shard_map/ppermute | solution.py:631
  318.1 19.2 %collective-permute-start.39 = (bf16[2,176,1152]{2,1,0:T(8,128)(2,1)S(1)}, bf16[2,176,1152]{2,1,0:T(8,128)(2,1)S(1)}, u32[]{:S(2)}, u32[]{:S(2)}) collective-permute-start(bf16[2,176,1152]{2,1,0:T(8,128)(2,1)S(1)} %multiply_convert_fusion.1), channel_id=1, source_target_pairs={{0,2},{2,0},{1,3},{3,1},{4,6},{6,4},{5,7},{7,5},{8,10},{10,8},{9,1... | collective-permute-start | bytes 2433032 | tf_op jit(solution)/shard_map/ppermute | solution.py:631
  339.9 98.3 %collective-permute-start.38 = (bf16[2,176,1152]{2,1,0:T(8,128)(2,1)}, bf16[2,176,1152]{2,1,0:T(8,128)(2,1)}, u32[]{:S(2)}, u32[]{:S(2)}) collective-permute-start(bf16[2,176,1152]{2,1,0:T(8,128)(2,1)} %bitcast.102), channel_id=1, source_target_pairs={{0,1},{1,0},{2,3},{3,2},{4,5},{5,4},{6,7},{7,6},{8,9},{9,8},{10,11... | collective-permute-start | bytes 2433032 | tf_op jit(solution)/shard_map/ppermute | solution.py:631
  355.5 41.1 %collective-permute-start.41 = (bf16[2,176,1152]{2,1,0:T(8,128)(2,1)S(1)}, bf16[2,176,1152]{2,1,0:T(8,128)(2,1)S(1)}, u32[]{:S(2)}, u32[]{:S(2)}) collective-permute-start(bf16[2,176,1152]{2,1,0:T(8,128)(2,1)S(1)} %bitcast.534), channel_id=1, source_target_pairs={{0,1},{1,0},{2,3},{3,2},{4,5},{5,4},{6,7},{7,6},{8,9},{9,8},{10,11... | collective-permute-start | bytes 2433032 | tf_op jit(solution)/shard_map/ppermute | solution.py:631
  359.7 17.8 %collective-permute-start.68 = (bf16[2,144,1152]{2,1,0:T(8,128)(2,1)S(1)}, bf16[2,144,1152]{2,1,0:T(8,128)(2,1)S(1)}, u32[]{:S(2)}, u32[]{:S(2)}) collective-permute-start(bf16[2,144,1152]{2,1,0:T(8,128)(2,1)S(1)} %pad_maximum_fusion.18), channel_id=1, source_target_pairs={{0,8},{8,0},{1,9},{9,1},{2,10},{10,2},{3,11},{11,3},{4,12},{12,4},... | collective-permute-start | bytes 1990664 | tf_op jit(solution)/shard_map/ppermute | solution.py:631
  360.8 17.9 %collective-permute-start.70 = (bf16[2,144,1152]{2,1,0:T(8,128)(2,1)S(1)}, bf16[2,144,1152]{2,1,0:T(8,128)(2,1)S(1)}, u32[]{:S(2)}, u32[]{:S(2)}) collective-permute-start(bf16[2,144,1152]{2,1,0:T(8,128)(2,1)S(1)} %pad_maximum_fusion.19), channel_id=1, source_target_pairs={{0,16},{16,0},{1,17},{17,1},{2,18},{18,2},{3,19},{19,3},{4,20},{20... | collective-permute-start | bytes 1990664 | tf_op jit(solution)/shard_map/ppermute | solution.py:631
  366.6 24.2 %collective-permute-start.77 = (bf16[2,72,2304]{2,1,0:T(8,128)(2,1)S(1)}, bf16[2,72,2304]{2,1,0:T(8,128)(2,1)S(1)}, u32[]{:S(2)}, u32[]{:S(2)}) collective-permute-start(bf16[2,72,2304]{2,1,0:T(8,128)(2,1)S(1)} %pad_maximum_fusion.20), channel_id=1, source_target_pairs={{0,8},{8,0},{1,9},{9,1},{2,10},{10,2},{3,11},{11,3},{4,12},{12,4},... | collective-permute-start | bytes 1990664 | tf_op jit(solution)/shard_map/ppermute | solution.py:631
  377.5 17.8 %collective-permute-start.79 = (bf16[2,72,2304]{2,1,0:T(8,128)(2,1)S(1)}, bf16[2,72,2304]{2,1,0:T(8,128)(2,1)S(1)}, u32[]{:S(2)}, u32[]{:S(2)}) collective-permute-start(bf16[2,72,2304]{2,1,0:T(8,128)(2,1)S(1)} %pad_maximum_fusion.21), channel_id=1, source_target_pairs={{0,16},{16,0},{1,17},{17,1},{2,18},{18,2},{3,19},{19,3},{4,20},{20... | collective-permute-start | bytes 1990664 | tf_op jit(solution)/shard_map/ppermute | solution.py:631
  378.9 23.5 %collective-permute-start.69 = (bf16[144,1152]{1,0:T(8,128)(2,1)S(1)}, bf16[144,1152]{1,0:T(8,128)(2,1)S(1)}, u32[]{:S(2)}, u32[]{:S(2)}) collective-permute-start(bf16[144,1152]{1,0:T(8,128)(2,1)S(1)} %get-tuple-element.106), channel_id=1, source_target_pairs={{0,16},{16,0},{1,17},{17,1},{2,18},{18,2},{3,19},{19,3},{4,20},{20... | collective-permute-start | bytes 995336 | tf_op jit(solution)/shard_map/ppermute | solution.py:631
  402.5 36.7 %collective-permute-start.42 = (bf16[2,176,1152]{2,1,0:T(8,128)(2,1)}, bf16[2,176,1152]{2,1,0:T(8,128)(2,1)}, u32[]{:S(2)}, u32[]{:S(2)}) collective-permute-start(bf16[2,176,1152]{2,1,0:T(8,128)(2,1)} %fusion.65), channel_id=1, source_target_pairs={{0,2},{2,0},{1,3},{3,1},{4,6},{6,4},{5,7},{7,5},{8,10},{10,8},{9,1... | collective-permute-start | bytes 2433032 | tf_op jit(solution)/shard_map/ppermute | solution.py:631
  404.1 22.4 %collective-permute-start.72 = (bf16[288,576]{1,0:T(8,128)(2,1)}, bf16[288,576]{1,0:T(8,128)(2,1)}, u32[]{:S(2)}, u32[]{:S(2)}) collective-permute-start(bf16[288,576]{1,0:T(8,128)(2,1)} %fusion.78), channel_id=1, source_target_pairs={{0,4},{4,0},{1,5},{5,1},{2,6},{6,2},{3,7},{7,3},{8,12},{12,8},{9,1... | collective-permute-start | bytes 995336 | tf_op jit(solution)/shard_map/ppermute | solution.py:631
  408.6 26.4 %collective-permute-start.81 = (bf16[144,1152]{1,0:T(8,128)(2,1)}, bf16[144,1152]{1,0:T(8,128)(2,1)}, u32[]{:S(2)}, u32[]{:S(2)}) collective-permute-start(bf16[144,1152]{1,0:T(8,128)(2,1)} %fusion.86), channel_id=1, source_target_pairs={{0,4},{4,0},{1,5},{5,1},{2,6},{6,2},{3,7},{7,3},{8,12},{12,8},{9,1... | collective-permute-start | bytes 995336 | tf_op jit(solution)/shard_map/ppermute | solution.py:631
  428.7 32.3 %collective-permute-start.73 = (bf16[288,576]{1,0:T(8,128)(2,1)}, bf16[288,576]{1,0:T(8,128)(2,1)}, u32[]{:S(2)}, u32[]{:S(2)}) collective-permute-start(bf16[288,576]{1,0:T(8,128)(2,1)} %get-tuple-element.70), channel_id=1, source_target_pairs={{0,8},{8,0},{1,9},{9,1},{2,10},{10,2},{3,11},{11,3},{4,12},{12,4},... | collective-permute-start | bytes 995336 | tf_op jit(solution)/shard_map/ppermute | solution.py:631
  429.6 29.2 %collective-permute-start.74 = (bf16[288,576]{1,0:T(8,128)(2,1)}, bf16[288,576]{1,0:T(8,128)(2,1)}, u32[]{:S(2)}, u32[]{:S(2)}) collective-permute-start(bf16[288,576]{1,0:T(8,128)(2,1)} %get-tuple-element.70), channel_id=1, source_target_pairs={{0,16},{16,0},{1,17},{17,1},{2,18},{18,2},{3,19},{19,3},{4,20},{20... | collective-permute-start | bytes 995336 | tf_op jit(solution)/shard_map/ppermute | solution.py:631
  437.2 27.7 %collective-permute-start.82 = (bf16[144,1152]{1,0:T(8,128)(2,1)}, bf16[144,1152]{1,0:T(8,128)(2,1)}, u32[]{:S(2)}, u32[]{:S(2)}) collective-permute-start(bf16[144,1152]{1,0:T(8,128)(2,1)} %get-tuple-element.68), channel_id=1, source_target_pairs={{0,8},{8,0},{1,9},{9,1},{2,10},{10,2},{3,11},{11,3},{4,12},{12,4},... | collective-permute-start | bytes 995336 | tf_op jit(solution)/shard_map/ppermute | solution.py:631
  438.1 24.8 %collective-permute-start.83 = (bf16[144,1152]{1,0:T(8,128)(2,1)}, bf16[144,1152]{1,0:T(8,128)(2,1)}, u32[]{:S(2)}, u32[]{:S(2)}) collective-permute-start(bf16[144,1152]{1,0:T(8,128)(2,1)} %get-tuple-element.68), channel_id=1, source_target_pairs={{0,16},{16,0},{1,17},{17,1},{2,18},{18,2},{3,19},{19,3},{4,20},{20... | collective-permute-start | bytes 995336 | tf_op jit(solution)/shard_map/ppermute | solution.py:631
  451.3 31.4 %collective-permute-start.43 = (bf16[2,176,1152]{2,1,0:T(8,128)(2,1)}, bf16[2,176,1152]{2,1,0:T(8,128)(2,1)}, u32[]{:S(2)}, u32[]{:S(2)}) collective-permute-start(bf16[2,176,1152]{2,1,0:T(8,128)(2,1)} %get-tuple-element.97), channel_id=1, source_target_pairs={{0,1},{1,0},{2,3},{3,2},{4,5},{5,4},{6,7},{7,6},{8,9},{9,8},{10,11... | collective-permute-start | bytes 2433032 | tf_op jit(solution)/shard_map/ppermute | solution.py:631
  463.9 14.1 %collective-permute-start.85 = (bf16[72,1152]{1,0:T(8,128)(2,1)S(1)}, bf16[72,1152]{1,0:T(8,128)(2,1)}, u32[]{:S(2)}, u32[]{:S(2)}) collective-permute-start(bf16[72,1152]{1,0:T(8,128)(2,1)S(1)} %slice.719), channel_id=1, source_target_pairs={{0,8},{8,0},{1,9},{9,1},{2,10},{10,2},{3,11},{11,3},{4,12},{12,4},... | collective-permute-start | bytes 497672 | tf_op jit(solution)/shard_map/ppermute | solution.py:631
  487.3 15.4 %collective-permute-start.44 = (bf16[2,2,176,288]{3,2,1,0:T(8,128)(2,1)}, bf16[2,2,176,288]{3,2,1,0:T(8,128)(2,1)S(1)}, u32[]{:S(2)}, u32[]{:S(2)}) collective-permute-start(bf16[2,2,176,288]{3,2,1,0:T(8,128)(2,1)} %bitcast.114), channel_id=1, source_target_pairs={{0,2},{2,0},{1,3},{3,1},{4,6},{6,4},{5,7},{7,5},{8,10},{10,8},{9,1... | collective-permute-start | bytes 1216520 | tf_op jit(solution)/shard_map/ppermute | solution.py:631
  494.9 62.4 %collective-permute-start.58 = (bf16[288,1152]{1,0:T(8,128)(2,1)}, bf16[288,1152]{1,0:T(8,128)(2,1)}, u32[]{:S(2)}, u32[]{:S(2)}) collective-permute-start(bf16[288,1152]{1,0:T(8,128)(2,1)} %fusion.29), channel_id=1, source_target_pairs={{0,2},{2,0},{1,3},{3,1},{4,6},{6,4},{5,7},{7,5},{8,10},{10,8},{9,1... | collective-permute-start | bytes 1990664 | tf_op jit(solution)/shard_map/ppermute | solution.py:631
  540.2 82.1 %collective-permute-start.46 = (bf16[2,176,1152]{2,1,0:T(8,128)(2,1)}, bf16[2,176,1152]{2,1,0:T(8,128)(2,1)}, u32[]{:S(2)}, u32[]{:S(2)}) collective-permute-start(bf16[2,176,1152]{2,1,0:T(8,128)(2,1)} %bitcast.120), channel_id=1, source_target_pairs={{0,1},{1,0},{2,3},{3,2},{4,5},{5,4},{6,7},{7,6},{8,9},{9,8},{10,11... | collective-permute-start | bytes 2433032 | tf_op jit(solution)/shard_map/ppermute | solution.py:631
  544.5 95.2 %collective-permute-start.45 = (bf16[2,176,1152]{2,1,0:T(8,128)(2,1)}, bf16[2,176,1152]{2,1,0:T(8,128)(2,1)}, u32[]{:S(2)}, u32[]{:S(2)}) collective-permute-start(bf16[2,176,1152]{2,1,0:T(8,128)(2,1)} %bitcast.117), channel_id=1, source_target_pairs={{0,1},{1,0},{2,3},{3,2},{4,5},{5,4},{6,7},{7,6},{8,9},{9,8},{10,11... | collective-permute-start | bytes 2433032 | tf_op jit(solution)/shard_map/ppermute | solution.py:631
  553.8 22.4 %collective-permute-start.49 = (bf16[2,144,864]{2,1,0:T(8,128)(2,1)}, bf16[2,144,864]{2,1,0:T(8,128)(2,1)}, u32[]{:S(2)}, u32[]{:S(2)}) collective-permute-start(bf16[2,144,864]{2,1,0:T(8,128)(2,1)} %pad_maximum_fusion.23), channel_id=1, source_target_pairs={{0,8},{8,0},{1,9},{9,1},{2,10},{10,2},{3,11},{11,3},{4,12},{12,4},... | collective-permute-start | bytes 1493000 | tf_op jit(solution)/shard_map/ppermute | solution.py:631
  576.2 14.8 %collective-permute-start.51 = (bf16[2,144,864]{2,1,0:T(8,128)(2,1)S(1)}, bf16[2,144,864]{2,1,0:T(8,128)(2,1)S(1)}, u32[]{:S(2)}, u32[]{:S(2)}) collective-permute-start(bf16[2,144,864]{2,1,0:T(8,128)(2,1)S(1)} %pad_maximum_fusion.24), channel_id=1, source_target_pairs={{0,16},{16,0},{1,17},{17,1},{2,18},{18,2},{3,19},{19,3},{4,20},{20... | collective-permute-start | bytes 1493000 | tf_op jit(solution)/shard_map/ppermute | solution.py:631
  582.5 16.9 %collective-permute-start.50 = (bf16[144,864]{1,0:T(8,128)(2,1)S(1)}, bf16[144,864]{1,0:T(8,128)(2,1)S(1)}, u32[]{:S(2)}, u32[]{:S(2)}) collective-permute-start(bf16[144,864]{1,0:T(8,128)(2,1)S(1)} %fusion.125), channel_id=1, source_target_pairs={{0,16},{16,0},{1,17},{17,1},{2,18},{18,2},{3,19},{19,3},{4,20},{20... | collective-permute-start | bytes 746504 | tf_op jit(solution)/shard_map/ppermute | solution.py:631
  624.5 19.0 %collective-permute-start.47 = (bf16[2,176,1152]{2,1,0:T(8,128)(2,1)}, bf16[2,176,1152]{2,1,0:T(8,128)(2,1)}, u32[]{:S(2)}, u32[]{:S(2)}) collective-permute-start(bf16[2,176,1152]{2,1,0:T(8,128)(2,1)} %fusion.63), channel_id=1, source_target_pairs={{0,2},{2,0},{1,3},{3,1},{4,6},{6,4},{5,7},{7,5},{8,10},{10,8},{9,1... | collective-permute-start | bytes 2433032 | tf_op jit(solution)/shard_map/ppermute | solution.py:631
  693.4 53.1 %collective-permute-start.35 = (bf16[176,1152]{1,0:T(8,128)(2,1)}, bf16[176,1152]{1,0:T(8,128)(2,1)}, u32[]{:S(2)}, u32[]{:S(2)}) collective-permute-start(bf16[176,1152]{1,0:T(8,128)(2,1)} %bitcast.83), channel_id=1, source_target_pairs={{0,4},{4,0},{1,5},{5,1},{2,6},{6,2},{3,7},{7,3},{8,12},{12,8},{9,1... | collective-permute-start | bytes 1216520 | tf_op jit(solution)/shard_map/ppermute | solution.py:631
  705.4 44.6 %collective-permute-start.48 = (bf16[176,1152]{1,0:T(8,128)(2,1)S(1)}, bf16[176,1152]{1,0:T(8,128)(2,1)S(1)}, u32[]{:S(2)}, u32[]{:S(2)}) collective-permute-start(bf16[176,1152]{1,0:T(8,128)(2,1)S(1)} %bitcast.544), channel_id=1, source_target_pairs={{0,4},{4,0},{1,5},{5,1},{2,6},{6,2},{3,7},{7,3},{8,12},{12,8},{9,1... | collective-permute-start | bytes 1216520 | tf_op jit(solution)/shard_map/ppermute | solution.py:631
  (203 other events, 3149.4 us)

commit v2 on v1

--- a/solution.py
+++ b/solution.py
@@ -339,55 +339,14 @@
 HALF = SEQ // 2
 
 
-def block_place(scal, dq, dc, slot):
-    q = lax.rem(scal[0] + dq, 2)
-    c = lax.rem(scal[1] + dc, 2)
-    return pl.multiple_of(slot * HALF + q * (2 * BLK) + c * BLK, 16)
-
-
-def load_blocks(scal, refs, buf, sem):
-    copies = []
-    for dq in range(2):
-        for dc in range(2):
-            for slot in range(2):
-                copies.append(
-                    pltpu.make_async_copy(
-                        refs[dq].at[dc, slot],
-                        buf.at[pl.ds(block_place(scal, dq, dc, slot), BLK)],
-                        sem.at[dq * 4 + dc * 2 + slot],
-                    )
-                )
-    for copy in copies:
-        copy.start()
-    return copies
-
-
-def store_blocks(scal, buf, refs, sem):
-    copies = []
-    for dq in range(2):
-        for dc in range(2):
-            for slot in range(2):
-                copies.append(
-                    pltpu.make_async_copy(
-                        buf.at[pl.ds(block_place(scal, dq, dc, slot), BLK)],
-                        refs[dq].at[dc, slot],
-                        sem.at[dq * 4 + dc * 2 + slot],
-                    )
-                )
-    for copy in copies:
-        copy.start()
-    for copy in copies:
-        copy.wait()
-
-
 def each_crop(scal, body):
     def step(item, carry):
-        units = scal[2 + CROPS + item]
+        units = scal[CROPS + item]
         for count in range(2, 9):
 
             @pl.when(units == count)
             def _():
-                body(item, pl.multiple_of(scal[2 + item], UNIT), count * UNIT)
+                body(item, pl.multiple_of(scal[item], UNIT), count * UNIT)
 
         return carry
 
@@ -402,13 +361,11 @@
     return lax.dot_general(a, b, (((0,), (0,)), ((), ())), preferred_element_type=F32)
 
 
-def attn_fwd_kernel(scal, t0, t1, pack, o0, o1, lse, buf, obuf, sem):
-    for copy in load_blocks(scal, (t0, t1), buf, sem):
-        copy.wait()
+def attn_fwd_kernel(scal, buf, pack, obuf, lse):
     lane = lax.broadcasted_iota(jnp.int32, (1, LANES), 1)
 
     def body(item, start, size):
-        live = scal[2 + 2 * CROPS + item]
+        live = scal[2 * CROPS + item]
         keys_live = lax.broadcasted_iota(jnp.int32, (1, size), 1) < live
         rows_live = (lax.broadcasted_iota(jnp.int32, (size, 1), 0) < live).astype(F32)
         window = pl.ds(start, size)
@@ -425,7 +382,7 @@
             total = jnp.sum(expo, axis=1, keepdims=True)
             prob = (expo * (1.0 / total)).astype(BF16)
             mixed = jnp.dot(prob, values, preferred_element_type=F32)
-            mask = scal[2 + 3 * CROPS + item * NH + head].astype(F32)
+            mask = scal[3 * CROPS + item * NH + head].astype(F32)
             mixed = (mixed * (rows_live * mask)).astype(BF16)
             packed += jnp.dot(
                 mixed, pack[head * LANES : (head + 1) * LANES, :], preferred_element_type=F32
@@ -435,17 +392,11 @@
         lse[window, :] = totals
 
     each_crop(scal, body)
-    store_blocks(scal, obuf, (o0, o1), sem)
-
-
-def attn_bwd_kernel(scal, t0, t1, g0, g1, lse, pack, d0, d1, buf, gbuf, dbuf, sem, gsem):
-    first = load_blocks(scal, (t0, t1), buf, sem)
-    second = load_blocks(scal, (g0, g1), gbuf, gsem)
-    for copy in first + second:
-        copy.wait()
-
+
+
+def attn_bwd_kernel(scal, buf, gbuf, lse, pack, dbuf):
     def body(item, start, size):
-        live = scal[2 + 2 * CROPS + item]
+        live = scal[2 * CROPS + item]
         keys_live = lax.broadcasted_iota(jnp.int32, (1, size), 1) < live
         rows_live = lax.broadcasted_iota(jnp.int32, (size, 1), 0) < live
         window = pl.ds(start, size)
@@ -456,7 +407,7 @@
             queries = buf[window, at : at + LANES]
             keys = buf[window, at + LANES : at + 2 * LANES]
             values = buf[window, at + 2 * LANES : at + 3 * LANES]
-            mask = scal[2 + 3 * CROPS + item * NH + head].astype(F32)
+            mask = scal[3 * CROPS + item * NH + head].astype(F32)
             grad = (nt(grads, pack[head * LANES : (head + 1) * LANES, :]) * mask).astype(BF16)
             scores = jnp.where(keys_live, nt(queries, keys) * SCALE, MASKED_SCORE)
             prob = jnp.exp(scores - lse[window, head : head + 1])
@@ -471,7 +422,6 @@
             dbuf[window, at + 2 * LANES : at + 3 * LANES] = grad_values.astype(BF16)
 
     each_crop(scal, body)
-    store_blocks(scal, dbuf, (d0, d1), sem)
 
 
 WIDE = NH * 3 * LANES
@@ -480,51 +430,29 @@
 ANY_SPEC = pl.BlockSpec(memory_space=pl.ANY)
 
 
-def attn_fwd(scal, t0, t1, pack):
+def attn_fwd(scal, triple, pack):
     return pl.pallas_call(
         attn_fwd_kernel,
         out_shape=(
-            jax.ShapeDtypeStruct((2, 2, BLK, NH * HD), BF16),
-            jax.ShapeDtypeStruct((2, 2, BLK, NH * HD), BF16),
+            jax.ShapeDtypeStruct((SEQ, NH * HD), BF16),
             jax.ShapeDtypeStruct((SEQ, LANES), F32),
         ),
-        in_specs=[SMEM_SPEC, ANY_SPEC, ANY_SPEC, VMEM_SPEC],
-        out_specs=(ANY_SPEC, ANY_SPEC, VMEM_SPEC),
-        scratch_shapes=[
-            pltpu.VMEM((SEQ, WIDE), BF16),
-            pltpu.VMEM((SEQ, NH * HD), BF16),
-            pltpu.SemaphoreType.DMA((8,)),
-        ],
+        in_specs=[SMEM_SPEC, VMEM_SPEC, VMEM_SPEC],
+        out_specs=(VMEM_SPEC, VMEM_SPEC),
         compiler_params=pltpu.CompilerParams(vmem_limit_bytes=48 * 2**20),
-        cost_estimate=pl.CostEstimate(
-            flops=4 * 10**9, bytes_accessed=6 * 10**6, transcendentals=4 * 10**6
-        ),
         name="attn_fwd",
-    )(scal, t0, t1, pack)
-
-
-def attn_bwd(scal, t0, t1, g0, g1, lse, pack):
+    )(scal, triple, pack)
+
+
+def attn_bwd(scal, triple, grads, lse, pack):
     return pl.pallas_call(
         attn_bwd_kernel,
-        out_shape=(
-            jax.ShapeDtypeStruct((2, 2, BLK, WIDE), BF16),
-            jax.ShapeDtypeStruct((2, 2, BLK, WIDE), BF16),
-        ),
-        in_specs=[SMEM_SPEC] + [ANY_SPEC] * 4 + [VMEM_SPEC] * 2,
-        out_specs=(ANY_SPEC, ANY_SPEC),
-        scratch_shapes=[
-            pltpu.VMEM((SEQ, WIDE), BF16),
-            pltpu.VMEM((SEQ, NH * HD), BF16),
-            pltpu.VMEM((SEQ, WIDE), BF16),
-            pltpu.SemaphoreType.DMA((8,)),
-            pltpu.SemaphoreType.DMA((8,)),
-        ],
+        out_shape=jax.ShapeDtypeStruct((SEQ, WIDE), BF16),
+        in_specs=[SMEM_SPEC] + [VMEM_SPEC] * 4,
+        out_specs=VMEM_SPEC,
         compiler_params=pltpu.CompilerParams(vmem_limit_bytes=48 * 2**20),
-        cost_estimate=pl.CostEstimate(
-            flops=12 * 10**9, bytes_accessed=12 * 10**6, transcendentals=4 * 10**6
-        ),
         name="attn_bwd",
-    )(scal, t0, t1, g0, g1, lse, pack)
+    )(scal, triple, grads, lse, pack)
 
 
 def line_kernel(pick, src, out, send_sem, recv_sem, loc_sem):
@@ -627,6 +555,649 @@
     )(src)
 
 
+QTR = 144
+WROWS = 576
+BIAS = 1408
+GROUPS = 24
+UNIT_ROWS = 6 * HD
+CUT = 80
+
+
+def remote(src, dst, sems, k, **where):
+    return pltpu.make_async_remote_copy(
+        src_ref=src,
+        dst_ref=dst,
+        send_sem=sems[0].at[k],
+        recv_sem=sems[1].at[k],
+        device_id=where,
+        device_id_type=MESH,
+    )
+
+
+def greet(peers):
+    barrier = pltpu.get_barrier_semaphore()
+    for where in peers:
+        pl.semaphore_signal(barrier, inc=1, device_id=where, device_id_type=MESH)
+    pl.semaphore_wait(barrier, len(peers))
+
+
+def line_peers(p, q, c):
+    out = []
+    for k in range(1, 8):
+        out.append(
+            {
+                "p": lax.rem(p + k // 4, 2),
+                "q": lax.rem(q + (k // 2) % 2, 2),
+                "c": lax.rem(c + k % 2, 2),
+            }
+        )
+    return out
+
+
+def rows_at(start, size):
+    return pl.ds(pl.multiple_of(start, 16), size)
+
+
+class PlaneGather:
+    def __init__(self, src, dst, sems, k, y, x, p):
+        self.dst, self.sems, self.k, self.y, self.x = dst, sems, k, y, x
+        self.rank = y * 2 + x
+        mine = rows_at(self.rank * QTR, QTR)
+        self.over = remote(src.at[mine], dst.at[mine], sems, k, p=1 - p)
+        self.to_x = remote(dst.at[mine], dst.at[mine], sems, k + 1, x=1 - x)
+        self.to_y = remote(dst.at[mine], dst.at[mine], sems, k + 2, y=1 - y)
+        from_x = rows_at((y * 2 + 1 - x) * QTR, CUT)
+        from_y = rows_at(((1 - y) * 2 + x) * QTR + CUT, QTR - CUT)
+        self.on_y = remote(dst.at[from_x], dst.at[from_x], sems, k + 3, y=1 - y)
+        self.on_x = remote(dst.at[from_y], dst.at[from_y], sems, k + 4, x=1 - x)
+
+    def start(self):
+        self.over.start()
+
+    def spread(self):
+        self.over.wait_recv()
+        self.to_x.start()
+        self.to_y.start()
+
+    def forward(self):
+        self.to_x.wait_recv()
+        self.on_y.start()
+        self.to_y.wait_recv()
+        self.on_x.start()
+
+    def finish(self):
+        self.on_y.wait_recv()
+        self.on_x.wait_recv()
+
+    def sent(self):
+        for copy in (self.over, self.to_x, self.to_y, self.on_y, self.on_x):
+            copy.wait_send()
+
+
+def norm_tile(values):
+    average = jnp.mean(values, axis=1, keepdims=True)
+    centred = values - average
+    inverse = lax.rsqrt(jnp.mean(centred * centred, axis=1, keepdims=True) + EPSILON)
+    return centred * inverse, inverse
+
+
+def front_kernel(
+    part, x_pair, k_pair, act, bias_own, w_a, spread, hot,
+    t_out, h_out, x_out, k_out, modg_out, wide_out, wo_out, bias_out, act_out,
+    mods, modg, h, wide, other_a, own_a, tbuf, send, recv, loc,
+):
+    y, x, p, q, c = (lax.axis_index(name) for name in "yxpqc")
+    sems = (send, recv)
+    pair = [
+        {"q": lax.rem(q + k // 2, 2), "c": lax.rem(c + k % 2, 2)} for k in range(1, 4)
+    ]
+    plane = [{"y": lax.rem(y + k // 2, 2), "x": lax.rem(x + k % 2, 2)} for k in range(1, 4)]
+    greet(pair + plane + [{"p": 1 - p}])
+    rank = y * 2 + x
+    waits = []
+
+    def keep_local(src, dst, k):
+        copy = pltpu.make_async_copy(src, dst, loc.at[k])
+        copy.start()
+        return copy
+
+    def spot(pp, qq, cc):
+        return pp * 4 + qq * 2 + cc
+
+    mod_over = remote(part.at[1 - p], mods.at[spot(p, q, c)], sems, 0, p=1 - p)
+    mod_over.start()
+    bias_copy = remote(bias_own, bias_out.at[1], sems, 7, p=1 - p)
+    bias_copy.start()
+    x_copy = remote(x_pair.at[1 - p], x_out.at[p], sems, 8, p=1 - p)
+    x_copy.start()
+    k_copy = remote(k_pair.at[1 - p], k_out.at[p], sems, 9, p=1 - p)
+    k_copy.start()
+    take_a = PlaneGather(w_a, other_a, sems, 10, y, x, p)
+    take_a.start()
+    own_mod = keep_local(part.at[p], mods.at[spot(p, q, c)], 1)
+    mod_own = []
+    mod_far = []
+    for k, where in enumerate(pair):
+        mine = mods.at[spot(p, q, c)]
+        copy = remote(part.at[p], mine, sems, 1 + k, **where)
+        copy.start()
+        mod_own.append(copy)
+    load_a = keep_local(w_a, own_a, 0)
+    waits.append(keep_local(x_pair.at[p], x_out.at[p], 2))
+    waits.append(keep_local(k_pair.at[p], k_out.at[p], 3))
+    waits.append(keep_local(bias_own, bias_out.at[0], 4))
+    waits.append(keep_local(act, act_out.at[rank], 5))
+    acts = []
+    for k, where in enumerate(plane):
+        copy = remote(act, act_out.at[rank], sems, 15 + k, **where)
+        copy.start()
+        acts.append(copy)
+    mod_over.wait_recv()
+    for k, where in enumerate(pair):
+        far = mods.at[spot(1 - p, q, c)]
+        copy = remote(far, far, sems, 4 + k, **where)
+        copy.start()
+        mod_far.append(copy)
+
+    load_a.wait()
+    wide[: 6 * LANES, :] = jnp.dot(
+        spread[...], own_a[:UNIT_ROWS, :], preferred_element_type=F32
+    ).astype(BF16)
+
+    own_mod.wait()
+    for copy in mod_own + mod_far:
+        copy.wait_recv()
+    full = jnp.concatenate([mods[k] for k in range(8)], axis=1)
+    modg[...] = jnp.dot(
+        hot[...], full, preferred_element_type=F32, precision=lax.Precision.HIGHEST
+    )
+    waits.append(keep_local(modg, modg_out, 6))
+
+    def place(slot, chip, core):
+        return slot * HALF + chip * (2 * BLK) + core * BLK
+
+    def modulate(src, slot):
+        base = place(slot, q, c)
+
+        def group(g, carry):
+            values = src[rows_at(g * 16, 16), :].astype(F32)
+            normed, _ = norm_tile(values)
+            row = slot * (BLK // 16) + g
+            shift = modg[pl.ds(row, 1), 0:D]
+            scale = modg[pl.ds(row, 1), D : 2 * D]
+            h[rows_at(base + g * 16, 16), :] = (normed * (1.0 + scale) + shift).astype(BF16)
+            return carry
+
+        lax.fori_loop(0, BLK // 16, group, 0)
+
+    def block(slot, chip, core):
+        return h.at[rows_at(place(slot, chip, core), BLK)]
+
+    hops = {}
+    for i in range(2):
+        slot = p if i == 0 else 1 - p
+        mine = block(slot, q, c)
+        other = block(slot, 1 - q, c)
+        hops[i] = (
+            remote(mine, mine, sems, 18 + 3 * i, q=1 - q),
+            remote(mine, mine, sems, 19 + 3 * i, c=1 - c),
+            remote(other, other, sems, 20 + 3 * i, c=1 - c),
+        )
+
+    modulate(x_pair.at[p], p)
+    hops[0][0].start()
+    hops[0][1].start()
+    x_copy.wait_recv()
+    modulate(x_out.at[1 - p], 1 - p)
+    hops[1][0].start()
+    hops[1][1].start()
+    take_a.spread()
+    bias_copy.wait_recv()
+    for copy in waits[2:3]:
+        copy.wait()
+    hops[0][1].wait_recv()
+
+    def project(slot, chip, half):
+        rows = rows_at(place(slot, chip, 0), 2 * BLK)
+        cols = slice(half * 6 * LANES, (half + 1) * 6 * LANES)
+        line = bias_out[half, 0:1, : 6 * LANES]
+        tbuf[rows, cols] = (nt(h[rows, :], wide[cols, :]) + line).astype(BF16)
+
+    first, second = p, 1 - p
+    project(first, q, 0)
+    hops[0][0].wait_recv()
+    hops[0][2].start()
+    hops[1][1].wait_recv()
+    project(second, q, 0)
+    take_a.forward()
+    hops[0][2].wait_recv()
+    project(first, 1 - q, 0)
+    hops[1][0].wait_recv()
+    hops[1][2].start()
+    take_a.finish()
+    wide[6 * LANES :, :] = jnp.dot(
+        spread[...], other_a[:UNIT_ROWS, :], preferred_element_type=F32
+    ).astype(BF16)
+    waits.append(keep_local(wide, wide_out, 7))
+    tails = (own_a.at[UNIT_ROWS:], other_a.at[UNIT_ROWS:])
+    outer = [remote(tails[k], wo_out.at[2 + k], sems, 24 + k, q=1 - q) for k in range(2)]
+    for copy in outer:
+        copy.start()
+    for k in range(2):
+        waits.append(keep_local(tails[k], wo_out.at[k], 8 + k))
+    project(first, q, 1)
+    project(second, q, 1)
+    project(first, 1 - q, 1)
+    hops[1][2].wait_recv()
+    waits.append(keep_local(h, h_out, 10))
+    project(second, 1 - q, 0)
+    project(second, 1 - q, 1)
+    waits.append(keep_local(tbuf, t_out, 11))
+    for copy in outer + acts + [k_copy]:
+        copy.wait_recv()
+    for copy in [mod_over, bias_copy, x_copy, k_copy] + mod_own + mod_far + outer + acts:
+        copy.wait_send()
+    for i in range(2):
+        for copy in hops[i]:
+            copy.wait_send()
+    take_a.sent()
+    for k, copy in enumerate(waits):
+        if k != 2:
+            copy.wait()
+
+
+def shape_of(*shape, dtype=BF16):
+    return jax.ShapeDtypeStruct(shape, dtype)
+
+
+def front(part, x_pair, k_pair, act, bias_own, w_a, spread, hot):
+    return pl.pallas_call(
+        front_kernel,
+        out_shape=(
+            shape_of(SEQ, WIDE), shape_of(SEQ, D), shape_of(2, BLK, D), shape_of(2, BLK, LANES),
+            shape_of(GROUPS, 6 * D, dtype=F32), shape_of(WIDE, D), shape_of(4, QTR, D),
+            shape_of(2, 8, BIAS, dtype=F32), shape_of(4, 2, 16, D),
+        ),
+        in_specs=[VMEM_SPEC] * 5 + [ANY_SPEC] + [VMEM_SPEC] * 2,
+        out_specs=(
+            ANY_SPEC, ANY_SPEC, VMEM_SPEC, VMEM_SPEC, ANY_SPEC, ANY_SPEC, ANY_SPEC, VMEM_SPEC,
+            VMEM_SPEC,
+        ),
+        scratch_shapes=[
+            pltpu.VMEM((8, 16, 6 * D // 8), F32),
+            pltpu.VMEM((GROUPS, 6 * D), F32),
+            pltpu.VMEM((SEQ, D), BF16),
+            pltpu.VMEM((WIDE, D), BF16),
+            pltpu.VMEM((WROWS, D), BF16),
+            pltpu.VMEM((WROWS, D), BF16),
+            pltpu.VMEM((SEQ, WIDE), BF16),
+            pltpu.SemaphoreType.DMA((26,)),
+            pltpu.SemaphoreType.DMA((26,)),
+            pltpu.SemaphoreType.DMA((12,)),
+        ],
+        compiler_params=pltpu.CompilerParams(
+            collective_id=6, has_side_effects=True, vmem_limit_bytes=56 * 2**20
+        ),
+        name="front",
+    )(part, x_pair, k_pair, act, bias_own, w_a, spread, hot)
+
+
+def gelu_both(u):
+    cube = 0.044715 * u * u
+    t = jnp.tanh(0.7978845608028654 * (u + cube * u))
+    half = 0.5 * (1.0 + t)
+    slope = half + 0.5 * u * (1.0 - t * t) * (0.7978845608028654 * (1.0 + 3.0 * cube))
+    return u * half, slope
+
+
+def middle_kernel(
+    o, x2, k2, modg, g_pair, wo, w_up, w_down, bias, consts, gmask,
+    final_out, dx_out, do_out, sums_out, small_out, up_out, down_out, gwo_out, bup_out,
+    g2, o_in, ybig, ysend, yrecv, y1, mixed, h2, dz, act, du, wup, wdown,
+    own, csend, crecv, qsend, qrecv, dy, dofar, wosend, worecv, send, recv, loc,
+):
+    y, x, p, q, c = (lax.axis_index(name) for name in "yxpqc")
+    sems = (send, recv)
+    greet([{"q": 1 - q}, {"c": 1 - c}, {"p": 1 - p}, {"x": 1 - x}, {"y": 1 - y}])
+    waits = []
+
+    def keep_local(src, dst, k):
+        copy = pltpu.make_async_copy(src, dst, loc.at[k])
+        copy.start()
+        return copy
+
+    def place(slot, chip, core):
+        return slot * HALF + chip * (2 * BLK) + core * BLK
+
+    o_copies = []
+    for slot in range(2):
+        copy = remote(
+            o.at[rows_at(place(slot, 1 - q, 0), 2 * BLK)], o_in.at[slot], sems, slot, q=1 - q
+        )
+        copy.start()
+        o_copies.append(copy)
+    g_copy = remote(g_pair.at[1 - p], g2.at[pl.ds(p * BLK, BLK)], sems, 2, p=1 - p)
+    g_copy.start()
+    take_up = PlaneGather(w_up, wup.at[WROWS:], sems, 3, y, x, p)
+    take_down = PlaneGather(w_down, wdown.at[WROWS:], sems, 8, y, x, p)
+    take_up.start()
+    take_down.start()
+    own_g = keep_local(g_pair.at[p], g2.at[pl.ds(p * BLK, BLK)], 0)
+    own_up = keep_local(w_up, wup.at[:WROWS], 1)
+    own_down = keep_local(w_down, wdown.at[:WROWS], 2)
+
+    y_copies = []
+    for slot in range(2):
+        rows = rows_at(place(slot, q, 0), 2 * BLK)
+        o_copies[slot].wait_recv()
+        ybig[...] = jnp.dot(o[rows, :], wo[0 : 2 * QTR, :], preferred_element_type=F32) + jnp.dot(
+            o_in[slot], wo[2 * QTR : 4 * QTR, :], preferred_element_type=F32
+        )
+        ysend[slot] = ybig[rows_at((1 - c) * BLK, BLK), :].astype(BF16)
+        y1[slot * BLK : (slot + 1) * BLK, :] = ybig[rows_at(c * BLK, BLK), :]
+        copy = remote(ysend.at[slot], yrecv.at[slot], sems, 13 + slot, c=1 - c)
+        copy.start()
+        y_copies.append(copy)
+
+    own_g.wait()
+    g_copy.wait_recv()
+    take_up.spread()
+    b_out, b_down, w_route = consts[0:1, :], consts[1:2, :], consts[2:3, :]
+
+    def routed(row):
+        rows = rows_at(row * 16, 16)
+        normed, inverse = norm_tile(mixed[rows, :])
+        hidden = normed * (1.0 + modg[pl.ds(row, 1), 4 * D : 5 * D]) + modg[
+            pl.ds(row, 1), 3 * D : 4 * D
+        ]
+        logit = jnp.sum(hidden * w_route, axis=1, keepdims=True)
+        route = 1.0 / (1.0 + jnp.exp(-logit))
+        kept = k2[rows, 0:1].astype(F32)
+        return rows, normed, inverse, hidden, route, kept
+
+    bufs = (h2, dz)
+
+    def hop(array, slot, kind):
+        mine = bufs[array].at[rows_at(place(slot, q, c), BLK)]
+        far = bufs[array].at[rows_at(place(slot, 1 - q, c), BLK)]
+        k = 15 + (slot * 2 + array) * 3 + kind
+        if kind == 0:
+            return remote(mine, mine, sems, k, q=1 - q)
+        if kind == 1:
+            return remote(mine, mine, sems, k, c=1 - c)
+        return remote(far, far, sems, k, c=1 - c)
+
+    for slot in range(2):
+        y_copies[slot].wait_recv()
+
+        def group(g, carry, slot=slot):
+            row = slot * (BLK // 16) + g
+            rows = rows_at(row * 16, 16)
+            branch = y1[rows, :] + yrecv[slot, rows_at(g * 16, 16), :].astype(F32) + b_out
+            y1[rows, :] = branch
+            mixed[rows, :] = x2[rows, :].astype(F32) + modg[pl.ds(row, 1), 2 * D : 3 * D] * branch
+            _, _, _, hidden, route, kept = routed(row)
+            there = rows_at(place(slot, q, c) + g * 16, 16)
+            h2[there, :] = hidden.astype(BF16)
+            gate = modg[pl.ds(row, 1), 5 * D : 6 * D]
+            dz[there, :] = (g2[rows, :].astype(F32) * gate * (kept * route)).astype(BF16)
+            return carry
+
+        lax.fori_loop(0, BLK // 16, group, 0)
+        for array in range(2):
+            hop(array, slot, 0).start()
+            hop(array, slot, 1).start()
+
+    take_up.forward()
+    take_down.spread()
+    own_up.wait()
+    own_down.wait()
+    take_up.finish()
+    take_down.forward()
+    take_down.finish()
+
+    def core_copy(array, side, slot):
+        k = 27 + (array * 2 + side) * 2 + slot
+        return remote(csend.at[array, side, slot], crecv.at[array, side, slot], sems, k, c=1 - c)
+
+    def chip_copy(array, slot):
+        return remote(qsend.at[array, slot], qrecv.at[array, slot], sems, 35 + array * 2 + slot, q=1 - q)
+
+    def far_out(slot):
+        for array in range(2):
+            core_copy(array, 1, slot).wait_recv()
+            qsend[array, slot] = (
+                own[array, 1, slot] + crecv[array, 1, slot].astype(F32)
+            ).astype(BF16)
+            chip_copy(array, slot).start()
+
+    def feed(step, carry):
+        side, slot = step // 2, lax.rem(step, 2)
+        chip = lax.rem(q + side, 2)
+        start = place(slot, chip, 0)
+
+        @pl.when(step == 0)
+        def _():
+            for array in range(2):
+                hop(array, 0, 1).wait_recv()
+
+        @pl.when(step == 1)
+        def _():
+            for array in range(2):
+                hop(array, 1, 1).wait_recv()
+
+        @pl.when(step == 2)
+        def _():
+            for array in range(2):
+                hop(array, 0, 0).wait_recv()
+                hop(array, 0, 2).start()
+            for array in range(2):
+                hop(array, 0, 2).wait_recv()
+
+        @pl.when(step == 3)
+        def _():
+            for array in range(2):
+                hop(array, 1, 0).wait_recv()
+                hop(array, 1, 2).start()
+            far_out(0)
+            for array in range(2):
+                hop(array, 1, 2).wait_recv()
+
+        def tile(part, carry):
+            rows = rows_at(start + part * BLK, BLK)
+            u = nt(h2[rows, :], wup[...]) + bias[0:1, :]
+            value, slope = gelu_both(u)
+            row0 = start // 16 + part * (BLK // 16)
+            mask = jnp.concatenate(
+                [
+                    jnp.broadcast_to(gmask[pl.ds(row0 + k, 1), :], (16, D))
+                    for k in range(BLK // 16)
+                ],
+                axis=0,
+            )
+            act[rows, :] = (value * mask).astype(BF16)
+            da = nt(dz[rows, :], wdown[...])
+            du[rows, :] = (slope * mask * da).astype(BF16)
+            z_part = jnp.dot(act[rows, :], wdown[...], preferred_element_type=F32)
+            h_part = jnp.dot(du[rows, :], wup[...], preferred_element_type=F32)
+
+            @pl.when(part == c)
+            def _():
+                own[0, side, slot] = z_part
+                own[1, side, slot] = h_part
+
+            @pl.when(part != c)
+            def _():
+                csend[0, side, slot] = z_part.astype(BF16)
+                csend[1, side, slot] = h_part.astype(BF16)
+
+            return carry
+
+        lax.fori_loop(0, 2, tile, 0)
+        for array in range(2):
+            core_copy(array, side, slot).start()
+        return carry
+
+    lax.fori_loop(0, 4, feed, 0)
+    far_out(1)
+
+    for copy in (take_up, take_down):
+        copy.sent()
+
+    def weight_chunk(j, carry):
+        cols = pl.ds(pl.multiple_of(j * 384, LANES), 384)
+        rows = rows_at(j * 384, 384)
+        wup[rows, :] = tn(du[:, cols], h2[...]).astype(BF16)
+        wdown[rows, :] = tn(act[:, cols], dz[...]).astype(BF16)
+        return carry
+
+    lax.fori_loop(0, 3, weight_chunk, 0)
+    waits.append(keep_local(wup, up_out, 3))
+    waits.append(keep_local(wdown, down_out, 4))
+    bup_out[...] = jnp.dot(jnp.ones((8, SEQ), BF16), du[...], preferred_element_type=F32)
+
+    small_out[...] = jnp.zeros_like(small_out)
+    sums_out[22:24, :] = jnp.zeros((2, 4 * D), F32)
+    dy_copies = []
+    do_copies = []
+    for slot in range(2):
+        for array in range(2):
+            core_copy(array, 0, slot).wait_recv()
+            chip_copy(array, slot).wait_recv()
+
+        def back(g, carry, slot=slot):
+            row = slot * (BLK // 16) + g
+            rows, normed, inverse, hidden, route, kept = routed(row)
+            here = rows_at(g * 16, 16)
+
+            def total(array):
+                return (
+                    own[array, 0, slot, here, :]
+                    + crecv[array, 0, slot, here, :].astype(F32)
+                    + qrecv[array, slot, here, :].astype(F32)
+                )
+
+            gate_one = modg[pl.ds(row, 1), 2 * D : 3 * D]
+            gate_two = modg[pl.ds(row, 1), 5 * D : 6 * D]
+            scale_two = modg[pl.ds(row, 1), 4 * D : 5 * D]
+            grad = g2[rows, :].astype(F32)
+            pass_on = kept * route
+            branch = total(0) + b_down
+            final_out[rows, :] = (mixed[rows, :] + gate_two * pass_on * branch).astype(BF16)
+            grad_gate_two = grad * pass_on * branch
+            gated = grad * gate_two
+            logit = (
+                jnp.sum(gated * branch, axis=1, keepdims=True) * kept * route * (1.0 - route)
+            )
+            dh = total(1) + logit * w_route
+            e = dh * (1.0 + scale_two)
+            dx = grad + inverse * (
+                e
+                - jnp.mean(e, axis=1, keepdims=True)
+                - normed * jnp.mean(e * normed, axis=1, keepdims=True)
+            )
+            dx_out[rows, :] = dx
+            dyb = dx * gate_one
+            dy[slot, c, here, :] = dyb.astype(BF16)
+
+            def down(v):
+                return jnp.sum(v, axis=0, keepdims=True)
+
+            small_out[0:1, :] += down(dyb)
+            small_out[1:2, :] += down(gated * pass_on)
+            small_out[2:3, :] += down(logit * hidden)
+            at = pl.ds(row, 1)
+            sums_out[at, 0:D] = down(dx * y1[rows, :])
+            sums_out[at, D : 2 * D] = down(dh)
+            sums_out[at, 2 * D : 3 * D] = down(dh * normed)
+            sums_out[at, 3 * D : 4 * D] = down(grad_gate_two)
+            return carry
+
+        lax.fori_loop(0, BLK // 16, back, 0)
+        copy = remote(dy.at[slot, c], dy.at[slot, c], sems, 39 + slot, c=1 - c)
+        copy.start()
+        dy_copies.append(copy)
+    for slot in range(2):
+        dy_copies[slot].wait_recv()
+        rows = rows_at(place(slot, q, 0), 2 * BLK)
+        grads = dy[slot].reshape(2 * BLK, D)
+        dofar[slot] = nt(grads, wo[2 * QTR : 4 * QTR, :]).astype(BF16)
+        copy = remote(dofar.at[slot], do_out.at[rows], sems, 41 + slot, q=1 - q)
+        copy.start()
+        do_copies.append(copy)
+        do_out[rows, :] = nt(grads, wo[0 : 2 * QTR, :]).astype(BF16)
+
+    def out_grad(left):
+        return sum(tn(left(slot), dy[slot].reshape(2 * BLK, D)) for slot in range(2))
+
+    wosend[...] = out_grad(lambda slot: o_in[slot]).astype(BF16)
+    wo_copy = remote(wosend, worecv, sems, 43, q=1 - q)
+    wo_copy.start()
+    near = out_grad(lambda slot: o[rows_at(place(slot, q, 0), 2 * BLK), :])
+    wo_copy.wait_recv()
+    gwo_out[...] = (near + worecv[...].astype(F32)).astype(BF16)
+    for copy in do_copies:
+        copy.wait_recv()
+    for copy in o_copies + [g_copy] + y_copies + dy_copies + do_copies + [wo_copy]:
+        copy.wait_send()
+    for slot in range(2):
+        for array in range(2):
+            for kind in range(3):
+                hop(array, slot, kind).wait_send()
+            for side in range(2):
+                core_copy(array, side, slot).wait_send()
+            chip_copy(array, slot).wait_send()
+    for copy in waits:
+        copy.wait()
+
+
+def middle(o, x2, k2, modg, g_pair, wo, w_up, w_down, bias, consts, gmask):
+    return pl.pallas_call(
+        middle_kernel,
+        out_shape=(
+            shape_of(2 * BLK, D), shape_of(2 * BLK, D, dtype=F32), shape_of(SEQ, NH * HD),
+            shape_of(GROUPS, 4 * D, dtype=F32), shape_of(8, D, dtype=F32), shape_of(D, D),
+            shape_of(D, D), shape_of(NH * HD, D), shape_of(8, D, dtype=F32),
+        ),
+        in_specs=[VMEM_SPEC] * 6 + [ANY_SPEC] * 2 + [VMEM_SPEC] * 3,
+        out_specs=(
+            VMEM_SPEC, VMEM_SPEC, VMEM_SPEC, VMEM_SPEC, VMEM_SPEC, ANY_SPEC, ANY_SPEC, VMEM_SPEC,
+            VMEM_SPEC,
+        ),
+        scratch_shapes=[
+            pltpu.VMEM((2 * BLK, D), BF16),
+            pltpu.VMEM((2, 2 * BLK, NH * HD), BF16),
+            pltpu.VMEM((2 * BLK, D), F32),
+            pltpu.VMEM((2, BLK, D), BF16),
+            pltpu.VMEM((2, BLK, D), BF16),
+            pltpu.VMEM((2 * BLK, D), F32),
+            pltpu.VMEM((2 * BLK, D), F32),
+            pltpu.VMEM((SEQ, D), BF16),
+            pltpu.VMEM((SEQ, D), BF16),
+            pltpu.VMEM((SEQ, D), BF16),
+            pltpu.VMEM((SEQ, D), BF16),
+            pltpu.VMEM((D, D), BF16),
+            pltpu.VMEM((D, D), BF16),
+            pltpu.VMEM((2, 2, 2, BLK, D), F32),
+            pltpu.VMEM((2, 2, 2, BLK, D), BF16),
+            pltpu.VMEM((2, 2, 2, BLK, D), BF16),
+            pltpu.VMEM((2, 2, BLK, D), BF16),
+            pltpu.VMEM((2, 2, BLK, D), BF16),
+            pltpu.VMEM((2, 2, BLK, D), BF16),
+            pltpu.VMEM((2, 2 * BLK, NH * HD), BF16),
+            pltpu.VMEM((NH * HD, D), BF16),
+            pltpu.VMEM((NH * HD, D), BF16),
+            pltpu.SemaphoreType.DMA((44,)),
+            pltpu.SemaphoreType.DMA((44,)),
+            pltpu.SemaphoreType.DMA((5,)),
+        ],
+        compiler_params=pltpu.CompilerParams(
+            collective_id=7, has_side_effects=True, vmem_limit_bytes=63 * 2**20
+        ),
+        name="middle",
+    )(o, x2, k2, modg, g_pair, wo, w_up, w_down, bias, consts, gmask)
+
+
 def swap(values, axis):
     return lax.ppermute(values, axis, SWAP)
 
@@ -636,7 +1207,7 @@
 
 
 def plane_gather(part, rank):
-    half = part.shape[0] // 2
+    half = 80
     by_x = swap(part, "x")
     by_y = swap(part, "y")
     far = jnp.concatenate([swap(by_x[:half], "y"), swap(by_y[half:], "x")], axis=0)
@@ -647,10 +1218,10 @@
 
 
 def plane_scatter(parts, rank):
-    half = parts.shape[1] // 2
+    half = 80
     rel = [at_index(parts, rank ^ k) for k in range(4)]
-    low = [v[:half] for v in rel]
-    high = [v[half:] for v in rel]
+    low = [v[:, :half] for v in rel]
+    high = [v[:, half:] for v in rel]
     in_x = swap(jnp.stack([low[1], low[3]]), "x").astype(F32)
     in_y = swap(jnp.stack([high[2], high[3]]), "y").astype(F32)
     low_own = low[0].astype(F32) + in_x[0]
@@ -659,7 +1230,7 @@
     high_rest = (high[1].astype(F32) + in_y[1]).astype(BF16)
     low_own = low_own + swap(low_rest, "y").astype(F32)
     high_own = high_own + swap(high_rest, "x").astype(F32)
-    return jnp.concatenate([low_own, high_own], axis=0)
+    return jnp.concatenate([low_own, high_own], axis=1)
 
 
 def layer_device(
@@ -673,36 +1244,19 @@
     shard = p * 4 + q * 2 + c
     partner = shard ^ 4
 
-    def to_rows(values):
-        mine = jnp.where(first, values[:, 0], values[:, 1])
-        other = swap(jnp.where(first, values[:, 1], values[:, 0]), "p")
-        return jnp.stack([jnp.where(first, mine, other), jnp.where(first, other, mine)])
-
-    def other_shard(weight):
-        quarter = weight.shape[0] // 4
-        mine = lax.dynamic_slice_in_dim(weight, rank * quarter, quarter, 0)
-        return plane_gather(swap(mine, "p"), rank).reshape(weight.shape)
-
-    token_low = to_rows(tokens)
-    spread = np.zeros((6 * HD, 6 * LANES), np.float32)
+    spread = np.zeros((6 * LANES, UNIT_ROWS), np.float32)
     for unit in range(6):
-        spread[np.arange(HD) + unit * HD, np.arange(HD) + unit * LANES] = 1.0
+        spread[np.arange(HD) + unit * LANES, np.arange(HD) + unit * HD] = 1.0
     spread = jnp.asarray(spread, BF16)
-    qkv_other = other_shard(w_qkv)
-    w_qkv_wide = jnp.concatenate(
-        [
-            jnp.dot(w_qkv, spread, preferred_element_type=F32).astype(BF16),
-            jnp.dot(qkv_other, spread, preferred_element_type=F32).astype(BF16),
-        ],
-        axis=1,
-    )
-    biases = jnp.concatenate([b_up, b_qv])
-    biases_other = swap(biases, "p")
-    pairs = jnp.stack([b_qv, biases_other[2 * GW :]]).reshape(4, 2, HD).astype(F32)
-    bias_wide = jnp.pad(
+    w_up_rows = jnp.transpose(w_up)
+    w_a = jnp.concatenate([jnp.transpose(w_qkv), w_out])
+    pairs = b_qv.reshape(2, 2, HD).astype(F32)
+    bias_own = jnp.pad(
         jnp.stack([pairs[:, 0], jnp.zeros_like(pairs[:, 0]), pairs[:, 1]], axis=1),
         ((0, 0), (0, 0), (0, LANES - HD)),
-    ).reshape(WIDE)
+    ).reshape(6 * LANES)
+    bias_own = jnp.pad(jnp.concatenate([bias_own, b_up.astype(F32)]), (0, BIAS - 1344))
+    bias_own = jnp.broadcast_to(bias_own, (8, BIAS))
 
     cvec = cond.astype(F32) + time_embed(timesteps)
     sig = lax.logistic(cvec)
@@ -710,9 +1264,6 @@
     mod_part = jnp.einsum("bcd,dm->bcm", act_low, ada_w, preferred_element_type=F32) + ada_b.astype(
         F32
     )
-    mod = line_exchange(mod_part, "row", 1, "mod_exchange")
-    mod = jnp.transpose(mod, (1, 0, 2)).reshape(16, 6 * D)
-
     def row_of(values):
         return jnp.where(first, values[0], values[1])
 
@@ -728,10 +1279,17 @@
         return jnp.pad(inside.astype(F32), ((0, 0), (0, 0), (0, 5)))
 
     hot = group_hot(0, 0)
-    mod_groups = jnp.einsum("sgc,cm->sgm", hot, mod, precision=highest)
-    shift_one, scale_one, gate_one, shift_two, scale_two, gate_two = (
-        mod_groups[:, :, None, k * D : (k + 1) * D] for k in range(6)
-    )
+    hot_rows = jnp.pad(hot.reshape(22, 16), ((0, 2), (0, 0)))
+
+    def by_row(values):
+        return jnp.transpose(values, (1, 0, 2))
+
+    keep_wide = jnp.broadcast_to(keep.T.astype(BF16)[..., None], (2, BLK, LANES))
+    triple, hidden_one, token_low, keep_low, mod_groups, w_wide, w_out_all, biases, act_all = front(
+        mod_part, by_row(tokens), keep_wide, act_low, bias_own, w_a, spread, hot_rows
+    )
+    mod_rows = mod_groups[:22].reshape(2, BLK // 16, 6 * D)
+    scale_one = mod_rows[:, :, None, D : 2 * D]
 
     def grouped(values):
         return values.reshape(2, BLK // 16, 16, -1)
@@ -741,16 +1299,6 @@
 
     token_values = grouped(token_low.astype(F32))
     normed_one, inverse_one = norm_rows(token_values)
-    hidden_one = flat((normed_one * (1.0 + scale_one) + shift_one).astype(BF16))
-
-    def group_gather(block):
-        far = swap(block, "q")
-        near = swap(block, "c")
-        far_near = swap(far, "c")
-        return (
-            jnp.stack([block, near]).reshape(4 * BLK, -1),
-            jnp.stack([far, far_near]).reshape(4 * BLK, -1),
-        )
 
     def group_scatter(near_part, far_part):
         far_sum = (far_part[0].astype(F32) + swap(far_part[1], "c").astype(F32)).astype(BF16)
@@ -758,16 +1306,19 @@
         near_sum = near_part[0].astype(F32) + swap(near_part[1], "c").astype(F32)
         return near_sum + far_in.astype(F32)
 
-    h1_near, h1_far = group_gather(hidden_one)
-
-    def project(h):
-        return (
-            (jnp.dot(h, w_qkv_wide, preferred_element_type=F32) + bias_wide)
-            .astype(BF16)
-            .reshape(2, 2, BLK, WIDE)
-        )
-
-    t_near, t_far = project(h1_near), project(h1_far)
+    def split_chips(values):
+        parts = values.reshape(2, 2, 2, BLK, -1)
+
+        def chip(index):
+            one = lax.dynamic_index_in_dim(parts, index, 1, keepdims=False)
+            return jnp.stack(
+                [
+                    lax.dynamic_index_in_dim(one, c, 1, keepdims=False),
+                    lax.dynamic_index_in_dim(one, 1 - c, 1, keepdims=False),
+                ]
+            )
+
+        return chip(q), chip(1 - q)
 
     head_row = row_of(head_mask)
     heads_here = jnp.concatenate(
@@ -779,7 +1330,6 @@
     )
     scal = jnp.concatenate(
         [
-            jnp.stack([q, c]).astype(jnp.int32),
             starts,
             row_len // UNIT,
             row_len - row_pad,
@@ -790,34 +1340,7 @@
     for head in range(NH):
         pack[np.arange(HD) + head * LANES, np.arange(HD) + head * HD] = 1.0
     pack = jnp.asarray(pack, BF16)
-    o_near, o_far, lse = attn_fwd(scal, t_near, t_far, pack)
-
-    w_out_two = jnp.concatenate([w_out, other_shard(w_out)], axis=0)
-    w_out_far = swap(w_out_two, "q")
-    o_mine = o_near.reshape(4 * BLK, NH * HD)
-    o_in = swap(o_far, "q").reshape(4 * BLK, NH * HD)
-    y_part = jnp.dot(o_mine, w_out_two, preferred_element_type=F32) + jnp.dot(
-        o_in, w_out_far, preferred_element_type=F32
-    )
-    y_part = y_part.astype(BF16).reshape(2, 2, BLK, D)
-    projected = grouped(y_part[0].astype(F32) + swap(y_part[1], "c").astype(F32))
-    branch_one = projected + b_out.astype(F32)
-    mixed = token_values + gate_one * branch_one
-    normed_two, inverse_two = norm_rows(mixed)
-    hidden_two = normed_two * (1.0 + scale_two) + shift_two
-    route_w = w_route.astype(F32)
-    route = lax.logistic(jnp.sum(hidden_two * route_w, axis=-1, keepdims=True))
-    keep_values = grouped(to_rows(keep.astype(F32)[..., None]))
-    route_keep = keep_values * route
-    grad_low = to_rows(grad_out)
-    grad_final = grouped(grad_low.astype(F32))
-    grad_branch = grad_final * gate_two * route_keep
-    h2_near, h2_far = group_gather(flat(hidden_two.astype(BF16)))
-    dz_near, dz_far = group_gather(flat(grad_branch.astype(BF16)))
-
-    w_up_two = jnp.concatenate([w_up, other_shard(w_up)], axis=1)
-    w_down_two = jnp.concatenate([w_down, other_shard(w_down)], axis=0)
-    b_up_two = jnp.concatenate([b_up, biases_other[: 2 * GW]]).astype(F32)
+    attended, lse = attn_fwd(scal, triple, pack)
     group_row = row_of(group_mask)
     groups_here = jnp.concatenate(
         [
@@ -826,91 +1349,46 @@
         ],
         axis=1,
     ).astype(F32)
-    groups_here = jnp.pad(groups_here, ((0, 5), (0, 0)))
-
-    def feed(h2, dz, dq):
-        hots = jnp.stack([group_hot(dq, 0), group_hot(dq, 1)])
-        mask = jnp.einsum("usgc,ch->usgh", hots, groups_here, precision=highest)
-        mask = jnp.repeat(mask, GW, axis=-1)[:, :, :, None, :]
-
-        def spread_mask(values):
-            return (values.reshape(2, 2, BLK // 16, 16, 4 * GW) * mask).reshape(4 * BLK, 4 * GW)
-
-        upper = jnp.dot(h2, w_up_two, preferred_element_type=F32) + b_up_two
-        active, back = jax.vjp(gelu_tanh, upper)
-        active_low = spread_mask(active).astype(BF16)
-        z_part = jnp.dot(active_low, w_down_two, preferred_element_type=F32).astype(BF16)
-        grad_active = lax.dot_general(
-            dz, w_down_two, (((1,), (1,)), ((), ())), preferred_element_type=F32
-        )
-        (grad_upper,) = back(spread_mask(grad_active))
-        upper_low = grad_upper.astype(BF16)
-        dh_part = lax.dot_general(
-            upper_low, w_up_two, (((1,), (1,)), ((), ())), preferred_element_type=F32
-        ).astype(BF16)
-        return active_low, upper_low, z_part.reshape(2, 2, BLK, D), dh_part.reshape(2, 2, BLK, D)
-
-    a_far, u_far, z_far, dh_far = feed(h2_far, dz_far, 1)
-    a_near, u_near, z_near, dh_near = feed(h2_near, dz_near, 0)
-    lowered = grouped(group_scatter(z_near, z_far))
-    grad_hidden_two = grouped(group_scatter(dh_near, dh_far))
-    grad_w_up = tn(h2_near, u_near) + tn(h2_far, u_far)
-    grad_w_down = tn(a_near, dz_near) + tn(a_far, dz_far)
-    grad_b_up = jnp.sum(u_near, axis=0, dtype=F32) + jnp.sum(u_far, axis=0, dtype=F32)
-
-    branch = lowered + b_down.astype(F32)
-    final = mixed + gate_two * route_keep * branch
-    grad_gate_two = grad_final * route_keep * branch
-    grad_logit = (
-        jnp.sum(grad_final * gate_two * branch, axis=-1, keepdims=True)
-        * keep_values
-        * route
-        * (1.0 - route)
-    )
-    part_route = jnp.sum(grad_logit * hidden_two, axis=(0, 1, 2))
-    part_b_down = jnp.sum(grad_branch, axis=(0, 1, 2))
-    grad_hidden_two = grad_hidden_two + grad_logit * route_w
-    grad_scale_two = grad_hidden_two * normed_two
-    grad_mixed = grad_final + norm_back(
-        grad_hidden_two * (1.0 + scale_two), normed_two, inverse_two
-    )
-    grad_gate_one = grad_mixed * branch_one
-    grad_projected = grad_mixed * gate_one
-    part_b_out = jnp.sum(grad_projected, axis=(0, 1, 2))
-    dy_own = flat(grad_projected.astype(BF16))
-    dy = jnp.stack([dy_own, swap(dy_own, "c")]).reshape(4 * BLK, D)
-    do_out = nt(dy, w_out_far).astype(BF16).reshape(2, 2, BLK, NH * HD)
-    do_far = swap(do_out, "q")
-    do_near = nt(dy, w_out_two).astype(BF16).reshape(2, 2, BLK, NH * HD)
-    d_near, d_far = attn_bwd(scal, t_near, t_far, do_near, do_far, lse, pack)
-    d_near = d_near.reshape(4 * BLK, WIDE)
-    d_far = d_far.reshape(4 * BLK, WIDE)
-    dh1_far = nt(d_far, w_qkv_wide).astype(BF16).reshape(2, 2, BLK, D)
-    dh1_near = nt(d_near, w_qkv_wide).astype(BF16).reshape(2, 2, BLK, D)
+    all_places = jnp.arange(SEQ // 16)[:, None] * 16
+    all_hot = ((all_places >= starts) & (all_places < ends)).astype(F32)
+    group_wide = jnp.repeat(
+        jnp.dot(all_hot, groups_here, precision=highest), GW, axis=1
+    )
+    consts = jnp.pad(jnp.stack([b_out, b_down, w_route]).astype(F32), ((0, 5), (0, 0)))
+    b_up_two = jnp.concatenate([biases[0, :, 768:1344], biases[1, :, 768:1344]], axis=1)
+    final, grad_mixed, grad_attended, sums_two, smalls, up_low, down_low, wo_low, b_up_sums = middle(
+        attended, token_low.reshape(2 * BLK, D), keep_low.reshape(2 * BLK, LANES), mod_groups,
+        by_row(grad_out), w_out_all.reshape(4 * QTR, D), w_up_rows, w_down, b_up_two, consts,
+        group_wide,
+    )
+    grad_mixed = grouped(grad_mixed)
+    d_all = attn_bwd(scal, triple, grad_attended, lse, pack)
+    d_near, d_far = split_chips(jnp.dot(d_all, w_wide, preferred_element_type=F32).astype(BF16))
+    dh1_near, dh1_far = d_near, d_far
     grad_hidden_one = grouped(group_scatter(dh1_near, dh1_far))
 
     def reduce_pair(mine, other):
-        both = plane_scatter(jnp.concatenate([mine, other], axis=2), rank)
-        width = mine.shape[2]
-        total = both[:, :width] + swap(both[:, width:].astype(BF16), "p").astype(F32)
+        both = plane_scatter(jnp.stack([mine, other], axis=1), rank)
+        total = both[0] + swap(both[1].astype(BF16), "p").astype(F32)
         return plane_gather(total.astype(BF16), rank).astype(F32)
 
-    down_low = grad_w_down.astype(BF16).reshape(2, 4, GW // 2, D)
-    out_w_down = reduce_pair(down_low[0], down_low[1]).reshape(2 * GW, D)
-    up_low = grad_w_up.astype(BF16).reshape(4, D // 4, 4 * GW)
-    out_w_up = reduce_pair(up_low[:, :, : 2 * GW], up_low[:, :, 2 * GW :]).reshape(D, 2 * GW)
-    wo_near = tn(o_mine, dy).astype(BF16)
-    wo_far = swap(tn(o_in, dy).astype(BF16), "q").astype(F32)
-    wo_low = (wo_near.astype(F32) + wo_far).astype(BF16).reshape(2, 4, HD // 2, D)
-    out_w_out = reduce_pair(wo_low[0], wo_low[1]).reshape(2 * HD, D)
-    wide_low = (tn(h1_near, d_near) + tn(h1_far, d_far)).astype(BF16)
-    narrow = [
-        nt(wide_low[:, k * 6 * LANES : (k + 1) * 6 * LANES], spread)
-        .astype(BF16)
-        .reshape(4, D // 4, 6 * HD)
+    down_low = down_low.reshape(2, 4, QTR, D)
+    up_low = up_low.reshape(2, 4, QTR, D)
+    out_w_down = reduce_pair(down_low[0], down_low[1]).reshape(WROWS, D)
+    out_w_up = jnp.transpose(reduce_pair(up_low[0], up_low[1]).reshape(WROWS, D))
+    wide_low = tn(d_all, hidden_one).astype(BF16)
+    a_low = [
+        jnp.concatenate(
+            [
+                tn(spread, wide_low[k * 6 * LANES : (k + 1) * 6 * LANES]).astype(BF16),
+                wo_low[k * 2 * HD : (k + 1) * 2 * HD],
+            ]
+        ).reshape(4, QTR, D)
         for k in range(2)
     ]
-    out_w_qkv = reduce_pair(narrow[0], narrow[1]).reshape(D, 6 * HD)
+    out_a = reduce_pair(a_low[0], a_low[1]).reshape(WROWS, D)
+    out_w_qkv = jnp.transpose(out_a[:UNIT_ROWS])
+    out_w_out = out_a[UNIT_ROWS:]
 
     grad_tokens = flat(
         grad_mixed + norm_back(grad_hidden_one * (1.0 + scale_one), normed_one, inverse_one)
@@ -923,30 +1401,21 @@
             [jnp.where(first, mine, other), jnp.where(first, other, mine)], axis=1
         ).astype(dtype)
 
-    out_final = from_rows(flat(final.astype(BF16)), BF16)
+    out_final = from_rows(final.reshape(2, BLK, D), BF16)
     out_tokens = from_rows(grad_tokens, F32)
 
-    group_sums = [
-        jnp.sum(v, axis=2)
-        for v in (
-            grad_hidden_one,
-            grad_hidden_one * normed_one,
-            grad_gate_one,
-            grad_hidden_two,
-            grad_scale_two,
-            grad_final * route_keep * branch,
-        )
-    ]
+    group_sums = [jnp.sum(v, axis=2) for v in (grad_hidden_one, grad_hidden_one * normed_one)]
+    group_sums.append(sums_two[:22].reshape(2, BLK // 16, 4 * D))
     part_mod = jnp.einsum(
         "sgc,sgm->cm", hot, jnp.concatenate(group_sums, axis=-1), precision=highest
     )[:CROPS]
     part_mod = jnp.transpose(part_mod.reshape(CROPS, 8, 6 * D // 8), (1, 0, 2))
-    smalls = jnp.stack([part_b_out, part_b_down, part_route]).reshape(3, 8, D // 8)
+    smalls = smalls[:3].reshape(3, 8, D // 8)
     smalls = jnp.pad(jnp.transpose(smalls, (1, 0, 2)), ((0, 0), (0, 0), (0, 5 * D // 8)))
-    d_ones = jnp.sum(d_near, axis=0, dtype=F32) + jnp.sum(d_far, axis=0, dtype=F32)
+    d_ones = jnp.sum(d_all, axis=0, dtype=F32)
     d_ones = d_ones.reshape(2, 2, 3, LANES)[..., :HD]
     qv_sums = jnp.stack([d_ones[:, :, 0], d_ones[:, :, 2]], axis=2).reshape(2, 4 * HD)
-    bias_sums = jnp.concatenate([grad_b_up.reshape(2, 2 * GW), qv_sums], axis=1)
+    bias_sums = jnp.concatenate([b_up_sums[0].reshape(2, 2 * GW), qv_sums], axis=1)
     who = jnp.arange(8)[:, None]
     bias_rows = jnp.where(
         who == shard, bias_sums[0], jnp.where(who == partner, bias_sums[1], 0.0)
@@ -958,7 +1427,6 @@
     line_sum = jnp.sum(parcels.reshape(2, 4, 16, 6 * D // 8), axis=1)
     line_low = line_sum.astype(BF16)
     mod_low = line_low[:, :CROPS]
-    act_all = plane_exchange(act_low, 3, "act_exchange")
     plane_low = plane_exchange(line_low, 4, "small_exchange")
     mod_all = plane_low[:, :, :CROPS]
     grad_ada_w = jnp.einsum(

time: 759 us -> 555 us (0.73)
  Pallas kernels: 138 us -> 318 us
  waiting for transfers between devices: 163 us -> 61.6 us
  local copies, waits for them, and re-layouts: 138 us -> 48.3 us
  matrix products: 102 us -> 26.7 us
  other arithmetic: 120 us -> 55 us
  starting transfers between devices: 88.3 us -> 33.3 us
    pallas_call x2 -> x4, Pallas kernels: 30.9 us -> 280 us  [the longest x1 171 us: middle(): pl.pallas_call(middle_kernel, out_shape=(shape_of(2 * BLK, D), shape_of(2...]
    ppermute x86 -> x32, waiting for transfers between devices: 163 us -> 61.6 us  [swap(): return lax.ppermute(values, axis, SWAP)]
    dot_general x23 -> x2, matrix products: 70.9 us -> 9.22 us  [the longest x1 8.9 us: layer_device(): jnp.dot(d_all, w_wide, preferred_element_type=F32).astype(BF16)]
    pallas_call x3 -> x2, Pallas kernels: 89.3 us -> 30.1 us  [line_exchange(): pl.pallas_call(lambda *refs: line_kernel(pick, *refs), out_shape=jax.Shap...]
    ppermute x86 -> x32, starting transfers between devices: 88.3 us -> 33.3 us  [swap(): return lax.ppermute(values, axis, SWAP)]
    unnamed x344 -> x121, local copies, waits for them, and re-layouts: 30.9 us -> 11.2 us
    dynamic_update_slice x22 -> x6, local copies, waits for them, and re-layouts: 21.2 us -> 5.09 us  [plane_gather(): out = lax.dynamic_update_index_in_dim(out, block, rank ^ k, 0)]
    dot_general x8 -> x3, matrix products: 24.7 us -> 10.3 us  [tn(): lax.dot_general(a, b, (((0,), (0,)), ((), ())), preferred_element_type=F32)]
  transfers between devices with their start and end apart: 86 -> 32, of which waited for: 30 -> 10; matrix products, arithmetic and copies ran while one was open for 40% -> 18% of each run, Pallas kernels for 15% -> 10%
where the time goes in v2:
time: 555 us; the launch traced here: 545 us
  Pallas kernels  318 us (57%)
  waiting for transfers between devices  61.6 us (11%)
  other arithmetic  55 us (10%)
  local copies, waits for them, and re-layouts  48.3 us (9%)
  starting transfers between devices  33.3 us (6%)
  matrix products  26.7 us (5%)
    pallas_call x1, Pallas kernels, middle(): pl.pallas_call(middle_kernel, out_shape=(shape_of(2 * BLK, D), shape_of(2...  171 us
    pallas_call x1, Pallas kernels, front(): pl.pallas_call(front_kernel, out_shape=(shape_of(SEQ, WIDE), shape_of(SEQ...  81.5 us
    ppermute x32, waiting for transfers between devices, swap(): return lax.ppermute(values, axis, SWAP)  61.6 us
    ppermute x32, starting transfers between devices, swap(): return lax.ppermute(values, axis, SWAP)  33.3 us
    pallas_call x2, Pallas kernels, line_exchange(): pl.pallas_call(lambda *refs: line_kernel(pick, *refs), out_shape=jax.Shap...  30.1 us
    pallas_call x1, Pallas kernels, attn_bwd(): pl.pallas_call(attn_bwd_kernel, out_shape=jax.ShapeDtypeStruct((SEQ, WIDE...  16.5 us
    unnamed x121, local copies, waits for them, and re-layouts  11.2 us
  transfers between devices with their start and end apart: 32, of which 10 were waited for; matrix products, arithmetic and copies ran while one was open for 18% of the time, Pallas kernels for 10%

profile of v2, /device:TPU:0, one launch (start us, length us, event | category | flops | bytes accessed | tf_op | source)
XLA Modules:
  0.0 544.9 jit_solution(18243794406070713056)
XLA Ops:
  7.6 2.3 copy.111
  16.7 81.5 %front.1 = (bf16[1408,1536]{1,0:T(8,128)(2,1)}, bf16[1408,1152]{1,0:T(8,128)(2,1)}, bf16[2,176,1152]{2,1,0:T(8,128)(2,1)}, bf16[2,176,128]{2,1,0:T(8,128)(2,1)},...) custom-call(f32[2,16,864]{2,1,0:T(8,128)} %fusion.9.part, ...), custom_call_target="tpu_custom_call" | custom-call | tf_op jit(solution)/shard_map/front/pallas_call | solution.py:814
  100.9 10.8 %attn_fwd.1 = (bf16[1408,288]{1,0:T(8,128)(2,1)S(1)}, f32[1408,128]{1,0:T(8,128)S(1)}) custom-call(s32[77]{0:T(128)S(1)} %pad_add_fusion.1.scal, bf16[1408,1536]{1,0:T(8,128)(2,1)} %get-tuple-element.34.buf, bf16[512,288]{1,0:T(8,128)(2,1)S(1)} %copy-done), custom_call_target="tpu_custom_call" | custom-call | tf_op jit(solution)/shard_map/attn_fwd/pallas_call | solution.py:434
  114.2 171.0 %middle.1 = (bf16[352,1152]{1,0:T(8,128)(2,1)}, f32[352,1152]{1,0:T(8,128)}, bf16[1408,288]{1,0:T(8,128)(2,1)}, f32[24,4608]{1,0:T(8,128)}, f32[8,1152]{1,0:T(8,...) custom-call(bf16[1408,288]{1,0:T(8,128)(2,1)} %copy-done.1, ...), custom_call_target="tpu_custom_call" | custom-call | tf_op jit(solution)/shard_map/middle/pallas_call | solution.py:1155
  285.2 3.0 fusion.122
  288.2 2.4 fusion.46
  291.6 1.7 collective-permute-start.23
  298.4 1.6 collective-permute-start.16
  300.9 1.4 collective-permute-start
  302.3 16.5 %attn_bwd.1 = bf16[1408,1536]{1,0:T(8,128)(2,1)} custom-call(s32[77]{0:T(128)S(1)} %pad_add_fusion.1.scal, bf16[1408,1536]{1,0:T(8,128)(2,1)} %get-tuple-element.34.buf, bf16[1408,288]{1,0:T(8,128)(2,1)S(1)} %copy-done.2, f32[1408,128]{1,0:T(8,128)S(1)} %copy-done.4, bf16[512,288]{1,0:T(8,128)(2,1)S(1)} %copy-done), custom_call_target="tpu_custom_call" | custom-call | tf_op jit(solution)/shard_map/attn_bwd/pallas_call | solution.py:448
  318.8 8.1 %convolution_convert_fusion = bf16[1536,1152]{1,0:T(8,128)(2,1)S(1)} fusion(bf16[1408,1536]{1,0:T(8,128)(2,1)} %attn_bwd.1, bf16[1408,1152]{1,0:T(8,128)(2,1)S(1)} %copy-done.57), kind=kOutput, calls=%fused_computation.2 | convolution fusion | flops 4984602624 | bytes 11108352 | tf_op jit(solution)/shard_map/dot_general | solution.py:361
  333.3 3.1 convert_reduce_fusion
  337.9 8.9 %convolution_convert_fusion.1 = bf16[1408,1152]{1,0:T(8,128)(2,1)} fusion(bf16[1408,1536]{1,0:T(8,128)(2,1)} %attn_bwd.1, bf16[1536,1152]{1,0:T(8,128)(2,1)S(1)} %copy-done.56), kind=kOutput, calls=%fused_computation.3 | convolution fusion | flops 4984455168 | bytes 11108352 | tf_op jit(solution)/shard_map/dot_general | solution.py:1366
  348.6 1.9 reshape.417
  353.4 1.5 dynamic-slice_bitcast_fusion.1
  356.6 3.1 collective-permute-start.5
  360.9 1.5 copy.88
  366.8 7.0 %collective-permute-done.7 = bf16[2,2,64,1152]{3,2,1,0:T(8,128)(2,1)S(1)} collective-permute-done((bf16[2,2,64,1152]{3,2,1,0:T(8,128)(2,1)S(1)}, bf16[2,2,64,1152]{3,2,1,0:T(8,128)(2,1)S(1)}, u32[]{:S(2)}, u32[]{:S(2)}) %collective-permute-start.7) | collective-permute-done | bytes 589856 | tf_op jit(solution)/shard_map/ppermute | solution.py:1202
  376.5 1.8 collective-permute-start.17
  382.4 2.4 collective-permute-done.26
  385.2 5.9 %collective-permute-done.17 = bf16[2,64,1152]{2,1,0:T(8,128)(2,1)S(1)} collective-permute-done((bf16[2,64,1152]{2,1,0:T(8,128)(2,1)S(1)}, bf16[2,64,1152]{2,1,0:T(8,128)(2,1)S(1)}, u32[]{:S(2)}, u32[]{:S(2)}) %collective-permute-start.17) | collective-permute-done | bytes 294944 | tf_op jit(solution)/shard_map/ppermute | solution.py:1202
  391.6 5.5 %collective-permute-done.8 = bf16[2,64,1152]{2,1,0:T(8,128)(2,1)S(1)} collective-permute-done((bf16[2,64,1152]{2,1,0:T(8,128)(2,1)S(1)}, bf16[2,64,1152]{2,1,0:T(8,128)(2,1)S(1)}, u32[]{:S(2)}, u32[]{:S(2)}) %collective-permute-start.8) | collective-permute-done | bytes 294944 | tf_op jit(solution)/shard_map/ppermute | solution.py:1202
  397.0 2.6 collective-permute-start.3
  400.5 2.6 collective-permute-start.18
  403.2 4.1 collective-permute-done.6
  408.6 16.7 %collective-permute-done.27 = bf16[144,1152]{1,0:T(8,128)(2,1)S(1)} collective-permute-done((bf16[144,1152]{1,0:T(8,128)(2,1)S(1)}, bf16[144,1152]{1,0:T(8,128)(2,1)S(1)}, u32[]{:S(2)}, u32[]{:S(2)}) %collective-permute-start.27) | collective-permute-done | bytes 331808 | tf_op jit(solution)/shard_map/ppermute | solution.py:1202
  426.6 13.5 %collective-permute-done.18 = bf16[144,1152]{1,0:T(8,128)(2,1)S(1)} collective-permute-done((bf16[144,1152]{1,0:T(8,128)(2,1)S(1)}, bf16[144,1152]{1,0:T(8,128)(2,1)S(1)}, u32[]{:S(2)}, u32[]{:S(2)}) %collective-permute-start.18) | collective-permute-done | bytes 331808 | tf_op jit(solution)/shard_map/ppermute | solution.py:1202
  441.4 4.3 collective-permute-done.9
  446.9 1.7 collective-permute-start.20
  450.5 1.9 fusion.117
  453.3 1.6 fusion.83.refs_0_
  454.9 13.7 %dmod_exchange.1 = f32[8,16,864]{2,1,0:T(8,128)} custom-call(f32[8,16,864]{2,1,0:T(8,128)} %fusion.83.refs_0_), custom_call_target="tpu_custom_call" | custom-call | tf_op jit(solution)/shard_map/dmod_exchange/pallas_call | solution.py:500
  468.7 1.8 bitcast_reduce_fusion.src
  470.5 8.1 %small_exchange.1 = bf16[4,2,16,864]{3,2,1,0:T(8,128)(2,1)} custom-call(bf16[2,16,864]{2,1,0:T(8,128)(2,1)} %bitcast_reduce_fusion.src), custom_call_target="tpu_custom_call" | custom-call | tf_op jit(solution)/shard_map/small_exchange/pallas_call | solution.py:543
  478.6 2.7 convolution_convert_fusion.4
  482.8 2.9 multiply_add_fusion
  487.0 2.7 convolution_bitcast_fusion.1
  490.3 16.4 %cond_exchange.1 = bf16[8,2,16,1152]{3,2,1,0:T(8,128)(2,1)} custom-call(bf16[2,16,1152]{2,1,0:T(8,128)(2,1)} %pad.45.refs_0_), custom_call_target="tpu_custom_call" | custom-call | tf_op jit(solution)/shard_map/cond_exchange/pallas_call | solution.py:500
  513.8 1.4 collective-permute-start.11
  517.2 2.8 collective-permute-start.4
  524.6 1.5 collective-permute-start.31
  529.8 1.5 collective-permute-start.22
  532.9 1.5 collective-permute-start.13
  534.4 1.8 bitcast_convert_fusion
  536.2 1.9 collective-permute-done.13
  538.4 1.4 slice.438
  539.8 1.8 convert_bitcast_fusion
  542.7 2.0 copy.89
  (329 shorter events, 84.9 us)
Async XLA Ops:
  0.6 9.2 %copy-start.55 = (s32[176,2]{0,1:T(2,128)S(1)}, s32[176,2]{0,1:T(2,128)}, u32[]{:S(2)}) copy-start(s32[176,2]{0,1:T(2,128)} %param.29) | copy-start | bytes 4228
  16.7 82.4 %copy-start.33 = (bf16[176,2,1152]{2,1,0:T(2,128)(2,1)S(1)}, bf16[176,2,1152]{2,1,0:T(2,128)(2,1)}, u32[]{:S(2)}) copy-start(bf16[176,2,1152]{2,1,0:T(2,128)(2,1)} %param.41) | copy-start | bytes 2433028
  291.6 83.3 %collective-permute-start.23 = (bf16[2,2,80,1152]{3,2,1,0:T(8,128)(2,1)}, bf16[2,2,80,1152]{3,2,1,0:T(8,128)(2,1)}, u32[]{:S(2)}, u32[]{:S(2)}) collective-permute-start(bf16[2,2,80,1152]{3,2,1,0:T(8,128)(2,1)} %pad_maximum_fusion.7), channel_id=1, source_target_pairs={{0,8},{8,0},{1,9},{9,1},{2,10},{10,2},{3,11},{11,3},{4,12},{12,4},... | collective-permute-start | bytes 2211848 | tf_op jit(solution)/shard_map/ppermute | solution.py:1202
  294.3 68.1 %collective-permute-start.25 = (bf16[2,2,64,1152]{3,2,1,0:T(8,128)(2,1)}, bf16[2,2,64,1152]{3,2,1,0:T(8,128)(2,1)}, u32[]{:S(2)}, u32[]{:S(2)}) collective-permute-start(bf16[2,2,64,1152]{3,2,1,0:T(8,128)(2,1)} %pad_maximum_fusion.13), channel_id=1, source_target_pairs={{0,16},{16,0},{1,17},{17,1},{2,18},{18,2},{3,19},{19,3},{4,20},{20... | collective-permute-start | bytes 1769480 | tf_op jit(solution)/shard_map/ppermute | solution.py:1202
  297.2 79.4 %collective-permute-start.14 = (bf16[2,2,80,1152]{3,2,1,0:T(8,128)(2,1)}, bf16[2,2,80,1152]{3,2,1,0:T(8,128)(2,1)}, u32[]{:S(2)}, u32[]{:S(2)}) collective-permute-start(bf16[2,2,80,1152]{3,2,1,0:T(8,128)(2,1)} %pad_maximum_fusion.6), channel_id=1, source_target_pairs={{0,8},{8,0},{1,9},{9,1},{2,10},{10,2},{3,11},{11,3},{4,12},{12,4},... | collective-permute-start | bytes 2211848 | tf_op jit(solution)/shard_map/ppermute | solution.py:1202
  298.4 66.1 %collective-permute-start.16 = (bf16[2,2,64,1152]{3,2,1,0:T(8,128)(2,1)}, bf16[2,2,64,1152]{3,2,1,0:T(8,128)(2,1)}, u32[]{:S(2)}, u32[]{:S(2)}) collective-permute-start(bf16[2,2,64,1152]{3,2,1,0:T(8,128)(2,1)} %pad_maximum_fusion.12), channel_id=1, source_target_pairs={{0,16},{16,0},{1,17},{17,1},{2,18},{18,2},{3,19},{19,3},{4,20},{20... | collective-permute-start | bytes 1769480 | tf_op jit(solution)/shard_map/ppermute | solution.py:1202
  300.9 55.7 %collective-permute-start = (bf16[176,1152]{1,0:T(8,128)(2,1)}, bf16[176,1152]{1,0:T(8,128)(2,1)}, u32[]{:S(2)}, u32[]{:S(2)}) collective-permute-start(bf16[176,1152]{1,0:T(8,128)(2,1)} %broadcast_select_fusion), channel_id=1, source_target_pairs={{0,4},{4,0},{1,5},{5,1},{2,6},{6,2},{3,7},{7,3},{8,12},{12,8},{9,1... | collective-permute-start | bytes 1216520 | tf_op jit(solution)/shard_map/ppermute | solution.py:1202
  302.3 16.5 %copy-start.57 = (bf16[1408,1152]{1,0:T(8,128)(2,1)S(1)}, bf16[1408,1152]{1,0:T(8,128)(2,1)}, u32[]{:S(2)}) copy-start(bf16[1408,1152]{1,0:T(8,128)(2,1)} %get-tuple-element.50) | copy-start | bytes 9732100
  318.8 8.2 %copy-start.34 = (bf16[768,432]{1,0:T(8,128)(2,1)S(1)}, bf16[768,432]{1,0:T(8,128)(2,1)}, u32[]{:S(2)}) copy-start(bf16[768,432]{1,0:T(8,128)(2,1)} %constant.256.clone.spread) | copy-start | bytes 1990660
  330.6 6.6 %copy-start.23 = (bf16[2,144,1152]{2,1,0:T(8,128)(2,1)}, bf16[2,144,1152]{2,1,0:T(8,128)(2,1)S(1)}, u32[]{:S(2)}) copy-start(bf16[2,144,1152]{2,1,0:T(8,128)(2,1)S(1)} %get-tuple-element.129) | copy-start | bytes 1990660
  337.9 9.0 %copy-start.14 = (f32[24,6912]{1,0:T(8,128)S(1)}, f32[24,6912]{1,0:T(8,128)}, u32[]{:S(2)}) copy-start(f32[24,6912]{1,0:T(8,128)} %get-tuple-element.38.modg) | copy-start | bytes 1990660
  346.9 6.3 %copy-start.47 = (f32[2,176]{1,0:T(2,128)}, f32[2,176]{1,0:T(2,128)S(1)}, u32[]{:S(2)}) copy-start(f32[2,176]{1,0:T(2,128)S(1)} %add_rsqrt_fusion) | copy-start | bytes 4228
  356.6 92.4 %copy-start.28 = (f32[2,11,1152]{2,1,0:T(8,128)}, f32[2,11,1152]{2,1,0:T(8,128)S(1)}, u32[]{:S(2)}) copy-start(f32[2,11,1152]{2,1,0:T(8,128)S(1)} %slice_add_fusion) | copy-start | bytes 304132
  356.6 23.1 %collective-permute-start.5 = (bf16[2,2,80,1152]{3,2,1,0:T(8,128)(2,1)S(1)}, bf16[2,2,80,1152]{3,2,1,0:T(8,128)(2,1)S(1)}, u32[]{:S(2)}, u32[]{:S(2)}) collective-permute-start(bf16[2,2,80,1152]{3,2,1,0:T(8,128)(2,1)S(1)} %pad_maximum_fusion.5), channel_id=1, source_target_pairs={{0,8},{8,0},{1,9},{9,1},{2,10},{10,2},{3,11},{11,3},{4,12},{12,4},... | collective-permute-start | bytes 2211848 | tf_op jit(solution)/shard_map/ppermute | solution.py:1202
  362.4 11.4 %collective-permute-start.7 = (bf16[2,2,64,1152]{3,2,1,0:T(8,128)(2,1)S(1)}, bf16[2,2,64,1152]{3,2,1,0:T(8,128)(2,1)S(1)}, u32[]{:S(2)}, u32[]{:S(2)}) collective-permute-start(bf16[2,2,64,1152]{3,2,1,0:T(8,128)(2,1)S(1)} %pad_maximum_fusion.11), channel_id=1, source_target_pairs={{0,16},{16,0},{1,17},{17,1},{2,18},{18,2},{3,19},{19,3},{4,20},{20... | collective-permute-start | bytes 1769480 | tf_op jit(solution)/shard_map/ppermute | solution.py:1202
  364.6 16.4 %collective-permute-start.2 = (bf16[2,176,1152]{2,1,0:T(8,128)(2,1)S(1)}, bf16[2,176,1152]{2,1,0:T(8,128)(2,1)S(1)}, u32[]{:S(2)}, u32[]{:S(2)}) collective-permute-start(bf16[2,176,1152]{2,1,0:T(8,128)(2,1)S(1)} %get-tuple-element.113), channel_id=1, source_target_pairs={{0,1},{1,0},{2,3},{3,2},{4,5},{5,4},{6,7},{7,6},{8,9},{9,8},{10,11... | collective-permute-start | bytes 2433032 | tf_op jit(solution)/shard_map/ppermute | solution.py:1202
  373.8 73.1 %collective-permute-start.1 = (bf16[2,176,1152]{2,1,0:T(8,128)(2,1)S(1)}, bf16[2,176,1152]{2,1,0:T(8,128)(2,1)S(1)}, u32[]{:S(2)}, u32[]{:S(2)}) collective-permute-start(bf16[2,176,1152]{2,1,0:T(8,128)(2,1)S(1)} %get-tuple-element.112), channel_id=1, source_target_pairs={{0,1},{1,0},{2,3},{3,2},{4,5},{5,4},{6,7},{7,6},{8,9},{9,8},{10,11... | collective-permute-start | bytes 2433032 | tf_op jit(solution)/shard_map/ppermute | solution.py:1202
  374.9 9.9 %collective-permute-start.26 = (bf16[2,64,1152]{2,1,0:T(8,128)(2,1)S(1)}, bf16[2,64,1152]{2,1,0:T(8,128)(2,1)S(1)}, u32[]{:S(2)}, u32[]{:S(2)}) collective-permute-start(bf16[2,64,1152]{2,1,0:T(8,128)(2,1)S(1)} %fusion.71), channel_id=1, source_target_pairs={{0,8},{8,0},{1,9},{9,1},{2,10},{10,2},{3,11},{11,3},{4,12},{12,4},... | collective-permute-start | bytes 884744 | tf_op jit(solution)/shard_map/ppermute | solution.py:1202
  376.5 14.6 %collective-permute-start.17 = (bf16[2,64,1152]{2,1,0:T(8,128)(2,1)S(1)}, bf16[2,64,1152]{2,1,0:T(8,128)(2,1)S(1)}, u32[]{:S(2)}, u32[]{:S(2)}) collective-permute-start(bf16[2,64,1152]{2,1,0:T(8,128)(2,1)S(1)} %fusion.75), channel_id=1, source_target_pairs={{0,8},{8,0},{1,9},{9,1},{2,10},{10,2},{3,11},{11,3},{4,12},{12,4},... | collective-permute-start | bytes 884744 | tf_op jit(solution)/shard_map/ppermute | solution.py:1202
  379.6 17.4 %collective-permute-start.8 = (bf16[2,64,1152]{2,1,0:T(8,128)(2,1)S(1)}, bf16[2,64,1152]{2,1,0:T(8,128)(2,1)S(1)}, u32[]{:S(2)}, u32[]{:S(2)}) collective-permute-start(bf16[2,64,1152]{2,1,0:T(8,128)(2,1)S(1)} %fusion.79), channel_id=1, source_target_pairs={{0,8},{8,0},{1,9},{9,1},{2,10},{10,2},{3,11},{11,3},{4,12},{12,4},... | collective-permute-start | bytes 884744 | tf_op jit(solution)/shard_map/ppermute | solution.py:1202
  380.9 10.5 %copy-start.16 = (bf16[2,144,1152]{2,1,0:T(8,128)(2,1)S(1)}, bf16[2,144,1152]{2,1,0:T(8,128)(2,1)}, u32[]{:S(2)}) copy-start(bf16[2,144,1152]{2,1,0:T(8,128)(2,1)} %get-tuple-element.120) | copy-start | bytes 1990660
  380.9 18.8 %collective-permute-start.24 = (bf16[2,80,1152]{2,1,0:T(8,128)(2,1)S(1)}, bf16[2,80,1152]{2,1,0:T(8,128)(2,1)S(1)}, u32[]{:S(2)}, u32[]{:S(2)}) collective-permute-start(bf16[2,80,1152]{2,1,0:T(8,128)(2,1)S(1)} %fusion.20), channel_id=1, source_target_pairs={{0,16},{16,0},{1,17},{17,1},{2,18},{18,2},{3,19},{19,3},{4,20},{20... | collective-permute-start | bytes 1105928 | tf_op jit(solution)/shard_map/ppermute | solution.py:1202
  384.8 15.6 %collective-permute-start.15 = (bf16[2,80,1152]{2,1,0:T(8,128)(2,1)S(1)}, bf16[2,80,1152]{2,1,0:T(8,128)(2,1)S(1)}, u32[]{:S(2)}, u32[]{:S(2)}) collective-permute-start(bf16[2,80,1152]{2,1,0:T(8,128)(2,1)S(1)} %fusion.24), channel_id=1, source_target_pairs={{0,16},{16,0},{1,17},{17,1},{2,18},{18,2},{3,19},{19,3},{4,20},{20... | collective-permute-start | bytes 1105928 | tf_op jit(solution)/shard_map/ppermute | solution.py:1202
  391.1 16.2 %collective-permute-start.6 = (bf16[2,80,1152]{2,1,0:T(8,128)(2,1)S(1)}, bf16[2,80,1152]{2,1,0:T(8,128)(2,1)S(1)}, u32[]{:S(2)}, u32[]{:S(2)}) collective-permute-start(bf16[2,80,1152]{2,1,0:T(8,128)(2,1)S(1)} %fusion.28), channel_id=1, source_target_pairs={{0,16},{16,0},{1,17},{17,1},{2,18},{18,2},{3,19},{19,3},{4,20},{20... | collective-permute-start | bytes 1105928 | tf_op jit(solution)/shard_map/ppermute | solution.py:1202
  397.0 51.6 %collective-permute-start.3 = (bf16[2,176,1152]{2,1,0:T(8,128)(2,1)S(1)}, bf16[2,176,1152]{2,1,0:T(8,128)(2,1)S(1)}, u32[]{:S(2)}, u32[]{:S(2)}) collective-permute-start(bf16[2,176,1152]{2,1,0:T(8,128)(2,1)S(1)} %fusion.7), channel_id=1, source_target_pairs={{0,2},{2,0},{1,3},{3,1},{4,6},{6,4},{5,7},{7,5},{8,10},{10,8},{9,1... | collective-permute-start | bytes 2433032 | tf_op jit(solution)/shard_map/ppermute | solution.py:1202
  399.9 25.3 %collective-permute-start.27 = (bf16[144,1152]{1,0:T(8,128)(2,1)S(1)}, bf16[144,1152]{1,0:T(8,128)(2,1)S(1)}, u32[]{:S(2)}, u32[]{:S(2)}) collective-permute-start(bf16[144,1152]{1,0:T(8,128)(2,1)S(1)} %fusion.87), channel_id=1, source_target_pairs={{0,4},{4,0},{1,5},{5,1},{2,6},{6,2},{3,7},{7,3},{8,12},{12,8},{9,1... | collective-permute-start | bytes 995336 | tf_op jit(solution)/shard_map/ppermute | solution.py:1202
  400.5 39.5 %collective-permute-start.18 = (bf16[144,1152]{1,0:T(8,128)(2,1)S(1)}, bf16[144,1152]{1,0:T(8,128)(2,1)S(1)}, u32[]{:S(2)}, u32[]{:S(2)}) collective-permute-start(bf16[144,1152]{1,0:T(8,128)(2,1)S(1)} %fusion.86), channel_id=1, source_target_pairs={{0,4},{4,0},{1,5},{5,1},{2,6},{6,2},{3,7},{7,3},{8,12},{12,8},{9,1... | collective-permute-start | bytes 995336 | tf_op jit(solution)/shard_map/ppermute | solution.py:1202
  407.4 38.2 %collective-permute-start.9 = (bf16[144,1152]{1,0:T(8,128)(2,1)S(1)}, bf16[144,1152]{1,0:T(8,128)(2,1)S(1)}, u32[]{:S(2)}, u32[]{:S(2)}) collective-permute-start(bf16[144,1152]{1,0:T(8,128)(2,1)S(1)} %fusion.85), channel_id=1, source_target_pairs={{0,4},{4,0},{1,5},{5,1},{2,6},{6,2},{3,7},{7,3},{8,12},{12,8},{9,1... | collective-permute-start | bytes 995336 | tf_op jit(solution)/shard_map/ppermute | solution.py:1202
  426.3 87.5 %collective-permute-start.28 = (bf16[144,1152]{1,0:T(8,128)(2,1)}, bf16[144,1152]{1,0:T(8,128)(2,1)}, u32[]{:S(2)}, u32[]{:S(2)}) collective-permute-start(bf16[144,1152]{1,0:T(8,128)(2,1)} %get-tuple-element.103), channel_id=1, source_target_pairs={{0,8},{8,0},{1,9},{9,1},{2,10},{10,2},{3,11},{11,3},{4,12},{12,4},... | collective-permute-start | bytes 995336 | tf_op jit(solution)/shard_map/ppermute | solution.py:1202
  440.1 77.1 %collective-permute-start.29 = (bf16[144,1152]{1,0:T(8,128)(2,1)}, bf16[144,1152]{1,0:T(8,128)(2,1)}, u32[]{:S(2)}, u32[]{:S(2)}) collective-permute-start(bf16[144,1152]{1,0:T(8,128)(2,1)} %get-tuple-element.103), channel_id=1, source_target_pairs={{0,16},{16,0},{1,17},{17,1},{2,18},{18,2},{3,19},{19,3},{4,20},{20... | collective-permute-start | bytes 995336 | tf_op jit(solution)/shard_map/ppermute | solution.py:1202
  445.7 76.3 %collective-permute-start.19 = (bf16[144,1152]{1,0:T(8,128)(2,1)}, bf16[144,1152]{1,0:T(8,128)(2,1)}, u32[]{:S(2)}, u32[]{:S(2)}) collective-permute-start(bf16[144,1152]{1,0:T(8,128)(2,1)} %get-tuple-element.105), channel_id=1, source_target_pairs={{0,8},{8,0},{1,9},{9,1},{2,10},{10,2},{3,11},{11,3},{4,12},{12,4},... | collective-permute-start | bytes 995336 | tf_op jit(solution)/shard_map/ppermute | solution.py:1202
  446.9 77.7 %collective-permute-start.20 = (bf16[144,1152]{1,0:T(8,128)(2,1)}, bf16[144,1152]{1,0:T(8,128)(2,1)}, u32[]{:S(2)}, u32[]{:S(2)}) collective-permute-start(bf16[144,1152]{1,0:T(8,128)(2,1)} %get-tuple-element.105), channel_id=1, source_target_pairs={{0,16},{16,0},{1,17},{17,1},{2,18},{18,2},{3,19},{19,3},{4,20},{20... | collective-permute-start | bytes 995336 | tf_op jit(solution)/shard_map/ppermute | solution.py:1202
  448.7 79.4 %collective-permute-start.10 = (bf16[144,1152]{1,0:T(8,128)(2,1)}, bf16[144,1152]{1,0:T(8,128)(2,1)}, u32[]{:S(2)}, u32[]{:S(2)}) collective-permute-start(bf16[144,1152]{1,0:T(8,128)(2,1)} %get-tuple-element.107), channel_id=1, source_target_pairs={{0,8},{8,0},{1,9},{9,1},{2,10},{10,2},{3,11},{11,3},{4,12},{12,4},... | collective-permute-start | bytes 995336 | tf_op jit(solution)/shard_map/ppermute | solution.py:1202
  468.7 13.9 %copy-start.51 = (f32[2,176]{1,0:T(2,128)S(1)}, f32[2,176]{1,0:T(2,128)}, u32[]{:S(2)}) copy-start(f32[2,176]{1,0:T(2,128)} %get-tuple-element.96) | copy-start | bytes 4228
  468.7 14.0 %copy-start.50 = (f32[2,176]{1,0:T(2,128)S(1)}, f32[2,176]{1,0:T(2,128)}, u32[]{:S(2)}) copy-start(f32[2,176]{1,0:T(2,128)} %get-tuple-element.97) | copy-start | bytes 4228
  468.7 14.1 %copy-start.29 = (f32[2,11,1152]{2,1,0:T(8,128)S(1)}, f32[2,11,1152]{2,1,0:T(8,128)}, u32[]{:S(2)}) copy-start(f32[2,11,1152]{2,1,0:T(8,128)} %copy-done.28) | copy-start | bytes 304132
  468.7 14.1 %copy-start.43 = (f32[2,11,16]{2,1,0:T(8,128)S(1)}, f32[2,11,16]{2,1,0:T(8,128)}, u32[]{:S(2)}) copy-start(f32[2,11,16]{2,1,0:T(8,128)} %div.50) | copy-start | bytes 4228
  468.7 14.1 %copy-start.45 = (f32[2,11,16]{2,1,0:T(8,128)S(1)}, f32[2,11,16]{2,1,0:T(8,128)}, u32[]{:S(2)}) copy-start(f32[2,11,16]{2,1,0:T(8,128)} %rsqrt.13) | copy-start | bytes 4228
  506.7 10.5 %copy-start.37 = (bf16[1,11,16,1152]{3,2,1,0:T(8,128)(2,1)S(1)}, bf16[1,11,16,1152]{3,2,1,0:T(8,128)(2,1)}, u32[]{:S(2)}) copy-start(bf16[1,11,16,1152]{3,2,1,0:T(8,128)(2,1)} %select_convert_fusion) | copy-start | bytes 1216516
  507.9 15.7 %copy-start.9 = (bf16[4,144,1152]{2,1,0:T(8,128)(2,1)S(1)}, bf16[4,144,1152]{2,1,0:T(8,128)(2,1)}, u32[]{:S(2)}) copy-start(bf16[4,144,1152]{2,1,0:T(8,128)(2,1)} %copy-done.8) | copy-start | bytes 3981316
  513.8 15.9 %collective-permute-start.11 = (bf16[144,1152]{1,0:T(8,128)(2,1)}, bf16[144,1152]{1,0:T(8,128)(2,1)S(1)}, u32[]{:S(2)}, u32[]{:S(2)}) collective-permute-start(bf16[144,1152]{1,0:T(8,128)(2,1)} %get-tuple-element.107), channel_id=1, source_target_pairs={{0,16},{16,0},{1,17},{17,1},{2,18},{18,2},{3,19},{19,3},{4,20},{20... | collective-permute-start | bytes 995336 | tf_op jit(solution)/shard_map/ppermute | solution.py:1202
  517.2 25.3 %collective-permute-start.4 = (bf16[176,1152]{1,0:T(8,128)(2,1)S(1)}, bf16[176,1152]{1,0:T(8,128)(2,1)S(1)}, u32[]{:S(2)}, u32[]{:S(2)}) collective-permute-start(bf16[176,1152]{1,0:T(8,128)(2,1)S(1)} %bitcast.336), channel_id=1, source_target_pairs={{0,4},{4,0},{1,5},{5,1},{2,6},{6,2},{3,7},{7,3},{8,12},{12,8},{9,1... | collective-permute-start | bytes 1216520 | tf_op jit(solution)/shard_map/ppermute | solution.py:1202
  522.0 10.9 %collective-permute-start.30 = (bf16[80,1152]{1,0:T(8,128)(2,1)S(1)}, bf16[80,1152]{1,0:T(8,128)(2,1)S(1)}, u32[]{:S(2)}, u32[]{:S(2)}) collective-permute-start(bf16[80,1152]{1,0:T(8,128)(2,1)S(1)} %slice.473), channel_id=1, source_target_pairs={{0,16},{16,0},{1,17},{17,1},{2,18},{18,2},{3,19},{19,3},{4,20},{20... | collective-permute-start | bytes 552968 | tf_op jit(solution)/shard_map/ppermute | solution.py:1202
  524.6 7.6 %collective-permute-start.31 = (bf16[64,1152]{1,0:T(8,128)(2,1)S(1)}, bf16[64,1152]{1,0:T(8,128)(2,1)S(1)}, u32[]{:S(2)}, u32[]{:S(2)}) collective-permute-start(bf16[64,1152]{1,0:T(8,128)(2,1)S(1)} %slice.474), channel_id=1, source_target_pairs={{0,8},{8,0},{1,9},{9,1},{2,10},{10,2},{3,11},{11,3},{4,12},{12,4},... | collective-permute-start | bytes 442376 | tf_op jit(solution)/shard_map/ppermute | solution.py:1202
  528.1 11.7 %collective-permute-start.21 = (bf16[80,1152]{1,0:T(8,128)(2,1)S(1)}, bf16[80,1152]{1,0:T(8,128)(2,1)S(1)}, u32[]{:S(2)}, u32[]{:S(2)}) collective-permute-start(bf16[80,1152]{1,0:T(8,128)(2,1)S(1)} %slice.456), channel_id=1, source_target_pairs={{0,16},{16,0},{1,17},{17,1},{2,18},{18,2},{3,19},{19,3},{4,20},{20... | collective-permute-start | bytes 552968 | tf_op jit(solution)/shard_map/ppermute | solution.py:1202
  529.8 10.0 %collective-permute-start.22 = (bf16[64,1152]{1,0:T(8,128)(2,1)S(1)}, bf16[64,1152]{1,0:T(8,128)(2,1)S(1)}, u32[]{:S(2)}, u32[]{:S(2)}) collective-permute-start(bf16[64,1152]{1,0:T(8,128)(2,1)S(1)} %slice.457), channel_id=1, source_target_pairs={{0,8},{8,0},{1,9},{9,1},{2,10},{10,2},{3,11},{11,3},{4,12},{12,4},... | collective-permute-start | bytes 442376 | tf_op jit(solution)/shard_map/ppermute | solution.py:1202
  532.3 5.9 %collective-permute-start.12 = (bf16[80,1152]{1,0:T(8,128)(2,1)S(1)}, bf16[80,1152]{1,0:T(8,128)(2,1)S(1)}, u32[]{:S(2)}, u32[]{:S(2)}) collective-permute-start(bf16[80,1152]{1,0:T(8,128)(2,1)S(1)} %slice.436), channel_id=1, source_target_pairs={{0,16},{16,0},{1,17},{17,1},{2,18},{18,2},{3,19},{19,3},{4,20},{20... | collective-permute-start | bytes 552968 | tf_op jit(solution)/shard_map/ppermute | solution.py:1202
  532.9 5.2 collective-permute-start.13
  (42 other events, 113.3 us)

commit v3 on v2

--- a/solution.py
+++ b/solution.py
@@ -455,111 +455,12 @@
     )(scal, triple, grads, lse, pack)
 
 
-def line_kernel(pick, src, out, send_sem, recv_sem, loc_sem):
-    p, q, c = lax.axis_index("p"), lax.axis_index("q"), lax.axis_index("c")
-    me = p * 4 + q * 2 + c
-    peers = []
-    for k in range(1, 8):
-        pp, qq, cc = lax.rem(p + k // 4, 2), lax.rem(q + (k // 2) % 2, 2), lax.rem(c + k % 2, 2)
-        peers.append((pp, qq, cc))
-    barrier = pltpu.get_barrier_semaphore()
-    for pp, qq, cc in peers:
-        pl.semaphore_signal(
-            barrier, inc=1, device_id={"p": pp, "q": qq, "c": cc}, device_id_type=MESH
-        )
-    pl.semaphore_wait(barrier, 7)
-
-    def source(pp, qq, cc):
-        if pick == "row":
-            return src.at[pp]
-        if pick == "all":
-            return src
-        return src.at[pp * 4 + qq * 2 + cc]
-
-    copies = []
-    for k, (pp, qq, cc) in enumerate(peers):
-        copy = pltpu.make_async_remote_copy(
-            src_ref=source(pp, qq, cc),
-            dst_ref=out.at[me],
-            send_sem=send_sem.at[k],
-            recv_sem=recv_sem.at[k],
-            device_id={"p": pp, "q": qq, "c": cc},
-            device_id_type=MESH,
-        )
-        copy.start()
-        copies.append(copy)
-    own = pltpu.make_async_copy(source(p, q, c), out.at[me], loc_sem)
-    own.start()
-    own.wait()
-    for copy in copies:
-        copy.wait()
-
-
-def line_exchange(src, pick, collective_id, name):
-    shape = src.shape if pick == "all" else src.shape[1:]
-    return pl.pallas_call(
-        lambda *refs: line_kernel(pick, *refs),
-        out_shape=jax.ShapeDtypeStruct((8,) + shape, src.dtype),
-        in_specs=[VMEM_SPEC],
-        out_specs=VMEM_SPEC,
-        scratch_shapes=[
-            pltpu.SemaphoreType.DMA((7,)),
-            pltpu.SemaphoreType.DMA((7,)),
-            pltpu.SemaphoreType.DMA,
-        ],
-        compiler_params=pltpu.CompilerParams(collective_id=collective_id, has_side_effects=True),
-        name=name,
-    )(src)
-
-
-def plane_kernel(src, out, send_sem, recv_sem, loc_sem):
-    y, x = lax.axis_index("y"), lax.axis_index("x")
-    me = y * 2 + x
-    peers = [(lax.rem(y + k // 2, 2), lax.rem(x + k % 2, 2)) for k in range(1, 4)]
-    barrier = pltpu.get_barrier_semaphore()
-    for yy, xx in peers:
-        pl.semaphore_signal(barrier, inc=1, device_id={"y": yy, "x": xx}, device_id_type=MESH)
-    pl.semaphore_wait(barrier, 3)
-    copies = []
-    for k, (yy, xx) in enumerate(peers):
-        copy = pltpu.make_async_remote_copy(
-            src_ref=src,
-            dst_ref=out.at[me],
-            send_sem=send_sem.at[k],
-            recv_sem=recv_sem.at[k],
-            device_id={"y": yy, "x": xx},
-            device_id_type=MESH,
-        )
-        copy.start()
-        copies.append(copy)
-    own = pltpu.make_async_copy(src, out.at[me], loc_sem)
-    own.start()
-    own.wait()
-    for copy in copies:
-        copy.wait()
-
-
-def plane_exchange(src, collective_id, name):
-    return pl.pallas_call(
-        plane_kernel,
-        out_shape=jax.ShapeDtypeStruct((4,) + src.shape, src.dtype),
-        in_specs=[VMEM_SPEC],
-        out_specs=VMEM_SPEC,
-        scratch_shapes=[
-            pltpu.SemaphoreType.DMA((3,)),
-            pltpu.SemaphoreType.DMA((3,)),
-            pltpu.SemaphoreType.DMA,
-        ],
-        compiler_params=pltpu.CompilerParams(collective_id=collective_id, has_side_effects=True),
-        name=name,
-    )(src)
-
-
 QTR = 144
 WROWS = 576
 BIAS = 1408
 GROUPS = 24
 UNIT_ROWS = 6 * HD
+MODS = 6 * D // 8
 CUT = 80
 
 
@@ -1198,39 +1099,385 @@
     )(o, x2, k2, modg, g_pair, wo, w_up, w_down, bias, consts, gmask)
 
 
-def swap(values, axis):
-    return lax.ppermute(values, axis, SWAP)
-
-
-def at_index(stacked, index):
-    return lax.dynamic_index_in_dim(stacked, index, 0, keepdims=False)
-
-
-def plane_gather(part, rank):
-    half = 80
-    by_x = swap(part, "x")
-    by_y = swap(part, "y")
-    far = jnp.concatenate([swap(by_x[:half], "y"), swap(by_y[half:], "x")], axis=0)
-    out = jnp.zeros((4,) + part.shape, part.dtype)
-    for k, block in enumerate((part, by_x, by_y, far)):
-        out = lax.dynamic_update_index_in_dim(out, block, rank ^ k, 0)
-    return out
-
-
-def plane_scatter(parts, rank):
-    half = 80
-    rel = [at_index(parts, rank ^ k) for k in range(4)]
-    low = [v[:, :half] for v in rel]
-    high = [v[:, half:] for v in rel]
-    in_x = swap(jnp.stack([low[1], low[3]]), "x").astype(F32)
-    in_y = swap(jnp.stack([high[2], high[3]]), "y").astype(F32)
-    low_own = low[0].astype(F32) + in_x[0]
-    high_own = high[0].astype(F32) + in_y[0]
-    low_rest = (low[2].astype(F32) + in_x[1]).astype(BF16)
-    high_rest = (high[1].astype(F32) + in_y[1]).astype(BF16)
-    low_own = low_own + swap(low_rest, "y").astype(F32)
-    high_own = high_own + swap(high_rest, "x").astype(F32)
-    return jnp.concatenate([low_own, high_own], axis=1)
+class PlaneReduce:
+    def __init__(self, grads, bufs, sems, k, y, x):
+        self.grads, self.y, self.x = grads, y, x
+        self.low_in, self.high_in, self.low_out, self.high_out, self.low_end, self.high_end = bufs
+        self.first = [
+            remote(grads.at[:, self.low(y, 1 - x)], self.low_in.at[0], sems, k, x=1 - x),
+            remote(grads.at[:, self.low(1 - y, 1 - x)], self.low_in.at[1], sems, k + 1, x=1 - x),
+            remote(grads.at[:, self.high(1 - y, x)], self.high_in.at[0], sems, k + 2, y=1 - y),
+            remote(grads.at[:, self.high(1 - y, 1 - x)], self.high_in.at[1], sems, k + 3, y=1 - y),
+        ]
+        self.second = [
+            remote(self.low_out, self.low_end, sems, k + 4, y=1 - y),
+            remote(self.high_out, self.high_end, sems, k + 5, x=1 - x),
+        ]
+
+    def low(self, y, x):
+        return rows_at((y * 2 + x) * QTR, CUT)
+
+    def high(self, y, x):
+        return rows_at((y * 2 + x) * QTR + CUT, QTR - CUT)
+
+    def start(self):
+        for copy in self.first:
+            copy.start()
+
+    def middle(self):
+        y, x = self.y, self.x
+        for copy in self.first:
+            copy.wait_recv()
+        for shard in range(2):
+            self.low_out[shard] = (
+                self.grads[shard, self.low(1 - y, x), :].astype(F32)
+                + self.low_in[1, shard].astype(F32)
+            ).astype(BF16)
+            self.high_out[shard] = (
+                self.grads[shard, self.high(y, 1 - x), :].astype(F32)
+                + self.high_in[1, shard].astype(F32)
+            ).astype(BF16)
+        for copy in self.second:
+            copy.start()
+
+    def arrive(self):
+        for copy in self.second:
+            copy.wait_recv()
+
+    def total(self, shard):
+        low = (
+            self.grads[shard, self.low(self.y, self.x), :].astype(F32)
+            + self.low_in[0, shard].astype(F32)
+            + self.low_end[shard].astype(F32)
+        )
+        high = (
+            self.grads[shard, self.high(self.y, self.x), :].astype(F32)
+            + self.high_in[0, shard].astype(F32)
+            + self.high_end[shard].astype(F32)
+        )
+        return low, high
+
+    def sent(self):
+        for copy in self.first + self.second:
+            copy.wait_send()
+
+
+REDUCE_SCRATCH = [
+    pltpu.VMEM((2, 2, CUT, D), BF16),
+    pltpu.VMEM((2, 2, QTR - CUT, D), BF16),
+    pltpu.VMEM((2, CUT, D), BF16),
+    pltpu.VMEM((2, QTR - CUT, D), BF16),
+    pltpu.VMEM((2, CUT, D), BF16),
+    pltpu.VMEM((2, QTR - CUT, D), BF16),
+]
+
+
+class LineReduce:
+    def __init__(self, reduce, half, out, sems, k, y, x, p):
+        self.reduce, self.half, self.out = reduce, half, out
+        self.mine = rows_at((y * 2 + x) * QTR, QTR)
+        self.over = remote(half.at[0], half.at[1], sems, k, p=1 - p)
+        mine = out.at[self.mine]
+        self.to_x = remote(mine, mine, sems, k + 1, x=1 - x)
+        self.to_y = remote(mine, mine, sems, k + 2, y=1 - y)
+        from_x = out.at[rows_at((y * 2 + 1 - x) * QTR, CUT)]
+        from_y = out.at[rows_at(((1 - y) * 2 + x) * QTR + CUT, QTR - CUT)]
+        self.on_y = remote(from_x, from_x, sems, k + 3, y=1 - y)
+        self.on_x = remote(from_y, from_y, sems, k + 4, x=1 - x)
+
+    def start(self):
+        self.reduce.arrive()
+        low, high = self.reduce.total(1)
+        self.half[0, :CUT] = low.astype(BF16)
+        self.half[0, CUT:] = high.astype(BF16)
+        self.over.start()
+
+    def spread(self):
+        low, high = self.reduce.total(0)
+        self.over.wait_recv()
+        start = (self.reduce.y * 2 + self.reduce.x) * QTR
+        self.out[rows_at(start, CUT), :] = (low + self.half[1, :CUT].astype(F32)).astype(BF16)
+        self.out[rows_at(start + CUT, QTR - CUT), :] = (
+            high + self.half[1, CUT:].astype(F32)
+        ).astype(BF16)
+        self.to_x.start()
+        self.to_y.start()
+
+    def forward(self):
+        self.to_x.wait_recv()
+        self.on_y.start()
+        self.to_y.wait_recv()
+        self.on_x.start()
+
+    def finish(self):
+        self.on_y.wait_recv()
+        self.on_x.wait_recv()
+
+    def sent(self):
+        for copy in (self.over, self.to_x, self.to_y, self.on_y, self.on_x):
+            copy.wait_send()
+
+
+def back_kernel(
+    d, h1, wide, x2, dx, scale, sums_two, smalls, b_up, up_g, down_g, wo_g, hot, spread, final,
+    ada, slope,
+    final_out, tokens_out, a_out, up_out, down_out, mod_out, cond_out,
+    own, csend, crecv, qsend, qrecv, wideg, grads, sums, parcel, parcels, modline, condbuf,
+    tsend, halves, *rest,
+):
+    bufs = [rest[0:6], rest[6:12], rest[12:18]]
+    send, recv, loc = rest[18:]
+    y, x, p, q, c = (lax.axis_index(name) for name in "yxpqc")
+    sems = (send, recv)
+    line = line_peers(p, q, c)
+    plane = [{"y": lax.rem(y + k // 2, 2), "x": lax.rem(x + k % 2, 2)} for k in range(1, 4)]
+    greet(line + plane)
+    rank = y * 2 + x
+    me = p * 4 + q * 2 + c
+
+    def keep_local(src, dst, k):
+        copy = pltpu.make_async_copy(src, dst, loc.at[k])
+        copy.start()
+        return copy
+
+    def place(slot, chip, core):
+        return slot * HALF + chip * (2 * BLK) + core * BLK
+
+    outs = (down_out, up_out, a_out)
+    reduces = [PlaneReduce(grads.at[k], bufs[k], sems, 6 * k, y, x) for k in range(3)]
+    lines = [
+        LineReduce(reduces[k], halves.at[k], outs[k], sems, 18 + 5 * k, y, x, p) for k in range(3)
+    ]
+    loads = [keep_local(down_g, grads.at[0], 0), keep_local(up_g, grads.at[1], 1)]
+    for k in range(2):
+        loads[k].wait()
+        reduces[k].start()
+    final_copy = remote(
+        final.at[pl.ds(pl.multiple_of((1 - p) * BLK, 16), BLK)], final_out.at[p], sems, 33, p=1 - p
+    )
+    own_final = keep_local(
+        final.at[pl.ds(pl.multiple_of(p * BLK, 16), BLK)], final_out.at[p], 2
+    )
+
+    def core_copy(side, slot):
+        return remote(
+            csend.at[side, slot], crecv.at[side, slot], sems, 34 + side * 2 + slot, c=1 - c
+        )
+
+    def chip_copy(slot):
+        return remote(qsend.at[slot], qrecv.at[slot], sems, 38 + slot, q=1 - q)
+
+    def far_out(slot):
+        core_copy(1, slot).wait_recv()
+        qsend[slot] = (own[1, slot] + crecv[1, slot].astype(F32)).astype(BF16)
+        chip_copy(slot).start()
+
+    def through(step, carry):
+        side, slot = 1 - step // 2, lax.rem(step, 2)
+        start = place(slot, lax.rem(q + side, 2), 0)
+        rows = rows_at(start, 2 * BLK)
+        part = jnp.dot(d[rows, :], wide[...], preferred_element_type=F32)
+
+        @pl.when(c == 0)
+        def _():
+            own[side, slot] = part[:BLK]
+            csend[side, slot] = part[BLK:].astype(BF16)
+
+        @pl.when(c == 1)
+        def _():
+            own[side, slot] = part[BLK:]
+            csend[side, slot] = part[:BLK].astype(BF16)
+
+        core_copy(side, slot).start()
+
+        @pl.when(step == 1)
+        def _():
+            far_out(0)
+
+        @pl.when(step == 2)
+        def _():
+            far_out(1)
+
+        return carry
+
+    lax.fori_loop(0, 4, through, 0)
+
+    def weight_chunk(j, carry):
+        cols = pl.ds(pl.multiple_of(j * 384, LANES), 384)
+        wideg[rows_at(j * 384, 384), :] = tn(d[:, cols], h1[...]).astype(BF16)
+        return carry
+
+    lax.fori_loop(0, 4, weight_chunk, 0)
+    for shard in range(2):
+        grads[2, shard, :UNIT_ROWS, :] = tn(
+            spread[...], wideg[shard * 6 * LANES : (shard + 1) * 6 * LANES, :]
+        ).astype(BF16)
+        grads[2, shard, UNIT_ROWS:, :] = wo_g[shard * QTR : (shard + 1) * QTR, :]
+    reduces[2].start()
+    ones = jnp.ones((8, SEQ), BF16)
+    col_sums = jnp.dot(ones, d[...], preferred_element_type=F32)
+    reduces[0].middle()
+    final_copy.start()
+
+    sums[...] = jnp.zeros_like(sums)
+    for slot in range(2):
+        core_copy(0, slot).wait_recv()
+        chip_copy(slot).wait_recv()
+
+        def group(g, carry, slot=slot):
+            row = slot * (BLK // 16) + g
+            rows = rows_at(row * 16, 16)
+            here = rows_at(g * 16, 16)
+            normed, inverse = norm_tile(x2[rows, :].astype(F32))
+            dh = (
+                own[0, slot, here, :]
+                + crecv[0, slot, here, :].astype(F32)
+                + qrecv[slot, here, :].astype(F32)
+            )
+            at = pl.ds(row, 1)
+            e = dh * (1.0 + scale[at, :])
+            out = dx[rows, :] + inverse * (
+                e
+                - jnp.mean(e, axis=1, keepdims=True)
+                - normed * jnp.mean(e * normed, axis=1, keepdims=True)
+            )
+            tsend[slot, here, :] = out.astype(BF16)
+
+            @pl.when(slot == p)
+            def _():
+                tokens_out[p, here, :] = out
+
+            sums[at, 0:D] = jnp.sum(dh, axis=0, keepdims=True)
+            sums[at, D : 2 * D] = jnp.sum(dh * normed, axis=0, keepdims=True)
+            return carry
+
+        lax.fori_loop(0, BLK // 16, group, 0)
+
+    token_copy = remote(tsend.at[1 - p], tsend.at[2], sems, 40, p=1 - p)
+
+    two = jnp.concatenate([sums[...], sums_two[...]], axis=1)
+    full = lax.dot_general(
+        hot[...], two, (((0,), (0,)), ((), ())), preferred_element_type=F32,
+        precision=lax.Precision.HIGHEST,
+    )
+    for k in range(8):
+        parcel[k] = full[:, k * MODS : (k + 1) * MODS]
+        parcel[k, 11:14, : D // 8] = smalls[0:3, k * (D // 8) : (k + 1) * (D // 8)]
+    for shard in range(2):
+        heads = col_sums[0:1, shard * 6 * LANES : (shard + 1) * 6 * LANES]
+        pieces = [b_up[0:1, shard * WROWS : (shard + 1) * WROWS]]
+        for unit in (0, 2, 3, 5):
+            pieces.append(heads[:, unit * LANES : unit * LANES + HD])
+        owner = lax.rem(p + shard, 2) * 4 + q * 2 + c
+        parcel[owner, 14:15, :] = jnp.concatenate(pieces, axis=1)
+    copies = []
+    for k, where in enumerate(line):
+        copy = remote(
+            parcel.at[where["p"] * 4 + where["q"] * 2 + where["c"]], parcels.at[me], sems, 41 + k,
+            **where,
+        )
+        copy.start()
+        copies.append(copy)
+    own_parcel = keep_local(parcel.at[me], parcels.at[me], 3)
+    token_copy.start()
+    reduces[1].middle()
+    lines[0].start()
+    own_parcel.wait()
+    for copy in copies:
+        copy.wait_recv()
+    for row in range(2):
+        modline[row] = sum(parcels[row * 4 + k] for k in range(4)).astype(BF16)
+    mods = []
+    for k, where in enumerate(plane):
+        copy = remote(modline, mod_out.at[rank], sems, 48 + k, **where)
+        copy.start()
+        mods.append(copy)
+    own_mod = keep_local(modline, mod_out.at[rank], 4)
+
+    condbuf[0] = jnp.dot(
+        modline[...].reshape(32, MODS), ada[...], preferred_element_type=F32
+    ).astype(BF16)
+    conds = []
+    for k, where in enumerate(({"c": 1 - c}, {"q": 1 - q}, {"p": 1 - p})):
+        copy = remote(condbuf.at[2 * k], condbuf.at[2 * k + 1], sems, 51 + k, **where)
+        copy.start()
+        conds.append(copy)
+        if k == 0:
+            reduces[2].middle()
+        if k == 1:
+            lines[1].start()
+        if k == 2:
+            lines[0].spread()
+        copy.wait_recv()
+        total = condbuf[2 * k].astype(F32) + condbuf[2 * k + 1].astype(F32)
+        if k < 2:
+            condbuf[2 * k + 2] = total.astype(BF16)
+    cond_out[...] = total * slope[...]
+
+    lines[2].start()
+    lines[0].forward()
+    lines[1].spread()
+    token_copy.wait_recv()
+    tokens_out[1 - p] = tsend[2].astype(F32)
+    lines[0].finish()
+    lines[1].forward()
+    lines[2].spread()
+    lines[1].finish()
+    lines[2].forward()
+    lines[2].finish()
+    final_copy.wait_recv()
+    for copy in mods:
+        copy.wait_recv()
+    for copy in [final_copy, token_copy] + copies + mods + conds:
+        copy.wait_send()
+    for slot in range(2):
+        for side in range(2):
+            core_copy(side, slot).wait_send()
+        chip_copy(slot).wait_send()
+    for k in range(3):
+        reduces[k].sent()
+        lines[k].sent()
+    own_final.wait()
+    own_mod.wait()
+
+
+def back(d, h1, wide, x2, dx, scale, sums_two, smalls, b_up, up_g, down_g, wo_g, hot, spread, final, ada, slope):
+    return pl.pallas_call(
+        back_kernel,
+        out_shape=(
+            shape_of(2, BLK, D), shape_of(2, BLK, D, dtype=F32), shape_of(WROWS, D),
+            shape_of(WROWS, D), shape_of(WROWS, D), shape_of(4, 2, 16, MODS),
+            shape_of(32, D, dtype=F32),
+        ),
+        in_specs=[VMEM_SPEC] * 9 + [ANY_SPEC] * 2 + [VMEM_SPEC] * 6,
+        out_specs=(VMEM_SPEC,) * 7,
+        scratch_shapes=[
+            pltpu.VMEM((2, 2, BLK, D), F32),
+            pltpu.VMEM((2, 2, BLK, D), BF16),
+            pltpu.VMEM((2, 2, BLK, D), BF16),
+            pltpu.VMEM((2, BLK, D), BF16),
+            pltpu.VMEM((2, BLK, D), BF16),
+            pltpu.VMEM((WIDE, D), BF16),
+            pltpu.VMEM((3, 2, WROWS, D), BF16),
+            pltpu.VMEM((GROUPS, 2 * D), F32),
+            pltpu.VMEM((8, 16, MODS), F32),
+            pltpu.VMEM((8, 16, MODS), F32),
+            pltpu.VMEM((2, 16, MODS), BF16),
+            pltpu.VMEM((6, 32, D), BF16),
+            pltpu.VMEM((3, BLK, D), BF16),
+            pltpu.VMEM((3, 2, QTR, D), BF16),
+        ]
+        + REDUCE_SCRATCH * 3
+        + [
+            pltpu.SemaphoreType.DMA((54,)),
+            pltpu.SemaphoreType.DMA((54,)),
+            pltpu.SemaphoreType.DMA((5,)),
+        ],
+        compiler_params=pltpu.CompilerParams(
+            collective_id=8, has_side_effects=True, vmem_limit_bytes=63 * 2**20
+        ),
+        name="back",
+    )(d, h1, wide, x2, dx, scale, sums_two, smalls, b_up, up_g, down_g, wo_g, hot, spread, final, ada, slope)
 
 
 def layer_device(
@@ -1288,38 +1535,6 @@
     triple, hidden_one, token_low, keep_low, mod_groups, w_wide, w_out_all, biases, act_all = front(
         mod_part, by_row(tokens), keep_wide, act_low, bias_own, w_a, spread, hot_rows
     )
-    mod_rows = mod_groups[:22].reshape(2, BLK // 16, 6 * D)
-    scale_one = mod_rows[:, :, None, D : 2 * D]
-
-    def grouped(values):
-        return values.reshape(2, BLK // 16, 16, -1)
-
-    def flat(values):
-        return values.reshape(2, BLK, -1)
-
-    token_values = grouped(token_low.astype(F32))
-    normed_one, inverse_one = norm_rows(token_values)
-
-    def group_scatter(near_part, far_part):
-        far_sum = (far_part[0].astype(F32) + swap(far_part[1], "c").astype(F32)).astype(BF16)
-        far_in = swap(far_sum, "q")
-        near_sum = near_part[0].astype(F32) + swap(near_part[1], "c").astype(F32)
-        return near_sum + far_in.astype(F32)
-
-    def split_chips(values):
-        parts = values.reshape(2, 2, 2, BLK, -1)
-
-        def chip(index):
-            one = lax.dynamic_index_in_dim(parts, index, 1, keepdims=False)
-            return jnp.stack(
-                [
-                    lax.dynamic_index_in_dim(one, c, 1, keepdims=False),
-                    lax.dynamic_index_in_dim(one, 1 - c, 1, keepdims=False),
-                ]
-            )
-
-        return chip(q), chip(1 - q)
-
     head_row = row_of(head_mask)
     heads_here = jnp.concatenate(
         [
@@ -1361,91 +1576,23 @@
         by_row(grad_out), w_out_all.reshape(4 * QTR, D), w_up_rows, w_down, b_up_two, consts,
         group_wide,
     )
-    grad_mixed = grouped(grad_mixed)
     d_all = attn_bwd(scal, triple, grad_attended, lse, pack)
-    d_near, d_far = split_chips(jnp.dot(d_all, w_wide, preferred_element_type=F32).astype(BF16))
-    dh1_near, dh1_far = d_near, d_far
-    grad_hidden_one = grouped(group_scatter(dh1_near, dh1_far))
-
-    def reduce_pair(mine, other):
-        both = plane_scatter(jnp.stack([mine, other], axis=1), rank)
-        total = both[0] + swap(both[1].astype(BF16), "p").astype(F32)
-        return plane_gather(total.astype(BF16), rank).astype(F32)
-
-    down_low = down_low.reshape(2, 4, QTR, D)
-    up_low = up_low.reshape(2, 4, QTR, D)
-    out_w_down = reduce_pair(down_low[0], down_low[1]).reshape(WROWS, D)
-    out_w_up = jnp.transpose(reduce_pair(up_low[0], up_low[1]).reshape(WROWS, D))
-    wide_low = tn(d_all, hidden_one).astype(BF16)
-    a_low = [
-        jnp.concatenate(
-            [
-                tn(spread, wide_low[k * 6 * LANES : (k + 1) * 6 * LANES]).astype(BF16),
-                wo_low[k * 2 * HD : (k + 1) * 2 * HD],
-            ]
-        ).reshape(4, QTR, D)
-        for k in range(2)
-    ]
-    out_a = reduce_pair(a_low[0], a_low[1]).reshape(WROWS, D)
-    out_w_qkv = jnp.transpose(out_a[:UNIT_ROWS])
-    out_w_out = out_a[UNIT_ROWS:]
-
-    grad_tokens = flat(
-        grad_mixed + norm_back(grad_hidden_one * (1.0 + scale_one), normed_one, inverse_one)
-    )
-
-    def from_rows(values, dtype):
-        mine = jnp.where(first, values[0], values[1])
-        other = swap(jnp.where(first, values[1], values[0]).astype(BF16), "p").astype(dtype)
-        return jnp.stack(
-            [jnp.where(first, mine, other), jnp.where(first, other, mine)], axis=1
-        ).astype(dtype)
-
-    out_final = from_rows(final.reshape(2, BLK, D), BF16)
-    out_tokens = from_rows(grad_tokens, F32)
-
-    group_sums = [jnp.sum(v, axis=2) for v in (grad_hidden_one, grad_hidden_one * normed_one)]
-    group_sums.append(sums_two[:22].reshape(2, BLK // 16, 4 * D))
-    part_mod = jnp.einsum(
-        "sgc,sgm->cm", hot, jnp.concatenate(group_sums, axis=-1), precision=highest
-    )[:CROPS]
-    part_mod = jnp.transpose(part_mod.reshape(CROPS, 8, 6 * D // 8), (1, 0, 2))
-    smalls = smalls[:3].reshape(3, 8, D // 8)
-    smalls = jnp.pad(jnp.transpose(smalls, (1, 0, 2)), ((0, 0), (0, 0), (0, 5 * D // 8)))
-    d_ones = jnp.sum(d_all, axis=0, dtype=F32)
-    d_ones = d_ones.reshape(2, 2, 3, LANES)[..., :HD]
-    qv_sums = jnp.stack([d_ones[:, :, 0], d_ones[:, :, 2]], axis=2).reshape(2, 4 * HD)
-    bias_sums = jnp.concatenate([b_up_sums[0].reshape(2, 2 * GW), qv_sums], axis=1)
-    who = jnp.arange(8)[:, None]
-    bias_rows = jnp.where(
-        who == shard, bias_sums[0], jnp.where(who == partner, bias_sums[1], 0.0)
-    )
-    parcel = jnp.concatenate(
-        [part_mod, smalls, bias_rows[:, None], jnp.zeros((8, 1, 6 * D // 8), F32)], axis=1
-    )
-    parcels = line_exchange(parcel, "slice", 2, "dmod_exchange")
-    line_sum = jnp.sum(parcels.reshape(2, 4, 16, 6 * D // 8), axis=1)
-    line_low = line_sum.astype(BF16)
-    mod_low = line_low[:, :CROPS]
-    plane_low = plane_exchange(line_low, 4, "small_exchange")
-    mod_all = plane_low[:, :, :CROPS]
-    grad_ada_w = jnp.einsum(
-        "rbcd,rbcm->dm", act_all[:, :, :CROPS], mod_all, preferred_element_type=F32
-    )
-    grad_ada_b = jnp.sum(mod_all, axis=(0, 1, 2), dtype=F32)
-    rest = jnp.sum(plane_low[:, :, CROPS:], axis=(0, 1), dtype=F32)
-    grad_b_out, grad_b_down, grad_w_route = (rest[k, : D // 8] for k in range(3))
-    out_b_up = rest[3, : 2 * GW]
-    out_b_qv = rest[3, 2 * GW :]
-    part_activ = jnp.einsum("bcm,dm->bcd", mod_low, ada_w, preferred_element_type=F32)
-    part_activ = jnp.pad(part_activ.astype(BF16), ((0, 0), (0, 5), (0, 0)))
-    grad_activ = jnp.sum(
-        line_exchange(part_activ, "all", 5, "cond_exchange").astype(F32), axis=0
-    )[:, :CROPS]
-    grad_cond = grad_activ * sig * (1.0 + cvec * (1.0 - sig))
+    slope = jnp.pad(sig * (1.0 + cvec * (1.0 - sig)), ((0, 0), (0, 5), (0, 0))).reshape(32, D)
+    final_pair, token_pair, low_a, low_up, low_down, mod_all, grad_cond = back(
+        d_all, hidden_one, w_wide, token_low.reshape(2 * BLK, D), grad_mixed,
+        mod_groups[:, D : 2 * D], sums_two, smalls, b_up_sums, up_low.reshape(2, WROWS, D),
+        down_low.reshape(2, WROWS, D), wo_low, hot_rows, spread, final, jnp.transpose(ada_w), slope,
+    )
+    out_a = low_a.astype(F32)
+    mod_low = jnp.where(jnp.arange(16)[:, None] < CROPS, mod_all, 0)
+    grad_ada_w = tn(mod_low.reshape(128, MODS), act_all.reshape(128, D))
+    grad_ada_b = jnp.sum(mod_low, axis=(0, 1, 2), dtype=F32)
+    rest = jnp.sum(mod_all[:, :, CROPS:], axis=(0, 1), dtype=F32)
     return (
-        out_final, out_tokens, grad_cond, grad_ada_w, grad_ada_b, out_w_qkv, out_b_qv, out_w_out,
-        grad_b_out, out_w_up, out_b_up, out_w_down, grad_b_down, grad_w_route,
+        by_row(final_pair), by_row(token_pair), grad_cond.reshape(2, 16, D)[:, :CROPS],
+        jnp.transpose(grad_ada_w), grad_ada_b, jnp.transpose(out_a[:UNIT_ROWS]), rest[3, 2 * GW :],
+        out_a[UNIT_ROWS:], rest[0, : D // 8], jnp.transpose(low_up.astype(F32)), rest[3, : 2 * GW],
+        low_down.astype(F32), rest[1, : D // 8], rest[2, : D // 8],
     )
 
 

time: 555 us -> 481 us (0.87)
  Pallas kernels: 318 us -> 430 us
  waiting for transfers between devices: 61.6 us -> 0 us
  other arithmetic: 55 us -> 13 us
  starting transfers between devices: 33.3 us -> 0 us
  local copies, waits for them, and re-layouts: 48.3 us -> 22.7 us
  matrix products: 26.7 us -> 6.96 us
    pallas_call x3 -> x1, Pallas kernels: 38.2 us -> 146 us  [back(): pl.pallas_call(back_kernel, out_shape=(shape_of(2, BLK, D), shape_of(2, B...]
    ppermute x32 -> x0, waiting for transfers between devices: 61.6 us -> none  [swap(): return lax.ppermute(values, axis, SWAP)]
    ppermute x32 -> x0, starting transfers between devices: 33.3 us -> none  [swap(): return lax.ppermute(values, axis, SWAP)]
    dot_general x4 -> x0, matrix products: 14.7 us -> none  [the longest x1 8.9 us: layer_device(): jnp.dot(d_all, w_wide, preferred_element_type=F32).astype(BF16)]
    slice x17 -> x5, local copies, waits for them, and re-layouts: 15.1 us -> 4.27 us  [the longest x1 1.55 us: layer_device(): mod_groups[:, D:2 * D]]
    reduce_sum x9 -> x2, other arithmetic: 11.1 us -> 0.76 us  [the longest x1 0.72 us: layer_device(): grad_ada_b = jnp.sum(mod_low, axis=(0, 1, 2), dtype=F32)]
    convert_element_type x19 -> x2, other arithmetic: 9.64 us -> 1.88 us  [the longest x1 1.69 us: layer_device(): low_down.astype(F32)]
    dot_general x3 -> x1, matrix products: 10.3 us -> 3.78 us  [tn(): lax.dot_general(a, b, (((0,), (0,)), ((), ())), preferred_element_type=F32)]
  transfers between devices with their start and end apart: 32 -> 0, of which waited for: 10 -> 0; matrix products, arithmetic and copies ran while one was open for 18% -> 0% of each run, Pallas kernels for 10% -> 0%
where the time goes in v3:
time: 481 us; the launch traced here: 474 us
  Pallas kernels  430 us (89%)
  local copies, waits for them, and re-layouts  22.7 us (5%)
  other arithmetic  13 us (3%)
  matrix products  6.96 us (1%)
    pallas_call x1, Pallas kernels, middle(): pl.pallas_call(middle_kernel, out_shape=(shape_of(2 * BLK, D), shape_of(2...  170 us
    pallas_call x1, Pallas kernels, back(): pl.pallas_call(back_kernel, out_shape=(shape_of(2, BLK, D), shape_of(2, B...  146 us
    pallas_call x1, Pallas kernels, front(): pl.pallas_call(front_kernel, out_shape=(shape_of(SEQ, WIDE), shape_of(SEQ...  81.4 us
    pallas_call x1, Pallas kernels, attn_bwd(): pl.pallas_call(attn_bwd_kernel, out_shape=jax.ShapeDtypeStruct((SEQ, WIDE...  17.9 us
    pallas_call x1, Pallas kernels, attn_fwd(): pl.pallas_call(attn_fwd_kernel, out_shape=(jax.ShapeDtypeStruct((SEQ, NH...  14.4 us
    unnamed x51, local copies, waits for them, and re-layouts  11.4 us

profile of v3, /device:TPU:0, one launch (start us, length us, event | category | flops | bytes accessed | tf_op | source)
XLA Modules:
  0.0 474.4 jit_solution(4996732585272926422)
XLA Ops:
  0.7 0.9 broadcast_select_fusion.2
  2.1 0.8 and_select_fusion
  2.8 0.2 reduce-window.4
  3.0 0.8 bitcast_subtract_fusion.1
  4.0 0.6 pad_convert_fusion.hot
  4.7 0.7 convert_element_type.63
  5.4 0.4 multiply_cosine_fusion
  5.7 0.9 add_multiply_fusion
  6.6 0.7 convert_element_type.65
  7.3 2.9 fusion.2.part
  10.2 0.6 pad.33.act
  11.1 0.6 broadcast_in_dim.15.bias_own
  11.8 1.2 pad_maximum_fusion.w_a
  12.9 1.0 copy.83
  13.9 0.8 broadcast_in_dim.14.k_pair
  14.7 81.4 %front.1 = (bf16[1408,1536]{1,0:T(8,128)(2,1)}, bf16[1408,1152]{1,0:T(8,128)(2,1)}, bf16[2,176,1152]{2,1,0:T(8,128)(2,1)}, bf16[2,176,128]{2,1,0:T(8,128)(2,1)},...) custom-call(f32[2,16,864]{2,1,0:T(8,128)} %fusion.2.part, ...), custom_call_target="tpu_custom_call" | custom-call | tf_op jit(solution)/shard_map/front/pallas_call | solution.py:715
  96.1 14.4 %attn_fwd.1 = (bf16[1408,288]{1,0:T(8,128)(2,1)S(1)}, f32[1408,128]{1,0:T(8,128)S(1)}) custom-call(s32[77]{0:T(128)S(1)} %pad_add_fusion.1.scal, bf16[1408,1536]{1,0:T(8,128)(2,1)} %get-tuple-element.41.buf, bf16[512,288]{1,0:T(8,128)(2,1)S(1)} %copy-done), custom_call_target="tpu_custom_call" | custom-call | tf_op jit(solution)/shard_map/attn_fwd/pallas_call | solution.py:434
  110.5 1.0 copy-done.1
  111.4 0.9 copy-done.3
  112.6 0.3 fusion.11
  112.9 0.2 broadcast_in_dim.16
  113.1 1.0 reshape.188.gmask
  114.1 0.7 slice_bitcast_fusion.2
  114.9 0.7 pad_maximum_fusion.1.bias
  115.6 1.0 copy.82
  116.6 0.6 fusion.10.consts
  117.2 170.3 %middle.1 = (bf16[352,1152]{1,0:T(8,128)(2,1)}, f32[352,1152]{1,0:T(8,128)}, bf16[1408,288]{1,0:T(8,128)(2,1)}, f32[24,4608]{1,0:T(8,128)}, f32[8,1152]{1,0:T(8,...) custom-call(bf16[1408,288]{1,0:T(8,128)(2,1)} %copy-done.1, ...), custom_call_target="tpu_custom_call" | custom-call | tf_op jit(solution)/shard_map/middle/pallas_call | solution.py:1056
  287.5 1.2 copy-done.2
  288.8 1.1 copy-done.4
  289.9 17.9 %attn_bwd.1.d = bf16[1408,1536]{1,0:T(8,128)(2,1)} custom-call(s32[77]{0:T(128)S(1)} %pad_add_fusion.1.scal, bf16[1408,1536]{1,0:T(8,128)(2,1)} %get-tuple-element.41.buf, bf16[1408,288]{1,0:T(8,128)(2,1)S(1)} %copy-done.2, f32[1408,128]{1,0:T(8,128)S(1)} %copy-done.4, bf16[512,288]{1,0:T(8,128)(2,1)S(1)} %copy-done), custom_call_target="tpu_custom_call" | custom-call | tf_op jit(solution)/shard_map/attn_bwd/pallas_call | solution.py:448
  307.8 1.5 slice.78.scale
  309.3 0.7 pad.41
  310.0 146.4 %back.1 = (bf16[2,176,1152]{2,1,0:T(8,128)(2,1)}, f32[2,176,1152]{2,1,0:T(8,128)}, bf16[576,1152]{1,0:T(8,128)(2,1)}, bf16[576,1152]{1,0:T(8,128)(2,1)}, bf16[57...) custom-call(bf16[1408,1536]{1,0:T(8,128)(2,1)} %attn_bwd.1.d, ...), custom_call_target="tpu_custom_call" | custom-call | tf_op jit(solution)/shard_map/back/pallas_call | solution.py:1445
  456.5 3.8 convolution_bitcast_fusion
  460.2 0.2 convert_element_type.73
  460.4 1.4 slice_bitcast_fusion
  461.9 0.5 copy-done.9
  462.4 1.7 convert_bitcast_fusion
  464.2 1.7 convert_element_type.75
  465.9 0.4 copy-done.6
  466.3 2.0 copy.71
  468.3 1.5 copy.70
  469.8 0.9 slice.93
  470.7 0.7 copy.74
  471.4 0.6 slice_reduce_fusion
  472.1 0.6 fusion.23
  472.6 0.7 slice_reduce_fusion.1
  473.3 0.7 convert_reduce_fusion
  (73 shorter events, 1.5 us)
Async XLA Ops:
  0.6 10.2 %copy-start.22 = (bf16[288]{0:T(512)(128)(2,1)S(1)}, bf16[288]{0:T(512)(128)(2,1)}, u32[]{:S(2)}) copy-start(bf16[288]{0:T(512)(128)(2,1)} %param.33) | copy-start | bytes 1732
  0.7 10.5 %copy-start.20 = (bf16[576]{0:T(1024)(128)(2,1)S(1)}, bf16[576]{0:T(1024)(128)(2,1)}, u32[]{:S(2)}) copy-start(bf16[576]{0:T(1024)(128)(2,1)} %param.37) | copy-start | bytes 3460
  0.7 11.1 %copy-start.10 = (bf16[1152,432]{0,1:T(8,128)(2,1)S(1)}, bf16[1152,432]{0,1:T(8,128)(2,1)}, u32[]{:S(2)}) copy-start(bf16[1152,432]{0,1:T(8,128)(2,1)} %param.32) | copy-start | bytes 2985988
  0.7 11.1 %copy-start.14 = (bf16[144,1152]{1,0:T(8,128)(2,1)S(1)}, bf16[144,1152]{1,0:T(8,128)(2,1)}, u32[]{:S(2)}) copy-start(bf16[144,1152]{1,0:T(8,128)(2,1)} %param.34) | copy-start | bytes 995332
  10.2 2.7 copy-start.11
  11.8 2.1 copy-start.21
  13.9 82.2 %copy-start = (bf16[512,288]{1,0:T(8,128)(2,1)S(1)}, bf16[512,288]{1,0:T(8,128)(2,1)}, u32[]{:S(2)}) copy-start(bf16[512,288]{1,0:T(8,128)(2,1)} %constant.71.clone.pack) | copy-start | bytes 884740
  110.5 1.0 copy-start.1
  111.4 0.9 copy-start.3
  112.3 3.3 copy-start.12
  112.3 4.2 copy-start.17
  112.3 4.2 copy-start.18
  112.3 4.3 copy-start.19
  287.5 1.2 copy-start.2
  288.8 1.1 copy-start.4
  310.0 146.4 %copy-start.15 = (bf16[4,2,16,1152]{3,2,1,0:T(8,128)(2,1)S(1)}, bf16[4,2,16,1152]{3,2,1,0:T(8,128)(2,1)}, u32[]{:S(2)}) copy-start(bf16[4,2,16,1152]{3,2,1,0:T(8,128)(2,1)} %get-tuple-element.63) | copy-start | bytes 884740
  456.4 3.8 copy-start.5
  460.4 1.9 copy-start.9
  462.4 1.8 copy-start.8
  464.2 2.1 copy-start.6
  465.9 2.4 copy-start.13
  468.3 2.4 copy-start.16
  468.3 3.1 copy-start.7

commit v4 on v3

--- a/solution.py
+++ b/solution.py
@@ -500,38 +500,54 @@
 
 
 class PlaneGather:
-    def __init__(self, src, dst, sems, k, y, x, p):
-        self.dst, self.sems, self.k, self.y, self.x = dst, sems, k, y, x
-        self.rank = y * 2 + x
-        mine = rows_at(self.rank * QTR, QTR)
-        self.over = remote(src.at[mine], dst.at[mine], sems, k, p=1 - p)
-        self.to_x = remote(dst.at[mine], dst.at[mine], sems, k + 1, x=1 - x)
-        self.to_y = remote(dst.at[mine], dst.at[mine], sems, k + 2, y=1 - y)
-        from_x = rows_at((y * 2 + 1 - x) * QTR, CUT)
-        from_y = rows_at(((1 - y) * 2 + x) * QTR + CUT, QTR - CUT)
-        self.on_y = remote(dst.at[from_x], dst.at[from_x], sems, k + 3, y=1 - y)
-        self.on_x = remote(dst.at[from_y], dst.at[from_y], sems, k + 4, x=1 - x)
+    COPIES = 8
+
+    def __init__(self, src, dst, sems, k, y, x, p, loaded=None):
+        self.loaded = loaded
+        self.over, self.to_x, self.to_y = [], [], []
+        for i, (start, size) in enumerate(((0, CUT), (CUT, QTR - CUT))):
+            rows = rows_at((y * 2 + x) * QTR + start, size)
+            mine = dst.at[rows]
+            if loaded is None:
+                self.over.append(remote(src.at[rows], mine, sems, k + i, p=1 - p))
+            else:
+                self.over.append(
+                    pltpu.make_async_copy(src.at[start : start + size], mine, loaded.at[i])
+                )
+            self.to_x.append(remote(mine, mine, sems, k + 2 + i, x=1 - x))
+            self.to_y.append(remote(mine, mine, sems, k + 4 + i, y=1 - y))
+        from_x = dst.at[rows_at((y * 2 + 1 - x) * QTR, CUT)]
+        from_y = dst.at[rows_at(((1 - y) * 2 + x) * QTR + CUT, QTR - CUT)]
+        self.on_y = remote(from_x, from_x, sems, k + 6, y=1 - y)
+        self.on_x = remote(from_y, from_y, sems, k + 7, x=1 - x)
 
     def start(self):
-        self.over.start()
-
-    def spread(self):
-        self.over.wait_recv()
-        self.to_x.start()
-        self.to_y.start()
-
-    def forward(self):
-        self.to_x.wait_recv()
-        self.on_y.start()
-        self.to_y.wait_recv()
-        self.on_x.start()
+        for copy in self.over:
+            copy.start()
+
+    def spread(self, i):
+        if self.loaded is None:
+            self.over[i].wait_recv()
+        else:
+            self.over[i].wait()
+        self.to_x[i].start()
+        self.to_y[i].start()
+
+    def forward(self, i):
+        if i == 0:
+            self.to_x[0].wait_recv()
+            self.on_y.start()
+        else:
+            self.to_y[1].wait_recv()
+            self.on_x.start()
 
     def finish(self):
-        self.on_y.wait_recv()
-        self.on_x.wait_recv()
+        for copy in (self.to_y[0], self.to_x[1], self.on_y, self.on_x):
+            copy.wait_recv()
 
     def sent(self):
-        for copy in (self.over, self.to_x, self.to_y, self.on_y, self.on_x):
+        copies = self.to_x + self.to_y + [self.on_y, self.on_x]
+        for copy in copies if self.loaded is not None else self.over + copies:
             copy.wait_send()
 
 
@@ -543,9 +559,9 @@
 
 
 def front_kernel(
-    part, x_pair, k_pair, act, bias_own, w_a, spread, hot,
-    t_out, h_out, x_out, k_out, modg_out, wide_out, wo_out, bias_out, act_out,
-    mods, modg, h, wide, other_a, own_a, tbuf, send, recv, loc,
+    cvec_ref, x_pair, k_pair, g_pair, bias_own, w_a, spread, hot, ada, ada_b,
+    t_out, h_out, x_out, k_out, g_out, modg_out, wide_out, wo_out, bias_out, act_out, slope_out,
+    part, mods, modg, h, wide, other_a, own_a, tbuf, send, recv, loc,
 ):
     y, x, p, q, c = (lax.axis_index(name) for name in "yxpqc")
     sems = (send, recv)
@@ -553,7 +569,6 @@
         {"q": lax.rem(q + k // 2, 2), "c": lax.rem(c + k % 2, 2)} for k in range(1, 4)
     ]
     plane = [{"y": lax.rem(y + k // 2, 2), "x": lax.rem(x + k % 2, 2)} for k in range(1, 4)]
-    greet(pair + plane + [{"p": 1 - p}])
     rank = y * 2 + x
     waits = []
 
@@ -562,45 +577,61 @@
         copy.start()
         return copy
 
+    load_a = keep_local(w_a, own_a, 0)
+    cvec = cvec_ref[...]
+    sig = 1.0 / (1.0 + jnp.exp(-cvec))
+    slope_out[...] = sig * (1.0 + cvec * (1.0 - sig))
+    act = (cvec * sig).astype(BF16)
+    act_mine = act_out.at[rank]
+    act_mine[...] = act
+    mod_all = nt(act, ada[...]) + ada_b[...]
+    part[0] = mod_all[:16]
+    part[1] = mod_all[16:]
+
+    greet(pair + plane + [{"p": 1 - p}])
+
     def spot(pp, qq, cc):
         return pp * 4 + qq * 2 + cc
 
     mod_over = remote(part.at[1 - p], mods.at[spot(p, q, c)], sems, 0, p=1 - p)
     mod_over.start()
-    bias_copy = remote(bias_own, bias_out.at[1], sems, 7, p=1 - p)
-    bias_copy.start()
-    x_copy = remote(x_pair.at[1 - p], x_out.at[p], sems, 8, p=1 - p)
-    x_copy.start()
-    k_copy = remote(k_pair.at[1 - p], k_out.at[p], sems, 9, p=1 - p)
-    k_copy.start()
-    take_a = PlaneGather(w_a, other_a, sems, 10, y, x, p)
-    take_a.start()
     own_mod = keep_local(part.at[p], mods.at[spot(p, q, c)], 1)
     mod_own = []
     mod_far = []
     for k, where in enumerate(pair):
-        mine = mods.at[spot(p, q, c)]
-        copy = remote(part.at[p], mine, sems, 1 + k, **where)
+        copy = remote(part.at[p], mods.at[spot(p, q, c)], sems, 1 + k, **where)
         copy.start()
         mod_own.append(copy)
-    load_a = keep_local(w_a, own_a, 0)
+    bias_copy = remote(bias_own, bias_out.at[1], sems, 17, p=1 - p)
+    bias_copy.start()
+    k_copy = remote(k_pair.at[1 - p], k_out.at[p], sems, 18, p=1 - p)
+    k_copy.start()
+    take_a = PlaneGather(w_a, other_a, sems, 7, y, x, p)
+    take_a.start()
+    pieces = ((0, 96), (96, 80))
+    x_copies = []
+    for i, (start, size) in enumerate(pieces):
+        rows = slice(start, start + size)
+        x_copies.append(remote(x_pair.at[1 - p, rows], x_out.at[p, rows], sems, 15 + i, p=1 - p))
     waits.append(keep_local(x_pair.at[p], x_out.at[p], 2))
     waits.append(keep_local(k_pair.at[p], k_out.at[p], 3))
-    waits.append(keep_local(bias_own, bias_out.at[0], 4))
-    waits.append(keep_local(act, act_out.at[rank], 5))
-    acts = []
-    for k, where in enumerate(plane):
-        copy = remote(act, act_out.at[rank], sems, 15 + k, **where)
-        copy.start()
-        acts.append(copy)
+    waits.append(keep_local(g_pair.at[p], g_out.at[p], 5))
+    own_bias = keep_local(bias_own, bias_out.at[0], 4)
+    load_a.wait()
+    tails = (own_a.at[UNIT_ROWS:], other_a.at[UNIT_ROWS:])
+    outer = [remote(tails[k], wo_out.at[2 + k], sems, 19 + k, q=1 - q) for k in range(2)]
     mod_over.wait_recv()
     for k, where in enumerate(pair):
         far = mods.at[spot(1 - p, q, c)]
         copy = remote(far, far, sems, 4 + k, **where)
         copy.start()
         mod_far.append(copy)
-
-    load_a.wait()
+    acts = []
+    for k, where in enumerate(plane):
+        copy = remote(act_mine, act_mine, sems, 21 + k, **where)
+        copy.start()
+        acts.append(copy)
+
     wide[: 6 * LANES, :] = jnp.dot(
         spread[...], own_a[:UNIT_ROWS, :], preferred_element_type=F32
     ).astype(BF16)
@@ -617,7 +648,7 @@
     def place(slot, chip, core):
         return slot * HALF + chip * (2 * BLK) + core * BLK
 
-    def modulate(src, slot):
+    def modulate(src, slot, start, size):
         base = place(slot, q, c)
 
         def group(g, carry):
@@ -629,33 +660,31 @@
             h[rows_at(base + g * 16, 16), :] = (normed * (1.0 + scale) + shift).astype(BF16)
             return carry
 
-        lax.fori_loop(0, BLK // 16, group, 0)
-
-    def block(slot, chip, core):
-        return h.at[rows_at(place(slot, chip, core), BLK)]
-
-    hops = {}
-    for i in range(2):
-        slot = p if i == 0 else 1 - p
-        mine = block(slot, q, c)
-        other = block(slot, 1 - q, c)
-        hops[i] = (
-            remote(mine, mine, sems, 18 + 3 * i, q=1 - q),
-            remote(mine, mine, sems, 19 + 3 * i, c=1 - c),
-            remote(other, other, sems, 20 + 3 * i, c=1 - c),
+        lax.fori_loop(start // 16, (start + size) // 16, group, 0)
+
+    first, second = p, 1 - p
+    spans = [(first, 0, BLK)] + [(second, start, size) for start, size in pieces]
+    hops = []
+    for i, (slot, start, size) in enumerate(spans):
+        mine = h.at[rows_at(place(slot, q, c) + start, size)]
+        other = h.at[rows_at(place(slot, 1 - q, c) + start, size)]
+        hops.append(
+            (
+                remote(mine, mine, sems, 24 + 3 * i, q=1 - q),
+                remote(mine, mine, sems, 25 + 3 * i, c=1 - c),
+                remote(other, other, sems, 26 + 3 * i, c=1 - c),
+            )
         )
 
-    modulate(x_pair.at[p], p)
+    modulate(x_pair.at[p], first, 0, BLK)
     hops[0][0].start()
     hops[0][1].start()
-    x_copy.wait_recv()
-    modulate(x_out.at[1 - p], 1 - p)
-    hops[1][0].start()
-    hops[1][1].start()
-    take_a.spread()
+    take_a.spread(0)
+    own_bias.wait()
     bias_copy.wait_recv()
-    for copy in waits[2:3]:
-        copy.wait()
+    take_a.spread(1)
+    for copy in x_copies:
+        copy.start()
     hops[0][1].wait_recv()
 
     def project(slot, chip, half):
@@ -664,83 +693,180 @@
         line = bias_out[half, 0:1, : 6 * LANES]
         tbuf[rows, cols] = (nt(h[rows, :], wide[cols, :]) + line).astype(BF16)
 
-    first, second = p, 1 - p
+    def stored(slot, chip, k):
+        rows = rows_at(place(slot, chip, 0), 2 * BLK)
+        waits.append(keep_local(tbuf.at[rows], t_out.at[rows], k))
+        waits.append(keep_local(h.at[rows], h_out.at[rows], k + 4))
+
     project(first, q, 0)
+    take_a.forward(0)
     hops[0][0].wait_recv()
     hops[0][2].start()
-    hops[1][1].wait_recv()
-    project(second, q, 0)
-    take_a.forward()
+    outer[0].start()
+    take_a.forward(1)
     hops[0][2].wait_recv()
     project(first, 1 - q, 0)
-    hops[1][0].wait_recv()
-    hops[1][2].start()
     take_a.finish()
+    outer[1].start()
     wide[6 * LANES :, :] = jnp.dot(
         spread[...], other_a[:UNIT_ROWS, :], preferred_element_type=F32
     ).astype(BF16)
     waits.append(keep_local(wide, wide_out, 7))
-    tails = (own_a.at[UNIT_ROWS:], other_a.at[UNIT_ROWS:])
-    outer = [remote(tails[k], wo_out.at[2 + k], sems, 24 + k, q=1 - q) for k in range(2)]
-    for copy in outer:
-        copy.start()
     for k in range(2):
         waits.append(keep_local(tails[k], wo_out.at[k], 8 + k))
+    x_copies[0].wait_recv()
+    modulate(x_out.at[second], second, *pieces[0])
+    hops[1][0].start()
+    hops[1][1].start()
     project(first, q, 1)
+    stored(first, q, 10)
+    x_copies[1].wait_recv()
+    g_copy = remote(g_pair.at[1 - p], g_out.at[p], sems, 33, p=1 - p)
+    g_copy.start()
+    modulate(x_out.at[second], second, *pieces[1])
+    hops[2][0].start()
+    hops[2][1].start()
+    hops[1][0].wait_recv()
+    hops[1][2].start()
+    project(first, 1 - q, 1)
+    stored(first, 1 - q, 11)
+    hops[1][1].wait_recv()
+    hops[2][1].wait_recv()
+    project(second, q, 0)
+    hops[2][0].wait_recv()
+    hops[2][2].start()
     project(second, q, 1)
-    project(first, 1 - q, 1)
+    stored(second, q, 12)
     hops[1][2].wait_recv()
-    waits.append(keep_local(h, h_out, 10))
+    hops[2][2].wait_recv()
     project(second, 1 - q, 0)
     project(second, 1 - q, 1)
-    waits.append(keep_local(tbuf, t_out, 11))
-    for copy in outer + acts + [k_copy]:
+    stored(second, 1 - q, 13)
+    for copy in outer + acts + [k_copy, g_copy]:
         copy.wait_recv()
-    for copy in [mod_over, bias_copy, x_copy, k_copy] + mod_own + mod_far + outer + acts:
+    for copy in [mod_over, bias_copy, k_copy, g_copy] + x_copies + mod_own + mod_far + outer + acts:
         copy.wait_send()
-    for i in range(2):
-        for copy in hops[i]:
+    for group in hops:
+        for copy in group:
             copy.wait_send()
     take_a.sent()
-    for k, copy in enumerate(waits):
-        if k != 2:
-            copy.wait()
+    for copy in waits:
+        copy.wait()
 
 
 def shape_of(*shape, dtype=BF16):
     return jax.ShapeDtypeStruct(shape, dtype)
 
 
-def front(part, x_pair, k_pair, act, bias_own, w_a, spread, hot):
+def front(*args):
     return pl.pallas_call(
         front_kernel,
         out_shape=(
             shape_of(SEQ, WIDE), shape_of(SEQ, D), shape_of(2, BLK, D), shape_of(2, BLK, LANES),
-            shape_of(GROUPS, 6 * D, dtype=F32), shape_of(WIDE, D), shape_of(4, QTR, D),
-            shape_of(2, 8, BIAS, dtype=F32), shape_of(4, 2, 16, D),
+            shape_of(2, BLK, D), shape_of(GROUPS, 6 * D, dtype=F32), shape_of(WIDE, D),
+            shape_of(4, QTR, D), shape_of(2, 8, BIAS, dtype=F32), shape_of(4, 32, D),
+            shape_of(32, D, dtype=F32),
         ),
-        in_specs=[VMEM_SPEC] * 5 + [ANY_SPEC] + [VMEM_SPEC] * 2,
+        in_specs=[VMEM_SPEC] * 3 + [ANY_SPEC, VMEM_SPEC, ANY_SPEC] + [VMEM_SPEC] * 4,
         out_specs=(
-            ANY_SPEC, ANY_SPEC, VMEM_SPEC, VMEM_SPEC, ANY_SPEC, ANY_SPEC, ANY_SPEC, VMEM_SPEC,
-            VMEM_SPEC,
+            ANY_SPEC, ANY_SPEC, VMEM_SPEC, VMEM_SPEC, ANY_SPEC, ANY_SPEC, ANY_SPEC, ANY_SPEC,
+            VMEM_SPEC, VMEM_SPEC, VMEM_SPEC,
         ),
         scratch_shapes=[
-            pltpu.VMEM((8, 16, 6 * D // 8), F32),
+            pltpu.VMEM((2, 16, MODS), F32),
+            pltpu.VMEM((8, 16, MODS), F32),
             pltpu.VMEM((GROUPS, 6 * D), F32),
             pltpu.VMEM((SEQ, D), BF16),
             pltpu.VMEM((WIDE, D), BF16),
             pltpu.VMEM((WROWS, D), BF16),
             pltpu.VMEM((WROWS, D), BF16),
             pltpu.VMEM((SEQ, WIDE), BF16),
-            pltpu.SemaphoreType.DMA((26,)),
-            pltpu.SemaphoreType.DMA((26,)),
-            pltpu.SemaphoreType.DMA((12,)),
+            pltpu.SemaphoreType.DMA((34,)),
+            pltpu.SemaphoreType.DMA((34,)),
+            pltpu.SemaphoreType.DMA((18,)),
         ],
         compiler_params=pltpu.CompilerParams(
             collective_id=6, has_side_effects=True, vmem_limit_bytes=56 * 2**20
         ),
         name="front",
-    )(part, x_pair, k_pair, act, bias_own, w_a, spread, hot)
+    )(*args)
+
+
+class PlaneReduce:
+    def __init__(self, grads, bufs, sems, k, y, x, landed=False):
+        self.grads, self.y, self.x = grads, y, x
+        self.low_in, self.high_in, self.low_out, self.high_out, self.low_end, self.high_end = bufs
+        self.first = [] if landed else [
+            remote(grads.at[:, self.low(y, 1 - x)], self.low_in.at[0], sems, k, x=1 - x),
+            remote(grads.at[:, self.low(1 - y, 1 - x)], self.low_in.at[1], sems, k + 1, x=1 - x),
+            remote(grads.at[:, self.high(1 - y, x)], self.high_in.at[0], sems, k + 2, y=1 - y),
+            remote(grads.at[:, self.high(1 - y, 1 - x)], self.high_in.at[1], sems, k + 3, y=1 - y),
+        ]
+        if self.low_out is None:
+            return
+        self.second = [
+            remote(self.low_out, self.low_end, sems, k + 4, y=1 - y),
+            remote(self.high_out, self.high_end, sems, k + 5, x=1 - x),
+        ]
+
+    def low(self, y, x):
+        return rows_at((y * 2 + x) * QTR, CUT)
+
+    def high(self, y, x):
+        return rows_at((y * 2 + x) * QTR + CUT, QTR - CUT)
+
+    def start(self):
+        for copy in self.first:
+            copy.start()
+
+    def landed(self):
+        for copy in self.first:
+            copy.wait_recv()
+
+    def middle(self):
+        y, x = self.y, self.x
+        for shard in range(2):
+            self.low_out[shard] = (
+                self.grads[shard, self.low(1 - y, x), :].astype(F32)
+                + self.low_in[1, shard].astype(F32)
+            ).astype(BF16)
+            self.high_out[shard] = (
+                self.grads[shard, self.high(y, 1 - x), :].astype(F32)
+                + self.high_in[1, shard].astype(F32)
+            ).astype(BF16)
+        for copy in self.second:
+            copy.start()
+
+    def arrive(self):
+        for copy in self.second:
+            copy.wait_recv()
+
+    def total(self, shard):
+        low = (
+            self.grads[shard, self.low(self.y, self.x), :].astype(F32)
+            + self.low_in[0, shard].astype(F32)
+            + self.low_end[shard].astype(F32)
+        )
+        high = (
+            self.grads[shard, self.high(self.y, self.x), :].astype(F32)
+            + self.high_in[0, shard].astype(F32)
+            + self.high_end[shard].astype(F32)
+        )
+        return low, high
+
+    def sent(self, second=True):
+        for copy in self.first + (self.second if second else []):
+            copy.wait_send()
+
+
+REDUCE_SCRATCH = [
+    pltpu.VMEM((2, 2, CUT, D), BF16),
+    pltpu.VMEM((2, 2, QTR - CUT, D), BF16),
+    pltpu.VMEM((2, CUT, D), BF16),
+    pltpu.VMEM((2, QTR - CUT, D), BF16),
+    pltpu.VMEM((2, CUT, D), BF16),
+    pltpu.VMEM((2, QTR - CUT, D), BF16),
+]
 
 
 def gelu_both(u):
@@ -752,10 +878,10 @@
 
 
 def middle_kernel(
-    o, x2, k2, modg, g_pair, wo, w_up, w_down, bias, consts, gmask,
-    final_out, dx_out, do_out, sums_out, small_out, up_out, down_out, gwo_out, bup_out,
-    g2, o_in, ybig, ysend, yrecv, y1, mixed, h2, dz, act, du, wup, wdown,
-    own, csend, crecv, qsend, qrecv, dy, dofar, wosend, worecv, send, recv, loc,
+    o, x2, k2, modg, g2, wo, w_up, up_quarter, w_down, bias, consts, gmask,
+    fin_out, fin_send_out, dx_out, do_out, sums_out, small_out, up_out, down_out, gwo_out, gwo_far_out, bup_out, down_low, down_high, up_low, up_high,
+    o_in, ybig, ysend, yrecv, y1, mixed, h2, dz, act, du, wup, wdown,
+    own, csend, crecv, qsend, qrecv, dy, dofar, send, recv, loc,
 ):
     y, x, p, q, c = (lax.axis_index(name) for name in "yxpqc")
     sems = (send, recv)
@@ -777,15 +903,14 @@
         )
         copy.start()
         o_copies.append(copy)
-    g_copy = remote(g_pair.at[1 - p], g2.at[pl.ds(p * BLK, BLK)], sems, 2, p=1 - p)
-    g_copy.start()
-    take_up = PlaneGather(w_up, wup.at[WROWS:], sems, 3, y, x, p)
-    take_down = PlaneGather(w_down, wdown.at[WROWS:], sems, 8, y, x, p)
+    take_up = PlaneGather(up_quarter, wup.at[1], sems, 43, y, x, p, loc.at[5:7])
+    take_down = PlaneGather(w_down, wdown.at[1], sems, 51, y, x, p)
     take_up.start()
     take_down.start()
-    own_g = keep_local(g_pair.at[p], g2.at[pl.ds(p * BLK, BLK)], 0)
-    own_up = keep_local(w_up, wup.at[:WROWS], 1)
-    own_down = keep_local(w_down, wdown.at[:WROWS], 2)
+    take_up.spread(0)
+    take_up.spread(1)
+    own_up = keep_local(w_up, wup.at[0], 1)
+    own_down = keep_local(w_down, wdown.at[0], 2)
 
     y_copies = []
     for slot in range(2):
@@ -800,9 +925,10 @@
         copy.start()
         y_copies.append(copy)
 
-    own_g.wait()
-    g_copy.wait_recv()
-    take_up.spread()
+    take_up.forward(0)
+    take_up.forward(1)
+    take_down.spread(0)
+    take_down.spread(1)
     b_out, b_down, w_route = consts[0:1, :], consts[1:2, :], consts[2:3, :]
 
     def routed(row):
@@ -846,15 +972,16 @@
 
         lax.fori_loop(0, BLK // 16, group, 0)
         for array in range(2):
-            hop(array, slot, 0).start()
+            if slot == 0:
+                hop(array, slot, 0).start()
             hop(array, slot, 1).start()
-
-    take_up.forward()
-    take_down.spread()
+        if slot == 0:
+            take_down.forward(0)
+            take_down.forward(1)
+
     own_up.wait()
     own_down.wait()
     take_up.finish()
-    take_down.forward()
     take_down.finish()
 
     def core_copy(array, side, slot):
@@ -892,6 +1019,7 @@
             for array in range(2):
                 hop(array, 0, 0).wait_recv()
                 hop(array, 0, 2).start()
+                hop(array, 1, 0).start()
             for array in range(2):
                 hop(array, 0, 2).wait_recv()
 
@@ -906,7 +1034,9 @@
 
         def tile(part, carry):
             rows = rows_at(start + part * BLK, BLK)
-            u = nt(h2[rows, :], wup[...]) + bias[0:1, :]
+            up_all = wup[...].reshape(D, D)
+            down_all = wdown[...].reshape(D, D)
+            u = nt(h2[rows, :], up_all) + bias[0:1, :]
             value, slope = gelu_both(u)
             row0 = start // 16 + part * (BLK // 16)
             mask = jnp.concatenate(
@@ -917,10 +1047,10 @@
                 axis=0,
             )
             act[rows, :] = (value * mask).astype(BF16)
-            da = nt(dz[rows, :], wdown[...])
+            da = nt(dz[rows, :], down_all)
             du[rows, :] = (slope * mask * da).astype(BF16)
-            z_part = jnp.dot(act[rows, :], wdown[...], preferred_element_type=F32)
-            h_part = jnp.dot(du[rows, :], wup[...], preferred_element_type=F32)
+            z_part = jnp.dot(act[rows, :], down_all, preferred_element_type=F32)
+            h_part = jnp.dot(du[rows, :], up_all, preferred_element_type=F32)
 
             @pl.when(part == c)
             def _():
@@ -945,16 +1075,25 @@
     for copy in (take_up, take_down):
         copy.sent()
 
-    def weight_chunk(j, carry):
-        cols = pl.ds(pl.multiple_of(j * 384, LANES), 384)
-        rows = rows_at(j * 384, 384)
-        wup[rows, :] = tn(du[:, cols], h2[...]).astype(BF16)
-        wdown[rows, :] = tn(act[:, cols], dz[...]).astype(BF16)
-        return carry
-
-    lax.fori_loop(0, 3, weight_chunk, 0)
+    def weight_grads(left, right, out):
+        def chunk(j, carry):
+            cols = pl.ds(pl.multiple_of(j * 384, LANES), 384)
+            block = tn(left[:, cols], right[...]).astype(BF16)
+            for k in range(2):
+                at = j * 2 + k
+                out[at // 3, rows_at(lax.rem(at, 3) * 192, 192), :] = block[k * 192 : (k + 1) * 192]
+            return carry
+
+        lax.fori_loop(0, 3, chunk, 0)
+
+    down_sum = PlaneReduce(wdown, (down_low, down_high) + (None,) * 4, sems, 59, y, x)
+    up_sum = PlaneReduce(wup, (up_low, up_high) + (None,) * 4, sems, 63, y, x)
+    weight_grads(act, dz, wdown)
+    down_sum.start()
+    waits.append(keep_local(wdown, down_out, 4))
+    weight_grads(du, h2, wup)
+    up_sum.start()
     waits.append(keep_local(wup, up_out, 3))
-    waits.append(keep_local(wdown, down_out, 4))
     bup_out[...] = jnp.dot(jnp.ones((8, SEQ), BF16), du[...], preferred_element_type=F32)
 
     small_out[...] = jnp.zeros_like(small_out)
@@ -984,7 +1123,16 @@
             grad = g2[rows, :].astype(F32)
             pass_on = kept * route
             branch = total(0) + b_down
-            final_out[rows, :] = (mixed[rows, :] + gate_two * pass_on * branch).astype(BF16)
+            low = (mixed[rows, :] + gate_two * pass_on * branch).astype(BF16)
+
+            @pl.when(p == slot)
+            def _():
+                fin_out[here, :] = low
+
+            @pl.when(p != slot)
+            def _():
+                fin_send_out[here, :] = low
+
             grad_gate_two = grad * pass_on * branch
             gated = grad * gate_two
             logit = (
@@ -1031,16 +1179,15 @@
     def out_grad(left):
         return sum(tn(left(slot), dy[slot].reshape(2 * BLK, D)) for slot in range(2))
 
-    wosend[...] = out_grad(lambda slot: o_in[slot]).astype(BF16)
-    wo_copy = remote(wosend, worecv, sems, 43, q=1 - q)
-    wo_copy.start()
-    near = out_grad(lambda slot: o[rows_at(place(slot, q, 0), 2 * BLK), :])
-    wo_copy.wait_recv()
-    gwo_out[...] = (near + worecv[...].astype(F32)).astype(BF16)
+    gwo_far_out[...] = out_grad(lambda slot: o_in[slot]).astype(BF16)
+    gwo_out[...] = out_grad(lambda slot: o[rows_at(place(slot, q, 0), 2 * BLK), :]).astype(BF16)
     for copy in do_copies:
         copy.wait_recv()
-    for copy in o_copies + [g_copy] + y_copies + dy_copies + do_copies + [wo_copy]:
+    for copy in o_copies + y_copies + dy_copies + do_copies:
         copy.wait_send()
+    for total in (down_sum, up_sum):
+        total.landed()
+        total.sent(second=False)
     for slot in range(2):
         for array in range(2):
             for kind in range(3):
@@ -1052,21 +1199,22 @@
         copy.wait()
 
 
-def middle(o, x2, k2, modg, g_pair, wo, w_up, w_down, bias, consts, gmask):
+def middle(*args):
     return pl.pallas_call(
         middle_kernel,
         out_shape=(
-            shape_of(2 * BLK, D), shape_of(2 * BLK, D, dtype=F32), shape_of(SEQ, NH * HD),
-            shape_of(GROUPS, 4 * D, dtype=F32), shape_of(8, D, dtype=F32), shape_of(D, D),
-            shape_of(D, D), shape_of(NH * HD, D), shape_of(8, D, dtype=F32),
-        ),
-        in_specs=[VMEM_SPEC] * 6 + [ANY_SPEC] * 2 + [VMEM_SPEC] * 3,
+            shape_of(BLK, D), shape_of(BLK, D), shape_of(2 * BLK, D, dtype=F32),
+            shape_of(SEQ, NH * HD), shape_of(GROUPS, 4 * D, dtype=F32), shape_of(8, D, dtype=F32),
+            shape_of(2, WROWS, D), shape_of(2, WROWS, D), shape_of(NH * HD, D),
+            shape_of(NH * HD, D), shape_of(8, D, dtype=F32),
+        )
+        + (shape_of(2, 2, CUT, D), shape_of(2, 2, QTR - CUT, D)) * 2,
+        in_specs=[VMEM_SPEC] * 6 + [ANY_SPEC] * 3 + [VMEM_SPEC] * 3,
         out_specs=(
-            VMEM_SPEC, VMEM_SPEC, VMEM_SPEC, VMEM_SPEC, VMEM_SPEC, ANY_SPEC, ANY_SPEC, VMEM_SPEC,
-            VMEM_SPEC,
+            VMEM_SPEC, VMEM_SPEC, VMEM_SPEC, VMEM_SPEC, VMEM_SPEC, VMEM_SPEC, ANY_SPEC, ANY_SPEC,
+            VMEM_SPEC, VMEM_SPEC, VMEM_SPEC, VMEM_SPEC, VMEM_SPEC, VMEM_SPEC, VMEM_SPEC,
         ),
         scratch_shapes=[
-            pltpu.VMEM((2 * BLK, D), BF16),
             pltpu.VMEM((2, 2 * BLK, NH * HD), BF16),
             pltpu.VMEM((2 * BLK, D), F32),
             pltpu.VMEM((2, BLK, D), BF16),
@@ -1077,8 +1225,8 @@
             pltpu.VMEM((SEQ, D), BF16),
             pltpu.VMEM((SEQ, D), BF16),
             pltpu.VMEM((SEQ, D), BF16),
-            pltpu.VMEM((D, D), BF16),
-            pltpu.VMEM((D, D), BF16),
+            pltpu.VMEM((2, WROWS, D), BF16),
+            pltpu.VMEM((2, WROWS, D), BF16),
             pltpu.VMEM((2, 2, 2, BLK, D), F32),
             pltpu.VMEM((2, 2, 2, BLK, D), BF16),
             pltpu.VMEM((2, 2, 2, BLK, D), BF16),
@@ -1086,90 +1234,15 @@
             pltpu.VMEM((2, 2, BLK, D), BF16),
             pltpu.VMEM((2, 2, BLK, D), BF16),
             pltpu.VMEM((2, 2 * BLK, NH * HD), BF16),
-            pltpu.VMEM((NH * HD, D), BF16),
-            pltpu.VMEM((NH * HD, D), BF16),
-            pltpu.SemaphoreType.DMA((44,)),
-            pltpu.SemaphoreType.DMA((44,)),
-            pltpu.SemaphoreType.DMA((5,)),
+            pltpu.SemaphoreType.DMA((67,)),
+            pltpu.SemaphoreType.DMA((67,)),
+            pltpu.SemaphoreType.DMA((7,)),
         ],
         compiler_params=pltpu.CompilerParams(
             collective_id=7, has_side_effects=True, vmem_limit_bytes=63 * 2**20
         ),
         name="middle",
-    )(o, x2, k2, modg, g_pair, wo, w_up, w_down, bias, consts, gmask)
-
-
-class PlaneReduce:
-    def __init__(self, grads, bufs, sems, k, y, x):
-        self.grads, self.y, self.x = grads, y, x
-        self.low_in, self.high_in, self.low_out, self.high_out, self.low_end, self.high_end = bufs
-        self.first = [
-            remote(grads.at[:, self.low(y, 1 - x)], self.low_in.at[0], sems, k, x=1 - x),
-            remote(grads.at[:, self.low(1 - y, 1 - x)], self.low_in.at[1], sems, k + 1, x=1 - x),
-            remote(grads.at[:, self.high(1 - y, x)], self.high_in.at[0], sems, k + 2, y=1 - y),
-            remote(grads.at[:, self.high(1 - y, 1 - x)], self.high_in.at[1], sems, k + 3, y=1 - y),
-        ]
-        self.second = [
-            remote(self.low_out, self.low_end, sems, k + 4, y=1 - y),
-            remote(self.high_out, self.high_end, sems, k + 5, x=1 - x),
-        ]
-
-    def low(self, y, x):
-        return rows_at((y * 2 + x) * QTR, CUT)
-
-    def high(self, y, x):
-        return rows_at((y * 2 + x) * QTR + CUT, QTR - CUT)
-
-    def start(self):
-        for copy in self.first:
-            copy.start()
-
-    def middle(self):
-        y, x = self.y, self.x
-        for copy in self.first:
-            copy.wait_recv()
-        for shard in range(2):
-            self.low_out[shard] = (
-                self.grads[shard, self.low(1 - y, x), :].astype(F32)
-                + self.low_in[1, shard].astype(F32)
-            ).astype(BF16)
-            self.high_out[shard] = (
-                self.grads[shard, self.high(y, 1 - x), :].astype(F32)
-                + self.high_in[1, shard].astype(F32)
-            ).astype(BF16)
-        for copy in self.second:
-            copy.start()
-
-    def arrive(self):
-        for copy in self.second:
-            copy.wait_recv()
-
-    def total(self, shard):
-        low = (
-            self.grads[shard, self.low(self.y, self.x), :].astype(F32)
-            + self.low_in[0, shard].astype(F32)
-            + self.low_end[shard].astype(F32)
-        )
-        high = (
-            self.grads[shard, self.high(self.y, self.x), :].astype(F32)
-            + self.high_in[0, shard].astype(F32)
-            + self.high_end[shard].astype(F32)
-        )
-        return low, high
-
-    def sent(self):
-        for copy in self.first + self.second:
-            copy.wait_send()
-
-
-REDUCE_SCRATCH = [
-    pltpu.VMEM((2, 2, CUT, D), BF16),
-    pltpu.VMEM((2, 2, QTR - CUT, D), BF16),
-    pltpu.VMEM((2, CUT, D), BF16),
-    pltpu.VMEM((2, QTR - CUT, D), BF16),
-    pltpu.VMEM((2, CUT, D), BF16),
-    pltpu.VMEM((2, QTR - CUT, D), BF16),
-]
+    )(*args)
 
 
 class LineReduce:
@@ -1219,21 +1292,22 @@
 
 
 def back_kernel(
-    d, h1, wide, x2, dx, scale, sums_two, smalls, b_up, up_g, down_g, wo_g, hot, spread, final,
-    ada, slope,
-    final_out, tokens_out, a_out, up_out, down_out, mod_out, cond_out,
-    own, csend, crecv, qsend, qrecv, wideg, grads, sums, parcel, parcels, modline, condbuf,
+    d, h1, wide, x2, dx, scale, sums_two, smalls, b_up, up_g, down_g, wo_g, wo_in, hot, spread,
+    ada, slope, down_low, down_high, up_low, up_high,
+    tokens_out, a_out, up_out, down_out, mod_out, cond_out,
+    own, csend, crecv, qsend, qrecv, wideg, grads, sums, parcel, parcels, lsum, modline, condbuf,
     tsend, halves, *rest,
 ):
-    bufs = [rest[0:6], rest[6:12], rest[12:18]]
-    send, recv, loc = rest[18:]
+    bufs = [(down_low, down_high) + rest[0:4], (up_low, up_high) + rest[4:8], rest[8:14]]
+    send, recv, loc = rest[14:]
     y, x, p, q, c = (lax.axis_index(name) for name in "yxpqc")
     sems = (send, recv)
-    line = line_peers(p, q, c)
+    pair = [
+        {"q": lax.rem(q + k // 2, 2), "c": lax.rem(c + k % 2, 2)} for k in range(1, 4)
+    ]
     plane = [{"y": lax.rem(y + k // 2, 2), "x": lax.rem(x + k % 2, 2)} for k in range(1, 4)]
-    greet(line + plane)
+    greet(pair + plane + [{"p": 1 - p}])
     rank = y * 2 + x
-    me = p * 4 + q * 2 + c
 
     def keep_local(src, dst, k):
         copy = pltpu.make_async_copy(src, dst, loc.at[k])
@@ -1244,20 +1318,33 @@
         return slot * HALF + chip * (2 * BLK) + core * BLK
 
     outs = (down_out, up_out, a_out)
-    reduces = [PlaneReduce(grads.at[k], bufs[k], sems, 6 * k, y, x) for k in range(3)]
+    reduces = [PlaneReduce(grads.at[k], bufs[k], sems, 6 * k, y, x, landed=k < 2) for k in range(3)]
     lines = [
-        LineReduce(reduces[k], halves.at[k], outs[k], sems, 18 + 5 * k, y, x, p) for k in range(3)
+        LineReduce(reduces[k], halves.at[k], outs[k], sems, 18 + 5 * k, y, x, p)
+        for k in range(3)
     ]
     loads = [keep_local(down_g, grads.at[0], 0), keep_local(up_g, grads.at[1], 1)]
     for k in range(2):
         loads[k].wait()
-        reduces[k].start()
-    final_copy = remote(
-        final.at[pl.ds(pl.multiple_of((1 - p) * BLK, 16), BLK)], final_out.at[p], sems, 33, p=1 - p
-    )
-    own_final = keep_local(
-        final.at[pl.ds(pl.multiple_of(p * BLK, 16), BLK)], final_out.at[p], 2
-    )
+        reduces[k].middle()
+
+    def weight_chunk(j, carry):
+        cols = pl.ds(pl.multiple_of(j * 384, LANES), 384)
+        wideg[rows_at(j * 384, 384), :] = tn(d[:, cols], h1[...]).astype(BF16)
+        return carry
+
+    lax.fori_loop(0, 4, weight_chunk, 0)
+    for shard in range(2):
+        grads[2, shard, :UNIT_ROWS, :] = tn(
+            spread[...], wideg[shard * 6 * LANES : (shard + 1) * 6 * LANES, :]
+        ).astype(BF16)
+        rows = slice(shard * QTR, (shard + 1) * QTR)
+        grads[2, shard, UNIT_ROWS:, :] = (
+            wo_g[rows, :].astype(F32) + wo_in[rows, :].astype(F32)
+        ).astype(BF16)
+    reduces[2].start()
+    lines[0].start()
+    lines[1].start()
 
     def core_copy(side, slot):
         return remote(
@@ -1302,22 +1389,14 @@
 
     lax.fori_loop(0, 4, through, 0)
 
-    def weight_chunk(j, carry):
-        cols = pl.ds(pl.multiple_of(j * 384, LANES), 384)
-        wideg[rows_at(j * 384, 384), :] = tn(d[:, cols], h1[...]).astype(BF16)
-        return carry
-
-    lax.fori_loop(0, 4, weight_chunk, 0)
-    for shard in range(2):
-        grads[2, shard, :UNIT_ROWS, :] = tn(
-            spread[...], wideg[shard * 6 * LANES : (shard + 1) * 6 * LANES, :]
-        ).astype(BF16)
-        grads[2, shard, UNIT_ROWS:, :] = wo_g[shard * QTR : (shard + 1) * QTR, :]
-    reduces[2].start()
     ones = jnp.ones((8, SEQ), BF16)
     col_sums = jnp.dot(ones, d[...], preferred_element_type=F32)
-    reduces[0].middle()
-    final_copy.start()
+
+    reduces[2].landed()
+    reduces[2].middle()
+    lines[0].spread()
+    lines[2].start()
+    lines[0].forward()
 
     sums[...] = jnp.zeros_like(sums)
     for slot in range(2):
@@ -1354,39 +1433,43 @@
         lax.fori_loop(0, BLK // 16, group, 0)
 
     token_copy = remote(tsend.at[1 - p], tsend.at[2], sems, 40, p=1 - p)
-
     two = jnp.concatenate([sums[...], sums_two[...]], axis=1)
     full = lax.dot_general(
         hot[...], two, (((0,), (0,)), ((), ())), preferred_element_type=F32,
         precision=lax.Precision.HIGHEST,
     )
     for k in range(8):
-        parcel[k] = full[:, k * MODS : (k + 1) * MODS]
-        parcel[k, 11:14, : D // 8] = smalls[0:3, k * (D // 8) : (k + 1) * (D // 8)]
+        there = parcel.at[k // 4, (k // 2) % 2, k % 2]
+        there[...] = full[:, k * MODS : (k + 1) * MODS]
+        there[11:14, : D // 8] = smalls[0:3, k * (D // 8) : (k + 1) * (D // 8)]
     for shard in range(2):
         heads = col_sums[0:1, shard * 6 * LANES : (shard + 1) * 6 * LANES]
         pieces = [b_up[0:1, shard * WROWS : (shard + 1) * WROWS]]
         for unit in (0, 2, 3, 5):
             pieces.append(heads[:, unit * LANES : unit * LANES + HD])
-        owner = lax.rem(p + shard, 2) * 4 + q * 2 + c
-        parcel[owner, 14:15, :] = jnp.concatenate(pieces, axis=1)
+        parcel[lax.rem(p + shard, 2), q, c, 14:15, :] = jnp.concatenate(pieces, axis=1)
+    here = q * 2 + c
     copies = []
-    for k, where in enumerate(line):
+    for k, where in enumerate(pair):
         copy = remote(
-            parcel.at[where["p"] * 4 + where["q"] * 2 + where["c"]], parcels.at[me], sems, 41 + k,
-            **where,
+            parcel.at[:, where["q"], where["c"]], parcels.at[here], sems, 41 + k, **where
         )
         copy.start()
         copies.append(copy)
-    own_parcel = keep_local(parcel.at[me], parcels.at[me], 3)
-    token_copy.start()
-    reduces[1].middle()
-    lines[0].start()
+    own_parcel = keep_local(parcel.at[:, q, c], parcels.at[here], 3)
     own_parcel.wait()
     for copy in copies:
         copy.wait_recv()
-    for row in range(2):
-        modline[row] = sum(parcels[row * 4 + k] for k in range(4)).astype(BF16)
+    line_sum = sum(parcels[k] for k in range(4))
+    lsum[0:2] = line_sum
+    over = remote(lsum.at[1 - p], lsum.at[2], sems, 44, p=1 - p)
+    over.start()
+    copies.append(over)
+    token_copy.start()
+    lines[1].spread()
+    over.wait_recv()
+    modline[p] = lsum[p].astype(BF16)
+    modline[1 - p] = lsum[2].astype(BF16)
     mods = []
     for k, where in enumerate(plane):
         copy = remote(modline, mod_out.at[rank], sems, 48 + k, **where)
@@ -1403,32 +1486,23 @@
         copy.start()
         conds.append(copy)
         if k == 0:
-            reduces[2].middle()
+            lines[1].forward()
         if k == 1:
-            lines[1].start()
-        if k == 2:
-            lines[0].spread()
+            lines[2].spread()
         copy.wait_recv()
         total = condbuf[2 * k].astype(F32) + condbuf[2 * k + 1].astype(F32)
         if k < 2:
             condbuf[2 * k + 2] = total.astype(BF16)
     cond_out[...] = total * slope[...]
 
-    lines[2].start()
-    lines[0].forward()
-    lines[1].spread()
+    lines[2].forward()
     token_copy.wait_recv()
     tokens_out[1 - p] = tsend[2].astype(F32)
-    lines[0].finish()
-    lines[1].forward()
-    lines[2].spread()
-    lines[1].finish()
-    lines[2].forward()
-    lines[2].finish()
-    final_copy.wait_recv()
+    for k in range(3):
+        lines[k].finish()
     for copy in mods:
         copy.wait_recv()
-    for copy in [final_copy, token_copy] + copies + mods + conds:
+    for copy in [token_copy] + copies + mods + conds:
         copy.wait_send()
     for slot in range(2):
         for side in range(2):
@@ -1437,20 +1511,18 @@
     for k in range(3):
         reduces[k].sent()
         lines[k].sent()
-    own_final.wait()
     own_mod.wait()
 
 
-def back(d, h1, wide, x2, dx, scale, sums_two, smalls, b_up, up_g, down_g, wo_g, hot, spread, final, ada, slope):
+def back(*args):
     return pl.pallas_call(
         back_kernel,
         out_shape=(
-            shape_of(2, BLK, D), shape_of(2, BLK, D, dtype=F32), shape_of(WROWS, D),
-            shape_of(WROWS, D), shape_of(WROWS, D), shape_of(4, 2, 16, MODS),
-            shape_of(32, D, dtype=F32),
+            shape_of(2, BLK, D, dtype=F32), shape_of(WROWS, D), shape_of(WROWS, D),
+            shape_of(WROWS, D), shape_of(4, 2, 16, MODS), shape_of(32, D, dtype=F32),
         ),
-        in_specs=[VMEM_SPEC] * 9 + [ANY_SPEC] * 2 + [VMEM_SPEC] * 6,
-        out_specs=(VMEM_SPEC,) * 7,
+        in_specs=[VMEM_SPEC] * 9 + [ANY_SPEC] * 2 + [VMEM_SPEC] * 10,
+        out_specs=(VMEM_SPEC,) * 6,
         scratch_shapes=[
             pltpu.VMEM((2, 2, BLK, D), F32),
             pltpu.VMEM((2, 2, BLK, D), BF16),
@@ -1460,14 +1532,16 @@
             pltpu.VMEM((WIDE, D), BF16),
             pltpu.VMEM((3, 2, WROWS, D), BF16),
             pltpu.VMEM((GROUPS, 2 * D), F32),
-            pltpu.VMEM((8, 16, MODS), F32),
-            pltpu.VMEM((8, 16, MODS), F32),
+            pltpu.VMEM((2, 2, 2, 16, MODS), F32),
+            pltpu.VMEM((4, 2, 16, MODS), F32),
+            pltpu.VMEM((3, 16, MODS), F32),
             pltpu.VMEM((2, 16, MODS), BF16),
             pltpu.VMEM((6, 32, D), BF16),
             pltpu.VMEM((3, BLK, D), BF16),
             pltpu.VMEM((3, 2, QTR, D), BF16),
         ]
-        + REDUCE_SCRATCH * 3
+        + REDUCE_SCRATCH[2:] * 2
+        + REDUCE_SCRATCH
         + [
             pltpu.SemaphoreType.DMA((54,)),
             pltpu.SemaphoreType.DMA((54,)),
@@ -1477,7 +1551,11 @@
             collective_id=8, has_side_effects=True, vmem_limit_bytes=63 * 2**20
         ),
         name="back",
-    )(d, h1, wide, x2, dx, scale, sums_two, smalls, b_up, up_g, down_g, wo_g, hot, spread, final, ada, slope)
+    )(*args)
+
+
+def swap(values, axis):
+    return lax.ppermute(values, axis, SWAP)
 
 
 def layer_device(
@@ -1505,12 +1583,6 @@
     bias_own = jnp.pad(jnp.concatenate([bias_own, b_up.astype(F32)]), (0, BIAS - 1344))
     bias_own = jnp.broadcast_to(bias_own, (8, BIAS))
 
-    cvec = cond.astype(F32) + time_embed(timesteps)
-    sig = lax.logistic(cvec)
-    act_low = jnp.pad((cvec * sig).astype(BF16), ((0, 0), (0, 5), (0, 0)))
-    mod_part = jnp.einsum("bcd,dm->bcm", act_low, ada_w, preferred_element_type=F32) + ada_b.astype(
-        F32
-    )
     def row_of(values):
         return jnp.where(first, values[0], values[1])
 
@@ -1531,10 +1603,23 @@
     def by_row(values):
         return jnp.transpose(values, (1, 0, 2))
 
+    def items(values):
+        return jnp.pad(values, ((0, 0), (0, 5), (0, 0))).reshape(32, -1)
+
     keep_wide = jnp.broadcast_to(keep.T.astype(BF16)[..., None], (2, BLK, LANES))
-    triple, hidden_one, token_low, keep_low, mod_groups, w_wide, w_out_all, biases, act_all = front(
-        mod_part, by_row(tokens), keep_wide, act_low, bias_own, w_a, spread, hot_rows
-    )
+    ada_rows = jnp.transpose(ada_w)
+    (
+        triple, hidden_one, token_low, keep_low, grad_low, mod_groups, w_wide, w_out_all, biases,
+        act_all, slope,
+    ) = front(
+        items(cond.astype(F32) + time_embed(timesteps)), by_row(tokens), keep_wide, by_row(grad_out), bias_own, w_a, spread,
+        hot_rows, ada_rows, ada_b.astype(F32)[None],
+    )
+    up_quarter, triple = lax.optimization_barrier(
+        (lax.dynamic_slice_in_dim(w_up_rows, rank * QTR, QTR, 0), triple)
+    )
+    up_quarter = swap(up_quarter, "p")
+
     head_row = row_of(head_mask)
     heads_here = jnp.concatenate(
         [
@@ -1571,17 +1656,22 @@
     )
     consts = jnp.pad(jnp.stack([b_out, b_down, w_route]).astype(F32), ((0, 5), (0, 0)))
     b_up_two = jnp.concatenate([biases[0, :, 768:1344], biases[1, :, 768:1344]], axis=1)
-    final, grad_mixed, grad_attended, sums_two, smalls, up_low, down_low, wo_low, b_up_sums = middle(
+    (
+        final, final_send, grad_mixed, grad_attended, sums_two, smalls, up_low, down_low, wo_low, wo_far,
+        b_up_sums, *landed,
+    ) = middle(
         attended, token_low.reshape(2 * BLK, D), keep_low.reshape(2 * BLK, LANES), mod_groups,
-        by_row(grad_out), w_out_all.reshape(4 * QTR, D), w_up_rows, w_down, b_up_two, consts,
-        group_wide,
-    )
+        grad_low.reshape(2 * BLK, D), w_out_all.reshape(4 * QTR, D), w_up_rows, up_quarter, w_down,
+        b_up_two, consts, group_wide,
+    )
+    wo_in = swap(wo_far, "q")
+    final_in = swap(final_send, "p")
+    final_pair = jnp.stack([jnp.where(first, final, final_in), jnp.where(first, final_in, final)])
     d_all = attn_bwd(scal, triple, grad_attended, lse, pack)
-    slope = jnp.pad(sig * (1.0 + cvec * (1.0 - sig)), ((0, 0), (0, 5), (0, 0))).reshape(32, D)
-    final_pair, token_pair, low_a, low_up, low_down, mod_all, grad_cond = back(
+    token_pair, low_a, low_up, low_down, mod_all, grad_cond = back(
         d_all, hidden_one, w_wide, token_low.reshape(2 * BLK, D), grad_mixed,
-        mod_groups[:, D : 2 * D], sums_two, smalls, b_up_sums, up_low.reshape(2, WROWS, D),
-        down_low.reshape(2, WROWS, D), wo_low, hot_rows, spread, final, jnp.transpose(ada_w), slope,
+        mod_groups[:, D : 2 * D], sums_two, smalls, b_up_sums, up_low, down_low, wo_low, wo_in,
+        hot_rows, spread, ada_rows, slope, *landed,
     )
     out_a = low_a.astype(F32)
     mod_low = jnp.where(jnp.arange(16)[:, None] < CROPS, mod_all, 0)

time: 481 us -> 430 us (0.89)
  Pallas kernels: 430 us -> 370 us
  starting transfers between devices: 0 us -> 5.61 us
  local copies, waits for them, and re-layouts: 22.7 us -> 27.8 us
    pallas_call x2, Pallas kernels: 317 us -> 252 us  [the longest x1 132 us: middle(): pl.pallas_call(middle_kernel, out_shape=(shape_of(BLK, D), shape_of(BLK,...]
    ppermute x0 -> x3, starting transfers between devices: none -> 5.61 us  [swap(): return lax.ppermute(values, axis, SWAP)]
    unnamed x51 -> x50, local copies, waits for them, and re-layouts: 11.4 us -> 11.1 us
  transfers between devices with their start and end apart: 0 -> 3, of which waited for: 0 -> 0; matrix products, arithmetic and copies ran while one was open for 0% -> 2% of each run, Pallas kernels for 0% -> 8%
where the time goes in v4:
time: 430 us; the launch traced here: 422 us
  Pallas kernels  370 us (86%)
  local copies, waits for them, and re-layouts  27.8 us (6%)
  other arithmetic  14.6 us (3%)
  starting transfers between devices  5.61 us (1%)
    pallas_call x1, Pallas kernels, middle(): pl.pallas_call(middle_kernel, out_shape=(shape_of(BLK, D), shape_of(BLK,...  132 us
    pallas_call x1, Pallas kernels, back(): pl.pallas_call(back_kernel, out_shape=(shape_of(2, BLK, D, dtype=F32), sh...  120 us
    pallas_call x1, Pallas kernels, front(): pl.pallas_call(front_kernel, out_shape=(shape_of(SEQ, WIDE), shape_of(SEQ...  85.3 us
    pallas_call x1, Pallas kernels, attn_bwd(): pl.pallas_call(attn_bwd_kernel, out_shape=jax.ShapeDtypeStruct((SEQ, WIDE...  18 us
    pallas_call x1, Pallas kernels, attn_fwd(): pl.pallas_call(attn_fwd_kernel, out_shape=(jax.ShapeDtypeStruct((SEQ, NH...  14.3 us
    unnamed x50, local copies, waits for them, and re-layouts  11.1 us
  transfers between devices with their start and end apart: 3, of which 0 were waited for; matrix products, arithmetic and copies ran while one was open for 2% of the time, Pallas kernels for 8%

profile of v4, /device:TPU:0, one launch (start us, length us, event | category | flops | bytes accessed | tf_op | source)
XLA Modules:
  0.0 422.1 jit_solution(2051398187694127352)
XLA Ops:
  0.7 0.8 convert_element_type.56
  1.5 0.7 convert_bitcast_fusion.1
  2.2 0.8 and_select_fusion
  3.1 0.8 reshape.194
  4.1 0.8 bitcast_subtract_fusion.1
  5.0 1.3 reshape.195.ada_b
  6.3 0.7 convert_element_type.61
  7.0 0.6 pad_convert_fusion.hot
  7.7 0.9 multiply_cosine_fusion
  8.5 0.9 maximum_add_fusion
  9.5 0.7 pad.29.clone
  10.2 1.7 dynamic-slice_bitcast_fusion
  11.9 1.2 pad_maximum_fusion.w_a
  13.1 1.3 copy_bitcast_fusion
  14.4 0.6 broadcast_in_dim.19.bias_own
  15.0 0.8 broadcast_in_dim.18.k_pair
  15.8 85.3 %front.1 = (bf16[1408,1536]{1,0:T(8,128)(2,1)}, bf16[1408,1152]{1,0:T(8,128)(2,1)}, bf16[2,176,1152]{2,1,0:T(8,128)(2,1)}, bf16[2,176,128]{2,1,0:T(8,128)(2,1)},...) custom-call(f32[32,1152]{1,0:T(8,128)} %bitcast.78, ...), custom_call_target="tpu_custom_call" | custom-call | tf_op jit(solution)/shard_map/front/pallas_call | solution.py:762
  102.6 1.0 reshape.190.gmask
  103.7 0.7 slice_bitcast_fusion.2
  104.4 0.7 pad_maximum_fusion.1.bias
  105.2 14.3 %attn_fwd.1 = (bf16[1408,288]{1,0:T(8,128)(2,1)S(1)}, f32[1408,128]{1,0:T(8,128)S(1)}) custom-call(s32[77]{0:T(128)S(1)} %pad_add_fusion.1.scal, bf16[1408,1536]{1,0:T(8,128)(2,1)} %get-tuple-element.51.buf, bf16[512,288]{1,0:T(8,128)(2,1)S(1)} %copy-done), custom_call_target="tpu_custom_call" | custom-call | tf_op jit(solution)/shard_map/attn_fwd/pallas_call | solution.py:434
  119.6 1.0 copy-done.1
  120.5 0.9 copy-done.3
  121.4 0.6 fusion.5.consts
  122.0 0.7 copy-done.14
  122.8 131.9 %middle.1 = (bf16[176,1152]{1,0:T(8,128)(2,1)}, bf16[176,1152]{1,0:T(8,128)(2,1)}, f32[352,1152]{1,0:T(8,128)}, bf16[1408,288]{1,0:T(8,128)(2,1)}, f32[24,4608]{...) custom-call(bf16[1408,288]{1,0:T(8,128)(2,1)} %copy-done.1, ...), custom_call_target="tpu_custom_call" | custom-call | tf_op jit(solution)/shard_map/middle/pallas_call | solution.py:1203
  254.7 4.2 %collective-permute-start.1 = (bf16[176,1152]{1,0:T(8,128)(2,1)}, bf16[176,1152]{1,0:T(8,128)(2,1)S(1)}, u32[]{:S(2)}, u32[]{:S(2)}) collective-permute-start(bf16[176,1152]{1,0:T(8,128)(2,1)} %get-tuple-element.61), channel_id=1, source_target_pairs={{0,4},{4,0},{1,5},{5,1},{2,6},{6,2},{3,7},{7,3},{8,12},{12,8},{9,1... | collective-permute-start | bytes 1216520 | tf_op jit(solution)/shard_map/ppermute | solution.py:1558
  258.9 1.5 slice.78.scale
  260.5 1.3 collective-permute-start.2
  261.8 1.2 copy-done.2
  263.0 1.1 copy-done.4
  264.1 18.0 %attn_bwd.1.d = bf16[1408,1536]{1,0:T(8,128)(2,1)} custom-call(s32[77]{0:T(128)S(1)} %pad_add_fusion.1.scal, bf16[1408,1536]{1,0:T(8,128)(2,1)} %get-tuple-element.51.buf, bf16[1408,288]{1,0:T(8,128)(2,1)S(1)} %copy-done.2, f32[1408,128]{1,0:T(8,128)S(1)} %copy-done.4, bf16[512,288]{1,0:T(8,128)(2,1)S(1)} %copy-done), custom_call_target="tpu_custom_call" | custom-call | tf_op jit(solution)/shard_map/attn_bwd/pallas_call | solution.py:448
  282.3 1.5 copy.73
  283.8 120.1 %back.1 = (f32[2,176,1152]{2,1,0:T(8,128)}, bf16[576,1152]{1,0:T(8,128)(2,1)}, bf16[576,1152]{1,0:T(8,128)(2,1)}, bf16[576,1152]{1,0:T(8,128)(2,1)}, bf16[4,2,16...) custom-call(bf16[1408,1536]{1,0:T(8,128)(2,1)} %attn_bwd.1.d, bf16[1408,1152]{1,0:T(8,128)(2,1)} %get-tuple-element.64.h1, ...), custom_call_target="tpu_custom_call" | custom-call | tf_op jit(solution)/shard_map/back/pallas_call | solution.py:1518
  404.0 1.0 convert_reduce_fusion.1
  405.0 0.7 slice_reduce_fusion.1
  405.7 0.6 fusion.16
  406.3 0.6 slice_reduce_fusion
  406.9 1.9 slice.93
  408.9 1.2 copy-done.6
  410.2 2.0 copy.74
  412.1 0.7 copy.76
  412.8 0.7 convert_reduce_fusion
  413.6 1.4 slice_bitcast_fusion
  415.0 0.6 copy-done.8
  415.5 1.7 convert_bitcast_fusion
  417.3 1.7 convert_element_type.66
  419.0 2.7 fusion.18
  (81 shorter events, 2.6 us)
Async XLA Ops:
  0.6 11.3 %copy-start.15 = (bf16[144,1152]{1,0:T(8,128)(2,1)S(1)}, bf16[144,1152]{1,0:T(8,128)(2,1)}, u32[]{:S(2)}) copy-start(bf16[144,1152]{1,0:T(8,128)(2,1)} %param.34) | copy-start | bytes 995332
  0.7 11.3 %copy-start.9 = (bf16[1152,432]{0,1:T(8,128)(2,1)S(1)}, bf16[1152,432]{0,1:T(8,128)(2,1)}, u32[]{:S(2)}) copy-start(bf16[1152,432]{0,1:T(8,128)(2,1)} %param.32) | copy-start | bytes 2985988
  9.4 3.6 copy-start.10
  9.5 3.6 copy-start.11
  15.8 85.5 %copy-start.20 = (bf16[1152]{0:T(1024)(128)(2,1)S(1)}, bf16[1152]{0:T(1024)(128)(2,1)}, u32[]{:S(2)}) copy-start(bf16[1152]{0:T(1024)(128)(2,1)} %param.35) | copy-start | bytes 6916
  15.8 85.5 %copy-start.21 = (bf16[1152]{0:T(1024)(128)(2,1)S(1)}, bf16[1152]{0:T(1024)(128)(2,1)}, u32[]{:S(2)}) copy-start(bf16[1152]{0:T(1024)(128)(2,1)} %param.39) | copy-start | bytes 6916
  15.8 85.5 %copy-start.22 = (bf16[1152]{0:T(1024)(128)(2,1)S(1)}, bf16[1152]{0:T(1024)(128)(2,1)}, u32[]{:S(2)}) copy-start(bf16[1152]{0:T(1024)(128)(2,1)} %param.40) | copy-start | bytes 6916
  15.8 85.5 %copy-start.18 = (s32[2,11,16]{2,0,1:T(2,128)S(1)}, s32[2,11,16]{2,0,1:T(2,128)}, u32[]{:S(2)}) copy-start(s32[2,11,16]{2,0,1:T(2,128)} %param.28) | copy-start | bytes 4228
  15.8 85.6 %copy-start.19 = (s32[2,11,16]{2,0,1:T(2,128)S(1)}, s32[2,11,16]{2,0,1:T(2,128)}, u32[]{:S(2)}) copy-start(s32[2,11,16]{2,0,1:T(2,128)} %param.27) | copy-start | bytes 4228
  101.1 4.0 copy-start
  101.2 20.9 %collective-permute-start = (bf16[144,1152]{1,0:T(8,128)(2,1)}, bf16[144,1152]{1,0:T(8,128)(2,1)S(1)}, u32[]{:S(2)}, u32[]{:S(2)}) collective-permute-start(bf16[144,1152]{1,0:T(8,128)(2,1)} %dynamic-slice_bitcast_fusion), channel_id=1, source_target_pairs={{0,4},{4,0},{1,5},{5,1},{2,6},{6,2},{3,7},{7,3},{8,12},{12,8},{9,1... | collective-permute-start | bytes 995336 | tf_op jit(solution)/shard_map/ppermute | solution.py:1558
  119.5 1.0 copy-start.1
  120.5 0.9 copy-start.3
  122.0 0.7 copy-start.14
  254.7 27.4 %collective-permute-start.1 = (bf16[176,1152]{1,0:T(8,128)(2,1)}, bf16[176,1152]{1,0:T(8,128)(2,1)S(1)}, u32[]{:S(2)}, u32[]{:S(2)}) collective-permute-start(bf16[176,1152]{1,0:T(8,128)(2,1)} %get-tuple-element.61), channel_id=1, source_target_pairs={{0,4},{4,0},{1,5},{5,1},{2,6},{6,2},{3,7},{7,3},{8,12},{12,8},{9,1... | collective-permute-start | bytes 1216520 | tf_op jit(solution)/shard_map/ppermute | solution.py:1558
  260.5 23.3 %collective-permute-start.2 = (bf16[288,1152]{1,0:T(8,128)(2,1)}, bf16[288,1152]{1,0:T(8,128)(2,1)}, u32[]{:S(2)}, u32[]{:S(2)}) collective-permute-start(bf16[288,1152]{1,0:T(8,128)(2,1)} %get-tuple-element.73), channel_id=1, source_target_pairs={{0,2},{2,0},{1,3},{3,1},{4,6},{6,4},{5,7},{7,5},{8,10},{10,8},{9,1... | collective-permute-start | bytes 1990664 | tf_op jit(solution)/shard_map/ppermute | solution.py:1558
  261.8 1.2 copy-start.2
  263.0 1.1 copy-start.4
  264.1 18.0 %copy-start.13 = (bf16[176,1152]{1,0:T(8,128)(2,1)S(1)}, bf16[176,1152]{1,0:T(8,128)(2,1)}, u32[]{:S(2)}) copy-start(bf16[176,1152]{1,0:T(8,128)(2,1)} %get-tuple-element.60) | copy-start | bytes 1216516
  404.0 4.8 %copy-start.5 = (bf16[576,1152]{1,0:T(8,128)(2,1)S(1)}, bf16[576,1152]{1,0:T(8,128)(2,1)}, u32[]{:S(2)}) copy-start(bf16[576,1152]{1,0:T(8,128)(2,1)} %get-tuple-element.83) | copy-start | bytes 3981316
  408.7 1.4 copy-start.6
  408.9 3.2 copy-start.17
  408.9 3.9 copy-start.12
  413.6 2.0 copy-start.8
  415.5 1.8 copy-start.7
  417.3 1.7 copy-start.16
